TPU v7x, 32 devices: a whole 2x2x4 slice. The times are simulated.
32 devices in a mesh: dp: 32 (over z, y, x, core).
Axes of the slice: x: 2, y: 2, z: 4, core: 2. Of those that a mesh axis runs over, the one named last changes fastest.
Arguments:
- patches: bfloat16 [96, 256, 588], P('dp'), may hold values from -6 to 6
- valid_mask: int32 [96], replicated, may hold values from 0 to 1, as said below
- owners: int32 [12], replicated, may hold values from -1 to 31, as said below
- embedding: float32 [867, 384], P(None, 'dp')
- embedding_first: float32 [867, 384], P(None, 'dp'), may hold values from -1.1920929e-07 to 1.1920929e-07
- embedding_second: float32 [867, 384], P(None, 'dp'), may hold values from 1.790601e-17 to 2.8649616e-16
- layers: float32 [3, 4608, 384], P(None, 'dp')
- layers_first: float32 [3, 4608, 384], P(None, 'dp'), may hold values from -1.1920929e-07 to 1.1920929e-07
- layers_second: float32 [3, 4608, 384], P(None, 'dp'), may hold values from 1.790601e-17 to 2.8649616e-16
- layer_stats: float32 [3, 4, 384, 384], P(None, None, 'dp'), as said below
- layer_bases: float32 [3, 4, 384, 384], P(None, None, 'dp'), as said below
- head_hidden: float32 [2048, 2432], P('dp')
- hidden_first: float32 [2048, 2432], P('dp'), may hold values from -1.1920929e-07 to 1.1920929e-07
- hidden_second: float32 [2048, 2432], P('dp'), may hold values from 1.790601e-17 to 2.8649616e-16
- head_last: float32 [2048, 256], P(None, 'dp'), may hold values from -0.125 to 0.125
- last_first: float32 [2048, 256], P(None, 'dp'), may hold values from -1.1920929e-07 to 1.1920929e-07
- last_second: float32 [2048, 256], P(None, 'dp'), may hold values from 1.790601e-17 to 2.8649616e-16
- protos: float32 [256, 65536], P(None, 'dp')
- protos_first: float32 [256, 65536], P(None, 'dp'), may hold values from -1.1920929e-07 to 1.1920929e-07
- protos_second: float32 [256, 65536], P(None, 'dp'), may hold values from 1.790601e-17 to 2.8649616e-16
- teacher_embedding: float32 [867, 384], P(None, 'dp')
- teacher_layers: float32 [3, 4608, 384], P(None, 'dp')
- teacher_hidden: float32 [2048, 2432], P('dp')
- teacher_last: float32 [2048, 256], P(None, 'dp'), may hold values from -0.125 to 0.125
- teacher_protos: float32 [256, 65536], P(None, 'dp')
- centre: float32 [65536], P('dp'), may hold values from -0.3 to 0.3
Outputs:
- loss_sum: float32 [], replicated
- loss_count: float32 [], replicated
- grad_norm: float32 [], replicated
- next_embedding_first: float32 [867, 384], P(None, 'dp')
- next_embedding_second: float32 [867, 384], P(None, 'dp')
- next_embedding: float32 [867, 384], P(None, 'dp')
- next_layers_first: float32 [3, 4608, 384], P(None, 'dp')
- next_layers_second: float32 [3, 4608, 384], P(None, 'dp')
- next_layers: float32 [3, 4608, 384], P(None, 'dp')
- next_stats: float32 [3, 4, 384, 384], P(None, None, 'dp')
- next_bases: float32 [3, 4, 384, 384], P(None, None, 'dp')
- next_hidden_first: float32 [2048, 2432], P('dp')
- next_hidden_second: float32 [2048, 2432], P('dp')
- next_hidden: float32 [2048, 2432], P('dp')
- next_last_first: float32 [2048, 256], P(None, 'dp')
- next_last_second: float32 [2048, 256], P(None, 'dp')
- next_last: float32 [2048, 256], P(None, 'dp')
- next_protos_first: float32 [256, 65536], P(None, 'dp')
- next_protos_second: float32 [256, 65536], P(None, 'dp')
- next_protos: float32 [256, 65536], P(None, 'dp')
- next_teacher_embedding: float32 [867, 384], P(None, 'dp')
- next_teacher_layers: float32 [3, 4608, 384], P(None, 'dp')
- next_teacher_hidden: float32 [2048, 2432], P('dp')
- next_teacher_last: float32 [2048, 256], P(None, 'dp')
- next_teacher_protos: float32 [256, 65536], P(None, 'dp')
- next_centre: float32 [65536], P('dp')
Inputs may be any that keep to these rules, and one draw needn't show every extreme that they name: `valid_mask`: 1 marks an image that counts; the last image never counts, the one before it always. `owners`: -1 where layer matrix m keeps its basis, else the device that renews it. Each slice layer_stats[l, j] is symmetric positive definite. Each slice layer_bases[l, j] is orthogonal.
All inputs are finite; a program needn't handle non-finite values.
Results may differ from a plain program's by a relative error of at most 0.013.
The roundings to bfloat16 on the way count: a program that leaves them out, or rounds other values in their place, can miss the bound.
Values may be sent and summed in bfloat16 or wider, within the bound.
A program may use at most 256 MiB of HBM per device.

v0:
```python
import jax
import jax.numpy as jnp
from jax import lax
from jax.sharding import PartitionSpec as P

D = 384
HEADS = 6
HEAD_DIM = 64
MLP = 1536
PIX = 588
LAYERS = 3
STEP = 10
SEQ = 257


NORM_EPSILON = 1e-06
UNIT_EPSILON = 1e-06
TAU_STUDENT = 0.1
TAU_TEACHER = 0.07
CLIP_MAX = 0.001
BETA_ONE = 0.9
BETA_TWO = 0.999
ADAM_EPSILON = 1e-08
WEIGHT_DECAY = 0.04
RATE_MATRIX = 0.04
RATE_VECTOR = 0.2
BETA_STAT = 0.95
TEACHER_MOMENTUM = 0.8
CENTRE_MOMENTUM = 0.9
ROOT_HALF = 0.7071067811865476
DENSITY_SCALE = 0.3989422804014327


def joined(value, axis, join):
    pieces = jax.tree.map(lambda part: lax.all_gather(part, axis), value)
    head = jax.tree.map(lambda part: part[0], pieces)
    tail = jax.tree.map(lambda part: part[1:], pieces)
    running, _ = lax.scan(lambda running, piece: (join(running, piece), None), head, tail)
    return running


def matmul_low(form, left, right):
    return jnp.einsum(form, left, right, preferred_element_type=jnp.float32)


def matmul_high(form, left, right):
    return jnp.einsum(form, left, right, precision=lax.Precision.HIGHEST)


def layer_norm(values, gain_row, shift_row):
    centred = values - jnp.mean(values, -1, keepdims=True)
    inverse_std = lax.rsqrt(jnp.mean(centred * centred, -1, keepdims=True) + NORM_EPSILON)
    return centred * inverse_std * gain_row + shift_row


def norm_back(values, gain_row, grad_out):
    centred = values - jnp.mean(values, -1, keepdims=True)
    inverse_std = lax.rsqrt(jnp.mean(centred * centred, -1, keepdims=True) + NORM_EPSILON)
    normed = centred * inverse_std
    scaled_grad = grad_out * gain_row
    grad_in = inverse_std * (
        scaled_grad
        - jnp.mean(scaled_grad, -1, keepdims=True)
        - normed * jnp.mean(scaled_grad * normed, -1, keepdims=True)
    )
    leading = tuple(range(values.ndim - 1))
    return (grad_in, jnp.sum(grad_out * normed, leading), jnp.sum(grad_out, leading))


def gelu_exact(values):
    return 0.5 * values * (1.0 + lax.erf(values * ROOT_HALF))


def gelu_slope(values):
    return (
        0.5 * (1.0 + lax.erf(values * ROOT_HALF))
        + values * jnp.exp(-0.5 * values * values) * DENSITY_SCALE
    )


def layer_bounds(devices):
    widths = [3 * D // devices, D // devices, MLP // devices, MLP // devices]
    lowers = [0, widths[0], widths[0] + widths[1], widths[0] + widths[1] + widths[2]]
    return [(lowers[segment], lowers[segment] + widths[segment]) for segment in range(4)]


def split_layer(weights, devices):
    blocks = weights.reshape(devices, -1, D)
    return [
        blocks[:, lower_row:upper_row].reshape(-1, D)
        for lower_row, upper_row in layer_bounds(devices)
    ]


def join_layer(members, devices):
    return jnp.concatenate([member.reshape(devices, -1, D) for member in members], 1).reshape(-1, D)


def layer_parts(inputs, matrices, vectors):
    joint_weight, output_weight, inner_weight, outer_weight = matrices
    images, tokens = (inputs.shape[0], inputs.shape[1])
    normed = layer_norm(inputs, vectors[0], vectors[1]).astype(jnp.bfloat16)
    joint = matmul_low("itd,ed->ite", normed, joint_weight).astype(jnp.bfloat16)
    head_split = joint.reshape(images, tokens, 3, HEADS, HEAD_DIM)
    queries, keys_in, values_in = (head_split[:, :, 0], head_split[:, :, 1], head_split[:, :, 2])
    scores = matmul_low("ithd,ishd->ihts", queries, keys_in) * HEAD_DIM ** (-0.5)
    attention = jax.nn.softmax(scores, axis=-1)
    mixed_heads = (
        matmul_low("ihts,ishd->ithd", attention.astype(jnp.bfloat16), values_in)
        .astype(jnp.bfloat16)
        .reshape(images, tokens, D)
    )
    attended = matmul_low("itd,ed->ite", mixed_heads, output_weight)
    middle = inputs + vectors[4] * attended
    normed_two = layer_norm(middle, vectors[2], vectors[3]).astype(jnp.bfloat16)
    inner_pre = matmul_low("itd,md->itm", normed_two, inner_weight)
    activated = gelu_exact(inner_pre).astype(jnp.bfloat16)
    outer_out = matmul_low("itm,md->itd", activated, outer_weight)
    result = middle + vectors[5] * outer_out
    return (
        normed,
        queries,
        keys_in,
        values_in,
        attention,
        mixed_heads,
        attended,
        middle,
        normed_two,
        inner_pre,
        activated,
        outer_out,
        result,
    )


def layer_backward(inputs, matrices, vectors, grad_result):
    joint_weight, output_weight, inner_weight, outer_weight = matrices
    (
        normed,
        queries,
        keys_in,
        values_in,
        attention,
        mixed_heads,
        attended,
        middle,
        normed_two,
        inner_pre,
        activated,
        outer_out,
        result,
    ) = layer_parts(inputs, matrices, vectors)
    images, tokens = (inputs.shape[0], inputs.shape[1])
    grad_outer = (vectors[5] * grad_result).astype(jnp.bfloat16)
    grad_scale_two = jnp.sum(grad_result * outer_out, (0, 1))
    grad_outer_weight = matmul_low("itm,itd->md", activated, grad_outer)
    grad_activated = matmul_low("itd,md->itm", grad_outer, outer_weight)
    grad_inner = (grad_activated * gelu_slope(inner_pre)).astype(jnp.bfloat16)
    grad_inner_weight = matmul_low("itm,itd->md", grad_inner, normed_two)
    grad_normed_two = matmul_low("itm,md->itd", grad_inner, inner_weight)
    grad_middle_norm, grad_gain_two, grad_shift_two = norm_back(middle, vectors[2], grad_normed_two)
    grad_middle = grad_result + grad_middle_norm
    grad_attended = (vectors[4] * grad_middle).astype(jnp.bfloat16)
    grad_scale_one = jnp.sum(grad_middle * attended, (0, 1))
    grad_output_weight = matmul_low("ite,itd->ed", grad_attended, mixed_heads)
    grad_mixed = (
        matmul_low("ite,ed->itd", grad_attended, output_weight)
        .astype(jnp.bfloat16)
        .reshape(images, tokens, HEADS, HEAD_DIM)
    )
    grad_attention = matmul_low("ithd,ishd->ihts", grad_mixed, values_in)
    grad_values = matmul_low("ihts,ithd->ishd", attention.astype(jnp.bfloat16), grad_mixed)
    grad_scores = (
        attention * (grad_attention - jnp.sum(attention * grad_attention, -1, keepdims=True))
    ).astype(jnp.bfloat16)
    grad_queries = matmul_low("ihts,ishd->ithd", grad_scores, keys_in) * HEAD_DIM ** (-0.5)
    grad_keys = matmul_low("ihts,ithd->ishd", grad_scores, queries) * HEAD_DIM ** (-0.5)
    grad_joint = (
        jnp.stack([grad_queries, grad_keys, grad_values], 2)
        .astype(jnp.bfloat16)
        .reshape(images, tokens, 3 * D)
    )
    grad_joint_weight = matmul_low("ite,itd->ed", grad_joint, normed)
    grad_normed = matmul_low("ite,ed->itd", grad_joint, joint_weight)
    grad_input_norm, grad_gain_one, grad_shift_one = norm_back(inputs, vectors[0], grad_normed)
    grad_vectors = jnp.stack(
        [
            grad_gain_one,
            grad_shift_one,
            grad_gain_two,
            grad_shift_two,
            grad_scale_one,
            grad_scale_two,
        ]
    )
    return (
        grad_middle + grad_input_norm,
        (grad_joint_weight, grad_output_weight, grad_inner_weight, grad_outer_weight),
        grad_vectors,
    )


def table_vectors(embed_table):
    return embed_table[PIX + SEQ : PIX + SEQ + 6 * LAYERS].astype(jnp.float32).reshape(LAYERS, 6, D)


def table_tail(embed_table):
    return embed_table[PIX + SEQ + 6 * LAYERS :].astype(jnp.float32)


def backbone(patches, embed_table, layer_stack, devices):
    vectors = table_vectors(embed_table)
    tail_rows = table_tail(embed_table)
    position = embed_table[PIX : PIX + SEQ].astype(jnp.float32)
    projected = matmul_low("ipc,cd->ipd", patches, embed_table[:PIX]) + tail_rows[0]
    leading = jnp.broadcast_to(tail_rows[1] + position[0], (patches.shape[0], 1, D))
    current = jnp.concatenate([leading, projected + position[1:]], 1)
    layer_inputs = []
    for layer_number in range(LAYERS):
        layer_inputs.append(current)
        current = layer_parts(
            current, split_layer(layer_stack[layer_number], devices), vectors[layer_number]
        )[-1]
    features = layer_norm(current[:, 0], tail_rows[2], tail_rows[3]).astype(jnp.bfloat16)
    return (features, layer_inputs, current)


def unchanged(values):
    return values


def backbone_back(
    patches,
    embed_table,
    layer_stack,
    layer_inputs,
    final_state,
    grad_features,
    devices,
    reduce_layer,
):
    vectors = table_vectors(embed_table)
    tail_rows = table_tail(embed_table)
    grad_cls, grad_gain, grad_shift = norm_back(final_state[:, 0], tail_rows[2], grad_features)
    grad_current = jnp.concatenate(
        [grad_cls[:, None], jnp.zeros((final_state.shape[0], SEQ - 1, D), jnp.float32)], 1
    )
    weight_grads = [None] * LAYERS
    vector_grads = [None] * LAYERS
    for layer_number in reversed(range(LAYERS)):
        grad_current, matrices, grad_vectors = layer_backward(
            layer_inputs[layer_number],
            split_layer(layer_stack[layer_number], devices),
            vectors[layer_number],
            grad_current,
        )
        weight_grads[layer_number] = reduce_layer(join_layer(matrices, devices))
        vector_grads[layer_number] = grad_vectors
    grad_patch_weight = matmul_low("ipc,ipd->cd", patches, grad_current[:, 1:].astype(jnp.bfloat16))
    grad_position = jnp.sum(grad_current, 0)
    tail_grads = jnp.stack(
        [
            jnp.sum(grad_current[:, 1:], (0, 1)),
            jnp.sum(grad_current[:, 0], 0),
            grad_gain,
            grad_shift,
        ]
    )
    grad_table = jnp.concatenate(
        [grad_patch_weight, grad_position, jnp.concatenate(vector_grads, 0), tail_grads], 0
    )
    return (grad_table, jnp.stack(weight_grads))


def unit_rows(bottle):
    inverse_norm = lax.rsqrt(jnp.sum(bottle * bottle, -1, keepdims=True) + UNIT_EPSILON)
    return (bottle * inverse_norm, inverse_norm)


def combine_parts(left_part, right_part):
    top_student = jnp.maximum(left_part[0], right_part[0])
    total_student = left_part[1] * jnp.exp(left_part[0] - top_student) + right_part[1] * jnp.exp(
        right_part[0] - top_student
    )
    top_teacher = jnp.maximum(left_part[2], right_part[2])
    left_weight = jnp.exp(left_part[2] - top_teacher)
    right_weight = jnp.exp(right_part[2] - top_teacher)
    return (
        top_student,
        total_student,
        top_teacher,
        left_part[3] * left_weight + right_part[3] * right_weight,
        left_part[4] * left_weight + right_part[4] * right_weight,
    )


def adam_step(weight, grad, first_moment, second_moment, rate, decay):
    first_new = BETA_ONE * first_moment + (1.0 - BETA_ONE) * grad
    second_new = BETA_TWO * second_moment + (1.0 - BETA_TWO) * grad * grad
    direction = (
        first_new
        / (1.0 - BETA_ONE**STEP)
        / (jnp.sqrt(second_new / (1.0 - BETA_TWO**STEP)) + ADAM_EPSILON)
    )
    return (first_new, second_new, weight - rate * (direction + decay * weight))


def renew(stat_matrix, basis):
    scaled = jnp.dot(stat_matrix, basis, precision=lax.Precision.HIGHEST) * (
        D / jnp.trace(stat_matrix)
    )
    gram = jnp.dot(scaled.T, scaled, precision=lax.Precision.HIGHEST)
    lower_factor = jnp.linalg.cholesky(gram)
    return lax.linalg.triangular_solve(lower_factor, scaled.T, left_side=True, lower=True).T


def nothing(stat_matrix, basis):
    return jnp.zeros_like(basis)


def follow(teacher_weight, student_weight):
    return TEACHER_MOMENTUM * teacher_weight + (1.0 - TEACHER_MOMENTUM) * student_weight


def per_device(
    patches,
    valid_mask,
    owners,
    embedding,
    embedding_first,
    embedding_second,
    layers,
    layers_first,
    layers_second,
    layer_stats,
    layer_bases,
    head_hidden,
    hidden_first,
    hidden_second,
    head_last,
    last_first,
    last_second,
    protos,
    protos_first,
    protos_second,
    teacher_embedding,
    teacher_layers,
    teacher_hidden,
    teacher_last,
    teacher_protos,
    centre,
):
    devices = lax.axis_size("dp")
    device_index = lax.axis_index("dp")
    fetched = (
        lax.all_gather(embedding.astype(jnp.bfloat16), "dp", axis=1, tiled=True),
        lax.all_gather(layers.astype(jnp.bfloat16), "dp", axis=1, tiled=True),
        lax.all_gather(teacher_embedding.astype(jnp.bfloat16), "dp", axis=1, tiled=True),
        lax.all_gather(teacher_layers.astype(jnp.bfloat16), "dp", axis=1, tiled=True),
    )
    stats_full, bases_full = (
        lax.all_gather(layer_stats.astype(jnp.bfloat16), "dp", axis=2, tiled=True).astype(
            layer_stats.dtype
        ),
        lax.all_gather(layer_bases.astype(jnp.bfloat16), "dp", axis=2, tiled=True).astype(
            layer_bases.dtype
        ),
    )
    embed_table, layer_full = (fetched[0], fetched[1])
    features, layer_inputs, final_state = backbone(patches, embed_table, layer_full, devices)
    teacher_features, unused_inputs, unused_final = backbone(
        patches, fetched[2], fetched[3], devices
    )
    all_features, all_teacher = (
        lax.all_gather(features, "dp", axis=0, tiled=True),
        lax.all_gather(teacher_features, "dp", axis=0, tiled=True),
    )
    first_weight = head_hidden[:, :D].astype(jnp.bfloat16)
    second_weight = head_hidden[:, D:].astype(jnp.bfloat16)
    last_weight = head_last.astype(jnp.bfloat16)
    proto_weight = protos.astype(jnp.bfloat16)
    teacher_first = teacher_hidden[:, :D].astype(jnp.bfloat16)
    teacher_second = teacher_hidden[:, D:].astype(jnp.bfloat16)
    pre_one = matmul_low("bd,hd->bh", all_features, first_weight)
    teacher_pre_one = matmul_low("bd,hd->bh", all_teacher, teacher_first)
    act_one = (
        lax.all_gather(gelu_exact(pre_one).astype(jnp.bfloat16), "dp", axis=1, tiled=True),
        lax.all_gather(gelu_exact(teacher_pre_one).astype(jnp.bfloat16), "dp", axis=1, tiled=True),
    )
    pre_two = matmul_low("bh,kh->bk", act_one[0], second_weight)
    teacher_pre_two = matmul_low("bh,kh->bk", act_one[1], teacher_second)
    act_two = (
        lax.all_gather(gelu_exact(pre_two).astype(jnp.bfloat16), "dp", axis=1, tiled=True),
        lax.all_gather(gelu_exact(teacher_pre_two).astype(jnp.bfloat16), "dp", axis=1, tiled=True),
    )
    bottles = (
        lax.all_gather(matmul_low("bh,hc->bc", act_two[0], last_weight), "dp", axis=1, tiled=True),
        lax.all_gather(
            matmul_low("bh,hc->bc", act_two[1], teacher_last.astype(jnp.bfloat16)),
            "dp",
            axis=1,
            tiled=True,
        ),
    )
    unit, inverse_norm = unit_rows(bottles[0])
    teacher_unit, unused_norm = unit_rows(bottles[1])
    unit_low = unit.astype(jnp.bfloat16)
    logits = matmul_low("bc,cp->bp", unit_low, proto_weight)
    teacher_logits = matmul_low(
        "bc,cp->bp", teacher_unit.astype(jnp.bfloat16), teacher_protos.astype(jnp.bfloat16)
    )
    scaled = logits / TAU_STUDENT
    student_top = jnp.max(scaled, -1)
    student_total = jnp.sum(jnp.exp(scaled - student_top[:, None]), -1)
    sharpened = (teacher_logits - centre) / TAU_TEACHER
    teacher_top = jnp.max(sharpened, -1)
    teacher_exp = jnp.exp(sharpened - teacher_top[:, None])
    merged = joined(
        (
            student_top,
            student_total,
            teacher_top,
            jnp.sum(teacher_exp, -1),
            jnp.sum(teacher_exp * scaled, -1),
        ),
        "dp",
        combine_parts,
    )
    log_total = merged[0] + jnp.log(merged[1])
    counted = valid_mask.astype(jnp.float32)
    loss_count = jnp.sum(counted)
    loss_sum = jnp.sum(counted * (log_total - merged[4] / merged[3]))
    student_prob = jnp.exp(scaled - log_total[:, None])
    teacher_prob = jnp.exp(sharpened - merged[2][:, None]) / merged[3][:, None]
    grad_logits = (
        (counted / loss_count)[:, None] * (student_prob - teacher_prob) / TAU_STUDENT
    ).astype(jnp.bfloat16)
    grad_protos = matmul_low("bc,bp->cp", unit_low, grad_logits)
    grad_unit = lax.psum(matmul_low("bp,cp->bc", grad_logits, proto_weight), "dp")
    grad_bottle = inverse_norm * (grad_unit - unit * jnp.sum(unit * grad_unit, -1, keepdims=True))
    last_width = head_last.shape[1]
    grad_bottle_own = lax.dynamic_slice_in_dim(
        grad_bottle, device_index * last_width, last_width, 1
    ).astype(jnp.bfloat16)
    grad_last = matmul_low("bh,bc->hc", act_two[0], grad_bottle_own)
    grad_act_two = lax.psum_scatter(
        matmul_low("bc,hc->bh", grad_bottle_own, last_weight), "dp", scatter_dimension=1, tiled=True
    )
    grad_pre_two = (grad_act_two * gelu_slope(pre_two)).astype(jnp.bfloat16)
    grad_second = matmul_low("bk,bh->kh", grad_pre_two, act_one[0])
    grad_act_one = lax.psum_scatter(
        matmul_low("bk,kh->bh", grad_pre_two, second_weight), "dp", scatter_dimension=1, tiled=True
    )
    grad_pre_one = (grad_act_one * gelu_slope(pre_one)).astype(jnp.bfloat16)
    grad_first = matmul_low("bh,bd->hd", grad_pre_one, all_features)
    grad_features = lax.psum_scatter(
        matmul_low("bh,hd->bd", grad_pre_one, first_weight), "dp", scatter_dimension=0, tiled=True
    )
    layer_again = lax.all_gather(layers.astype(jnp.bfloat16), "dp", axis=1, tiled=True)
    grad_table, grad_layers = backbone_back(
        patches,
        embed_table,
        layer_again,
        layer_inputs,
        final_state,
        grad_features,
        devices,
        unchanged,
    )
    summed = (
        lax.psum_scatter(grad_table, "dp", scatter_dimension=1, tiled=True),
        lax.psum_scatter(grad_layers, "dp", scatter_dimension=1, tiled=True),
    )
    grad_embed = summed[0]
    grad_layers_own = summed[1]
    grad_hidden = jnp.concatenate([grad_first, grad_second], 1)
    bounds = layer_bounds(devices)
    grams = jnp.stack(
        [
            matmul_high(
                "lcd,lce->lde",
                grad_layers_own[:, lower_row:upper_row],
                grad_layers_own[:, lower_row:upper_row],
            )
            for lower_row, upper_row in bounds
        ],
        1,
    )
    squares = (
        jnp.sum(grad_embed * grad_embed)
        + jnp.sum(grad_layers_own * grad_layers_own)
        + jnp.sum(grad_hidden * grad_hidden)
        + jnp.sum(grad_last * grad_last)
        + jnp.sum(grad_protos * grad_protos)
    )
    totals = lax.psum((squares, grams), "dp")
    grad_norm = jnp.sqrt(totals[0])
    clip_factor = jnp.minimum(1.0, CLIP_MAX / (grad_norm + 1e-06))
    next_stats = (
        BETA_STAT * stats_full + (1.0 - BETA_STAT) * (clip_factor * clip_factor) * totals[1]
    )
    rows = jnp.arange(embedding.shape[0])[:, None]
    is_matrix = rows < PIX + SEQ
    embed_out = adam_step(
        embedding,
        clip_factor * grad_embed,
        embedding_first,
        embedding_second,
        jnp.where(is_matrix, RATE_MATRIX, RATE_VECTOR),
        jnp.where(is_matrix, WEIGHT_DECAY, 0.0),
    )
    hidden_out = adam_step(
        head_hidden,
        clip_factor * grad_hidden,
        hidden_first,
        hidden_second,
        RATE_MATRIX,
        WEIGHT_DECAY,
    )
    last_out = adam_step(
        head_last, clip_factor * grad_last, last_first, last_second, RATE_MATRIX, WEIGHT_DECAY
    )
    protos_out = adam_step(
        protos, clip_factor * grad_protos, protos_first, protos_second, RATE_MATRIX, WEIGHT_DECAY
    )
    firsts, seconds, weights_new = ([], [], [])
    for segment, (lower_row, upper_row) in enumerate(bounds):
        basis = bases_full[:, segment]
        weight_block = layers[:, lower_row:upper_row]
        rotated = matmul_high(
            "lcd,ldk->lck", clip_factor * grad_layers_own[:, lower_row:upper_row], basis
        )
        first_new = BETA_ONE * layers_first[:, lower_row:upper_row] + (1.0 - BETA_ONE) * rotated
        second_new = (
            BETA_TWO * layers_second[:, lower_row:upper_row] + (1.0 - BETA_TWO) * rotated * rotated
        )
        direction = (
            first_new
            / (1.0 - BETA_ONE**STEP)
            / (jnp.sqrt(second_new / (1.0 - BETA_TWO**STEP)) + ADAM_EPSILON)
        )
        update = matmul_high("lck,ldk->lcd", direction, basis)
        firsts.append(first_new)
        seconds.append(second_new)
        weights_new.append(weight_block - RATE_MATRIX * (update + WEIGHT_DECAY * weight_block))
    next_layers = jnp.concatenate(weights_new, 1)
    flat_stats = next_stats.reshape(-1, D, D)
    flat_bases = bases_full.reshape(-1, D, D)

    def renew_owned(operands):
        return lax.cond(operands[2] == device_index, renew, nothing, operands[0], operands[1])

    renewed = lax.psum(lax.map(renew_owned, (flat_stats, flat_bases, owners)), "dp")
    next_bases = jnp.where(owners[:, None, None] >= 0, renewed, flat_bases).reshape(
        bases_full.shape
    )
    own_rows = layer_stats.shape[2]
    stats_own = lax.dynamic_slice_in_dim(next_stats, device_index * own_rows, own_rows, 2)
    bases_own = lax.dynamic_slice_in_dim(next_bases, device_index * own_rows, own_rows, 2)
    next_centre = (
        CENTRE_MOMENTUM * centre
        + (1.0 - CENTRE_MOMENTUM) * jnp.sum(counted[:, None] * teacher_logits, 0) / loss_count
    )
    return (
        loss_sum,
        loss_count,
        grad_norm,
        embed_out[0],
        embed_out[1],
        embed_out[2],
        jnp.concatenate(firsts, 1),
        jnp.concatenate(seconds, 1),
        next_layers,
        stats_own,
        bases_own,
        hidden_out[0],
        hidden_out[1],
        hidden_out[2],
        last_out[0],
        last_out[1],
        last_out[2],
        protos_out[0],
        protos_out[1],
        protos_out[2],
        follow(teacher_embedding, embed_out[2]),
        follow(teacher_layers, next_layers),
        follow(teacher_hidden, hidden_out[2]),
        follow(teacher_last, last_out[2]),
        follow(teacher_protos, protos_out[2]),
        next_centre,
    )


def solution(mesh):
    placed = (
        P("dp", None, None),
        P(),
        P(),
        P(None, "dp"),
        P(None, "dp"),
        P(None, "dp"),
        P(None, "dp", None),
        P(None, "dp", None),
        P(None, "dp", None),
        P(None, None, "dp", None),
        P(None, None, "dp", None),
        P("dp", None),
        P("dp", None),
        P("dp", None),
        P(None, "dp"),
        P(None, "dp"),
        P(None, "dp"),
        P(None, "dp"),
        P(None, "dp"),
        P(None, "dp"),
        P(None, "dp"),
        P(None, "dp", None),
        P("dp", None),
        P(None, "dp"),
        P(None, "dp"),
        P("dp"),
    )
    return jax.shard_map(
        per_device,
        mesh=mesh,
        in_specs=placed,
        out_specs=(
            P(),
            P(),
            P(),
            P(None, "dp"),
            P(None, "dp"),
            P(None, "dp"),
            P(None, "dp", None),
            P(None, "dp", None),
            P(None, "dp", None),
            P(None, None, "dp", None),
            P(None, None, "dp", None),
            P("dp", None),
            P("dp", None),
            P("dp", None),
            P(None, "dp"),
            P(None, "dp"),
            P(None, "dp"),
            P(None, "dp"),
            P(None, "dp"),
            P(None, "dp"),
            P(None, "dp"),
            P(None, "dp", None),
            P("dp", None),
            P(None, "dp"),
            P(None, "dp"),
            P("dp"),
        ),
        check_vma=False,
    )
```

profile of v0, /device:TPU:31, one launch (start us, length us, event | category | flops | bytes accessed | tf_op | source)
XLA Modules:
  0.0 2498.6 jit_solution(7646922607172854492)
XLA Ops:
  10.2 39.4 %all-gather.5 = bf16[32,12,867]{2,1,0:T(8,128)(2,1)S(1)} all-gather(bf16[1,12,867]{2,1,0:T(8,128)(2,1)S(1)} %convert_bitcast_fusion.1), channel_id=1, replica_groups=mesh['dp'=32] {'dp'}, dimensions={0}, use_global_device_ids=true | all-gather | bytes 686664 | tf_op jit(solution)/shard_map/all_gather | solution.py:357
  50.4 45.1 %all-gather.7 = bf16[32,12,867]{2,1,0:T(8,128)(2,1)S(1)} all-gather(bf16[1,12,867]{2,1,0:T(8,128)(2,1)S(1)} %convert_bitcast_fusion), channel_id=1, replica_groups=mesh['dp'=32] {'dp'}, dimensions={0}, use_global_device_ids=true | all-gather | bytes 686664 | tf_op jit(solution)/shard_map/all_gather | solution.py:359
  125.6 69.3 %all-gather.14.cloned.1.call-done = bf16[3,4608,384]{2,1,0:T(8,128)(2,1)} async-done(((bf16[3,144,384]{2,1,0:T(8,128)(2,1)}), bf16[3,4608,384]{2,1,0:T(8,128)(2,1)}) %all-gather.14.cloned.1.call-update) | async-done | bytes 10616848 | tf_op jit(solution)/shard_map/all_gather | solution.py:358
  419.1 38.7 %all-gather.6 = bf16[32,3,384]{2,1,0:T(4,128)(2,1)} all-gather(bf16[1,3,384]{2,1,0:T(4,128)(2,1)S(1)} %fusion.334), channel_id=1, replica_groups=mesh['dp'=32] {'dp'}, dimensions={0}, use_global_device_ids=true | all-gather | bytes 76032 | tf_op jit(solution)/shard_map/all_gather | solution.py:376
  460.4 40.4 %all_gather.76 = bf16[96,2048]{0,1:T(8,128)(2,1)S(1)} all-gather(bf16[96,64]{0,1:T(8,128)(2,1)S(1)} %get-tuple-element.540), channel_id=1, replica_groups=mesh['dp'=32] {'dp'}, dimensions={1}, use_global_device_ids=true | all-gather | bytes 405504 | tf_op jit(solution)/shard_map/all_gather | solution.py:388
  503.3 38.0 %all_gather.77 = bf16[96,2048]{0,1:T(8,128)(2,1)S(1)} all-gather(bf16[96,64]{0,1:T(8,128)(2,1)S(1)} %get-tuple-element.542), channel_id=1, replica_groups=mesh['dp'=32] {'dp'}, dimensions={1}, use_global_device_ids=true | all-gather | bytes 405504 | tf_op jit(solution)/shard_map/all_gather | solution.py:394
  542.3 38.3 %all_gather.78 = f32[96,256]{0,1:T(8,128)S(1)} all-gather(f32[96,8]{0,1:T(8,128)S(1)} %fusion.325), channel_id=1, replica_groups=mesh['dp'=32] {'dp'}, dimensions={1}, use_global_device_ids=true | all-gather | bytes 101376 | tf_op jit(solution)/shard_map/all_gather | solution.py:398
  582.9 39.5 %all-gather.8 = bf16[32,3,384]{2,1,0:T(4,128)(2,1)} all-gather(bf16[1,3,384]{2,1,0:T(4,128)(2,1)S(1)} %fusion.335), channel_id=1, replica_groups=mesh['dp'=32] {'dp'}, dimensions={0}, use_global_device_ids=true | all-gather | bytes 76032 | tf_op jit(solution)/shard_map/all_gather | solution.py:377
  625.3 39.4 %all_gather.86 = bf16[96,2048]{0,1:T(8,128)(2,1)S(1)} all-gather(bf16[96,64]{0,1:T(8,128)(2,1)S(1)} %multiply_convert_fusion.19), channel_id=1, replica_groups=mesh['dp'=32] {'dp'}, dimensions={1}, use_global_device_ids=true | all-gather | bytes 405504 | tf_op jit(solution)/shard_map/all_gather | solution.py:389
  665.9 38.1 %all_gather.87 = bf16[96,2048]{0,1:T(8,128)(2,1)S(1)} all-gather(bf16[96,64]{0,1:T(8,128)(2,1)S(1)} %multiply_convert_fusion.18), channel_id=1, replica_groups=mesh['dp'=32] {'dp'}, dimensions={1}, use_global_device_ids=true | all-gather | bytes 405504 | tf_op jit(solution)/shard_map/all_gather | solution.py:395
  705.0 38.3 %all_gather.88 = f32[96,256]{0,1:T(8,128)S(1)} all-gather(f32[96,8]{0,1:T(8,128)S(1)} %fusion.313), channel_id=1, replica_groups=mesh['dp'=32] {'dp'}, dimensions={1}, use_global_device_ids=true | all-gather | bytes 101376 | tf_op jit(solution)/shard_map/all_gather | solution.py:399
  752.6 39.7 %all-reduce.9 = (f32[3072]{0:T(1024)}, f32[3072]{0:T(1024)}, f32[3072]{0:T(1024)}, f32[3072]{0:T(1024)}, f32[3072]{0:T(1024)}) all-reduce(f32[3072]{0:T(1024)S(1)} %dynamic-update-slice.25, f32[3072]{0:T(1024)S(1)} %dynamic-update-slice.26, f32[3072]{0:T(1024)S(1)} %dynamic-update-slice.27, ...), channel_id=2, replica_groups=mesh['dp'=32] {'dp'}, use_global_device_ids=true, to_apply=%add.2 | all-reduce | flops 15360 | bytes 122880
  803.9 76.8 %while.30 = (s32[]{:T(128)}, f32[96]{0:T(128)}, f32[96]{0:T(128)}, f32[96]{0:T(128)S(1)}, f32[96]{0:T(128)}, /*index=5*/f32[96]{0:T(128)}, f32[31,96]{1,0:T(8,12...) while((s32[]{:T(128)}, f32[96]{0:T(128)}, f32[96]{0:T(128)}, ...), condition=%wide.region_48.49_spmd, body=%wide.region_47.48_spmd.sunk | while | flops 1634 | bytes 7813 | solution.py:38
  888.7 123.3 %all-reduce.16.cloned.1.call-done = f32[96,256]{0,1:T(8,128)} async-done(((f32[96,256]{0,1:T(8,128)}), f32[96,256]{0,1:T(8,128)}) %all-reduce.16.cloned.1.call-update) | async-done | bytes 98320 | tf_op jit(solution)/shard_map/psum | solution.py:440
  1015.6 131.7 %reduce-scatter.5.cloned.1.call-done = f32[96,64]{0,1:T(8,128)} async-done(((f32[96,2048]{0,1:T(8,128)}), f32[96,64]{0,1:T(8,128)}) %reduce-scatter.5.cloned.1.call-update) | async-done | bytes 24592 | tf_op jit(solution)/shard_map/reduce_scatter | solution.py:447
  1152.9 127.9 %reduce-scatter.7.cloned.1.call-done = f32[96,64]{0,1:T(8,128)} async-done(((f32[96,2048]{0,1:T(8,128)}), f32[96,64]{0,1:T(8,128)}) %reduce-scatter.7.cloned.1.call-update) | async-done | bytes 24592 | tf_op jit(solution)/shard_map/reduce_scatter | solution.py:452
  1286.2 121.2 %all-reduce.20.cloned.1.call-done = f32[96,384]{1,0:T(8,128)} async-done(((f32[96,384]{1,0:T(8,128)}), f32[96,384]{1,0:T(8,128)}) %all-reduce.20.cloned.1.call-update) | async-done | bytes 147472
  1660.7 203.3 %reduce-scatter.9.cloned.1.call-done = f32[3,144,384]{2,1,0:T(8,128)} async-done(((f32[3,4608,384]{2,1,0:T(8,128)}), f32[3,144,384]{2,1,0:T(8,128)}) %reduce-scatter.9.cloned.1.call-update) | async-done | bytes 663568 | tf_op jit(solution)/shard_map/reduce_scatter | solution.py:473
  1876.4 51.2 %all-gather.18.cloned.1.call-done = bf16[3,4,384,384]{3,1,0,2:T(4,128)(2,1)} async-done(((bf16[3,4,12,384]{3,1,0,2:T(4,128)(2,1)}), bf16[3,4,384,384]{3,1,0,2:T(4,128)(2,1)}) %all-gather.18.cloned.1.call-update) | async-done | bytes 3538960 | tf_op jit(solution)/shard_map/all_gather | solution.py:366
  1949.0 166.0 %all-reduce.22.cloned.1.call-done = (f32[867,384]{1,0:T(8,128)}, f32[3,4,384,384]{3,2,0,1:T(8,128)}) async-done(((f32[867,384]{1,0:T(8,128)}, f32[3,4,384,384]{3,2,0,1:T(8,128)}), (f32[867,384]{1,0:T(8,128)}, f32[3,4,384,384]{3,2,0,1:T(8,128)})) %all-reduce.22.cloned.1.call-update) | async-done | bytes 8409616
  2122.1 39.2 %psum.29 = f32[]{:T(128)} all-reduce(f32[]{:T(128)S(6)} %add.801), channel_id=1, replica_groups=mesh['dp'=32] {'dp'}, use_global_device_ids=true, to_apply=%region_103.104 | all-reduce | flops 1 | bytes 8 | tf_op jit(solution)/shard_map/psum | solution.py:497
  2187.9 133.2 %while.31 = (s32[]{:T(128)}, f32[12,384,384]{2,1,0:T(8,128)}, s32[12]{0:T(128)S(1)}, s32[]{:T(128)}, f32[12,384,384]{2,1,0:T(8,128)}, /*index=5*/f32[12,384,384]{2,1,0:T(8,128)}, s32[]{:T(128)}) while((s32[]{:T(128)}, f32[12,384,384]{2,1,0:T(8,128)}, s32[12]{0:T(128)S(1)}, s32[]{:T(128)}, f32[12,384,384]{2,1,0:T(8,128)}, ...), condition=%wide.region_115.116_spmd, body=%wide.region_105.115_spmd.sunk | while | flops 1990328704 | bytes 17044360 | solution.py:554
  2203.7 104.0 %conditional.2 = (f32[1,384,384]{1,2,0:T(8,128)S(1)}) conditional(s32[]{:T(128)} %convert_element_type.623, () %tuple.223, (f32[12,384,384]{2,1,0:T(8,128)}, s32[]{:T(128)}, f32[12,384,384]{2,1,0:T(8,128)}) %tuple.224), branch_computations={%region_106.106_spmd, %region_107.114_spmd} | conditional | flops 1990328704 | bytes 14684419 | solution.py:552
  2359.4 125.5 %all-reduce.18.cloned.1.call-done = f32[12,384,384]{2,1,0:T(8,128)} async-done(((f32[12,384,384]{2,1,0:T(8,128)}), f32[12,384,384]{2,1,0:T(8,128)}) %all-reduce.18.cloned.1.call-update) | async-done | bytes 7077904 | tf_op jit(solution)/shard_map/psum | solution.py:554
  (1143 shorter events, 877.2 us)
Async XLA Ops:
  7.2 102.9 %all-gather.16.cloned.1.call-start = ((), (), s32[]{:S(2)}) async-start(), calls=%async_computation.4 | async-start | bytes 10948608 | tf_op jit(solution)/shard_map/all_gather | solution.py:360
  9.3 185.6 %all-gather.14.cloned.1.call-start = ((), (), s32[]{:S(2)}) async-start(), calls=%async_computation.3 | async-start | bytes 10948608 | tf_op jit(solution)/shard_map/all_gather | solution.py:358
  10.1 1001.9 %all-reduce.16.cloned.1.call-start = ((), (), s32[]{:S(2)}) async-start(), calls=%async_computation.5 | async-start | bytes 262144 | tf_op jit(solution)/shard_map/psum | solution.py:440
  106.8 214.7 %copy-start.17 = (f32[3,256,384]{2,1,0:T(8,128)}, f32[3,256,384]{2,1,0:T(8,128)S(1)}, u32[]{:S(2)}) copy-start(f32[3,256,384]{2,1,0:T(8,128)S(1)} %fusion.128) | copy-start | bytes 3538948
  106.8 214.7 %copy-start.181 = (f32[3,1,384]{2,1,0:T(1,128)}, f32[3,1,384]{2,1,0:T(1,128)S(1)}, u32[]{:S(2)}) copy-start(f32[3,1,384]{2,1,0:T(1,128)S(1)} %broadcast_in_dim.38) | copy-start | bytes 13828
  109.1 214.6 %copy-start.209 = (f32[384]{0:T(512)}, f32[384]{0:T(512)S(1)}, u32[]{:S(2)}) copy-start(f32[384]{0:T(512)S(1)} %get-tuple-element.364) | copy-start | bytes 4612
  109.1 214.6 %copy-start.228 = (f32[384]{0:T(512)}, f32[384]{0:T(512)S(1)}, u32[]{:S(2)}) copy-start(f32[384]{0:T(512)S(1)} %get-tuple-element.363) | copy-start | bytes 4612
  109.1 219.8 %copy-start.217 = (f32[384]{0:T(512)}, f32[384]{0:T(512)S(1)}, u32[]{:S(2)}) copy-start(f32[384]{0:T(512)S(1)} %get-tuple-element.365) | copy-start | bytes 4612
  109.2 246.7 %copy-start.199 = (f32[384]{0:T(512)}, f32[384]{0:T(512)S(1)}, u32[]{:S(2)}) copy-start(f32[384]{0:T(512)S(1)} %get-tuple-element.362) | copy-start | bytes 4612
  109.2 250.6 %copy-start.205 = (f32[384]{0:T(512)}, f32[384]{0:T(512)S(1)}, u32[]{:S(2)}) copy-start(f32[384]{0:T(512)S(1)} %get-tuple-element.358) | copy-start | bytes 4612
  109.2 264.4 %copy-start.191 = (f32[384]{0:T(512)}, f32[384]{0:T(512)S(1)}, u32[]{:S(2)}) copy-start(f32[384]{0:T(512)S(1)} %get-tuple-element.355) | copy-start | bytes 4612
  888.6 258.6 %reduce-scatter.5.cloned.1.call-start = ((), (), s32[]{:S(2)}) async-start(), calls=%async_computation.6 | async-start | bytes 1081344 | tf_op jit(solution)/shard_map/reduce_scatter | solution.py:447
  1015.1 265.6 %reduce-scatter.7.cloned.1.call-start = ((), (), s32[]{:S(2)}) async-start(), calls=%async_computation.7 | async-start | bytes 1081344 | tf_op jit(solution)/shard_map/reduce_scatter | solution.py:452
  1149.6 257.8 %all-reduce.20.cloned.1.call-start = ((), (), s32[]{:S(2)}) async-start(), calls=%async_computation.12 | async-start | bytes 294912
  1152.8 254.5 %copy-start.184 = (f32[3,1,384]{2,1,0:T(1,128)S(1)}, f32[3,1,384]{2,1,0:T(1,128)}, u32[]{:S(2)}) copy-start(f32[3,1,384]{2,1,0:T(1,128)} %copy-done.183) | copy-start | bytes 13828
  1152.8 254.5 %copy-start.198 = (f32[384]{0:T(512)S(1)}, f32[384]{0:T(512)}, u32[]{:S(2)}) copy-start(f32[384]{0:T(512)} %get-tuple-element.375) | copy-start | bytes 4612
  1152.8 254.5 %copy-start.236 = (f32[3]{0:T(128)S(1)}, f32[3]{0:T(128)}, u32[]{:S(2)}) copy-start(f32[3]{0:T(128)} %copy-done.235) | copy-start | bytes 40
  1152.9 254.5 %copy-start.247 = (f32[3]{0:T(128)S(1)}, f32[3]{0:T(128)}, u32[]{:S(2)}) copy-start(f32[3]{0:T(128)} %copy-done.246) | copy-start | bytes 40
  1152.9 256.7 %copy-start.216 = (f32[384]{0:T(512)S(1)}, f32[384]{0:T(512)}, u32[]{:S(2)}) copy-start(f32[384]{0:T(512)} %get-tuple-element.351) | copy-start | bytes 4612
  1282.5 581.5 %reduce-scatter.9.cloned.1.call-start = ((), (), s32[]{:S(2)}) async-start(), calls=%async_computation.8 | async-start | bytes 21897216 | tf_op jit(solution)/shard_map/reduce_scatter | solution.py:473
  1645.3 282.3 %all-gather.18.cloned.1.call-start = ((), (), s32[]{:S(2)}) async-start(), calls=%async_computation.9 | async-start | bytes 3649536 | tf_op jit(solution)/shard_map/all_gather | solution.py:366
  1647.0 468.0 %all-reduce.22.cloned.1.call-start = ((), (), s32[]{:S(2)}) async-start(), calls=%async_computation.13 | async-start | bytes 16834560
  1874.7 303.0 %all-gather.20.cloned.1.call-start = ((), (), s32[]{:S(2)}) async-start(), calls=%async_computation.10 | async-start | bytes 3649536 | tf_op jit(solution)/shard_map/all_gather | solution.py:363
  1876.3 608.6 %all-reduce.18.cloned.1.call-start = ((), (), s32[]{:S(2)}) async-start(), calls=%async_computation.11 | async-start | bytes 14155776 | tf_op jit(solution)/shard_map/psum | solution.py:554
  (256 other events, 4011.9 us)
Sparse Core Ops, SparseCore 0:
  11.6 92.9 all-gather.15
  108.1 86.7 all-gather.13
  888.7 123.2 all-reduce.15
  1015.2 131.9 reduce-scatter.4
  1150.0 130.7 reduce-scatter.6
  1286.7 120.6 all-reduce.19
  1645.5 218.4 reduce-scatter.8
  1867.8 59.7 all-gather.17
  1934.6 180.3 all-reduce.21
  2118.3 59.3 all-gather.19
  2321.3 163.5 all-reduce.17
where the time goes:
time: 2520 us; the launch traced here: 2500 us
  waiting for transfers between devices  1140 us (45%)
  blocking collectives  474 us (19%)
  other arithmetic  366 us (15%)
  matrix products  269 us (11%)
  local copies, waits for them, and re-layouts  219 us (9%)
    unnamed x13, waiting for transfers between devices  287 us
    dot_general x88, matrix products, matmul_low(): return jnp.einsum(form, left, right, preferred_element_type=jnp.float32)  238 us
    reduce_scatter x1, waiting for transfers between devices, per_device(): lax.psum_scatter(grad_layers, 'dp', scatter_dimension=1, tiled=True)  203 us
    reduce_scatter x1, waiting for transfers between devices, per_device(): lax.psum_scatter(matmul_low('bc,hc->bh', grad_bottle_own, last_weight), '...  132 us
    reduce_scatter x1, waiting for transfers between devices, per_device(): lax.psum_scatter(matmul_low('bk,kh->bh', grad_pre_two, second_weight), 'd...  128 us
    psum x1, waiting for transfers between devices, per_device(): lax.psum(lax.map(renew_owned, (flat_stats, flat_bases, owners)), 'dp')  125 us
    psum x1, waiting for transfers between devices, per_device(): lax.psum(matmul_low('bp,cp->bc', grad_logits, proto_weight), 'dp')  123 us
    all_gather x1, waiting for transfers between devices, per_device(): lax.all_gather(layers.astype(jnp.bfloat16), 'dp', axis=1, tiled=True)  69.3 us
  transfers between devices with their start and end apart: 11, of which 10 were waited for; matrix products, arithmetic and copies ran while one was open for 5% of the time, Pallas kernels for 0%

commit v1 on v0

--- a/solution.py
+++ b/solution.py
@@ -1,6 +1,10 @@
+import functools
+
 import jax
 import jax.numpy as jnp
 from jax import lax
+from jax.experimental import pallas as pl
+from jax.experimental.pallas import tpu as pltpu
 from jax.sharding import PartitionSpec as P
 
 D = 384
@@ -323,6 +327,1220 @@
     return TEACHER_MOMENTUM * teacher_weight + (1.0 - TEACHER_MOMENTUM) * student_weight
 
 
+MESH = pl.DeviceIdType.MESH
+LANES = 128
+LOW = jnp.bfloat16
+FULL = jnp.float32
+
+
+def params(identity, vmem=None):
+    return pltpu.CompilerParams(
+        collective_id=identity, has_side_effects=True, vmem_limit_bytes=vmem or (48 << 20)
+    )
+
+
+def push(source, target, sent, landed, device):
+    copy = pltpu.make_async_remote_copy(
+        src_ref=source,
+        dst_ref=target,
+        send_sem=sent,
+        recv_sem=landed,
+        device_id=(device,),
+        device_id_type=MESH,
+    )
+    copy.start()
+    return copy
+
+
+def greet(peers):
+    barrier = pltpu.get_barrier_semaphore()
+    for peer in peers:
+        pl.semaphore_signal(barrier, inc=1, device_id=(peer,), device_id_type=MESH)
+    pl.semaphore_wait(barrier, len(peers))
+
+
+def dot_nt(left, right):
+    return lax.dot_general(left, right, (((1,), (1,)), ((), ())), preferred_element_type=FULL)
+
+
+def dot_nn(left, right):
+    return lax.dot_general(left, right, (((1,), (0,)), ((), ())), preferred_element_type=FULL)
+
+
+def dot_tn(left, right):
+    return lax.dot_general(left, right, (((0,), (0,)), ((), ())), preferred_element_type=FULL)
+
+
+def spread_kernel(depth, small_ref, columns_ref, all_ref, part_ref, own_sem, sent, landed, csent, clanded):
+    me = lax.axis_index("dp")
+    total = 8 * depth
+    core = lax.rem(me, 2)
+    x_at = lax.rem(me // 2, 2)
+    y_at = lax.rem(me // 4, 2)
+    z_at = me // 8
+    peers = [lax.rem(me + step, total) for step in range(1, total)]
+    greet(peers)
+
+    def place(y_pos, x_pos, c_pos):
+        return ((y_pos * 2 + x_pos) * 2 + c_pos) * depth
+
+    mine = place(y_at, x_at, core)
+    across_x = place(y_at, 1 - x_at, core)
+    across_y = place(1 - y_at, x_at, core)
+    across_d = place(1 - y_at, 1 - x_at, core)
+    partner = me + 1 - 2 * core
+    to_x = me + 2 - 4 * x_at
+    to_y = me + 4 - 8 * y_at
+    own = pltpu.make_async_copy(small_ref, all_ref.at[mine + z_at], own_sem.at[0])
+    own.start()
+    copies = []
+    z_copies = []
+    for step in range(1, depth):
+        peer = lax.rem(me + 8 * step, total)
+        z_copies.append(
+            push(small_ref, all_ref.at[mine + z_at], sent.at[step], landed.at[step], peer)
+        )
+    hid_rows = columns_ref.shape[0]
+    c_copies = []
+    for step, peer in enumerate(peers):
+        block = columns_ref.at[:, pl.ds(pl.multiple_of((peer // 2) * LANES, LANES), LANES)]
+        c_copies.append(push(block, part_ref.at[me], csent.at[step], clanded.at[step], peer))
+    own_block = columns_ref.at[:, pl.ds(pl.multiple_of((me // 2) * LANES, LANES), LANES)]
+    own_part = pltpu.make_async_copy(own_block, part_ref.at[me], own_sem.at[1])
+    own_part.start()
+    own.wait()
+    for copy in z_copies:
+        copy.wait_recv()
+    base = depth
+
+    def column(start, where, device):
+        view = all_ref.at[pl.ds(start, depth)]
+        return push(view, view, sent.at[where], landed.at[where], device)
+
+    x_copy = column(mine, base, to_x)
+    y_copy = column(mine, base + 1, to_y)
+    die_own = column(mine, base + 2, partner)
+    half = small_ref.shape[0] // 2
+    x_copy.wait_recv()
+    from_x = all_ref.at[pl.ds(across_x, depth), pl.ds(0, half)]
+    d_one = push(from_x, from_x, sent.at[base + 3], landed.at[base + 3], to_y)
+    die_x = column(across_x, base + 5, partner)
+    y_copy.wait_recv()
+    from_y = all_ref.at[pl.ds(across_y, depth), pl.ds(half, half)]
+    d_two = push(from_y, from_y, sent.at[base + 4], landed.at[base + 4], to_x)
+    die_y = column(across_y, base + 6, partner)
+    d_one.wait_recv()
+    d_two.wait_recv()
+    die_d = column(across_d, base + 7, partner)
+    for copy in (die_own, die_x, die_y, die_d):
+        copy.wait_recv()
+    for copy in c_copies:
+        copy.wait_recv()
+    own_part.wait()
+    for copy in z_copies + c_copies + [x_copy, y_copy, die_own, d_one, d_two, die_x, die_y, die_d]:
+        copy.wait_send()
+
+
+def spread(small, columns, devices):
+    depth = devices // 8
+    return pl.pallas_call(
+        functools.partial(spread_kernel, depth),
+        out_shape=(
+            jax.ShapeDtypeStruct((devices,) + small.shape, small.dtype),
+            jax.ShapeDtypeStruct((devices, columns.shape[0], LANES), columns.dtype),
+        ),
+        in_specs=[pl.BlockSpec(memory_space=pltpu.VMEM)] * 2,
+        out_specs=(pl.BlockSpec(memory_space=pltpu.VMEM),) * 2,
+        scratch_shapes=[
+            pltpu.SemaphoreType.DMA((2,)),
+            pltpu.SemaphoreType.DMA((depth + 8,)),
+            pltpu.SemaphoreType.DMA((depth + 8,)),
+            pltpu.SemaphoreType.DMA((devices - 1,)),
+            pltpu.SemaphoreType.DMA((devices - 1,)),
+        ],
+        compiler_params=params(1),
+        name="spread",
+    )(small, columns)
+
+
+def head_kernel(
+    devices,
+    feat_ref,
+    hidden_ref,
+    teacher_hidden_ref,
+    part_ref,
+    last_ref,
+    teacher_last_ref,
+    protos_ref,
+    teacher_protos_ref,
+    centre_ref,
+    mask_ref,
+    mask_row_ref,
+    scalars_ref,
+    grad_hidden_ref,
+    grad_last_ref,
+    grad_protos_ref,
+    grad_feat_ref,
+    centre_out_ref,
+    fb,
+    hid_low,
+    thid_low,
+    prot_low,
+    half_out,
+    half_in,
+    mine_buf,
+    other_buf,
+    act_s,
+    act_t,
+    act2_s,
+    act2_t,
+    pre1,
+    pre2,
+    unit_ref,
+    inv_ref,
+    exp_s,
+    exp_t,
+    stat_out,
+    stat_all,
+    pz_ref,
+    pz_all,
+    dz_own,
+    dz_all,
+    dp_own,
+    dp_in,
+    dp_cb,
+    dp_half,
+    dp_full,
+    df_part,
+    df_all,
+    df_sum,
+    df_other,
+    die_sent,
+    die_landed,
+    wide_sent,
+    wide_landed,
+    core_sent,
+    core_landed,
+):
+    me = lax.axis_index("dp")
+    core = lax.rem(me, 2)
+    chip = me // 2
+    chips = devices // 2
+    partner = me + 1 - 2 * core
+    everyone = [lax.rem(me + step, devices) for step in range(1, devices)]
+    same_core = [lax.rem(me + 2 * step, devices) for step in range(1, chips)]
+    images = mask_ref.shape[0]
+    units = hidden_ref.shape[0]
+    groups = images // 8
+    greet(everyone)
+    sends = []
+
+    def die(step, source, target):
+        copy = push(source, target, die_sent.at[step], die_landed.at[step], partner)
+        sends.append(copy)
+        return copy
+
+    def wide(step, source, target):
+        made = [
+            push(source, target, wide_sent.at[step, at], wide_landed.at[step, at], peer)
+            for at, peer in enumerate(everyone)
+        ]
+        sends.extend(made)
+        return made
+
+    def cores(step, source_of, target):
+        made = [
+            push(source_of(peer), target, core_sent.at[step, at], core_landed.at[step, at], peer)
+            for at, peer in enumerate(same_core)
+        ]
+        sends.extend(made)
+        return made
+
+    fb[me] = feat_ref[...]
+    copies = wide(0, feat_ref, fb.at[me])
+    hid_low[...] = hidden_ref[...].astype(LOW)
+    thid_low[...] = teacher_hidden_ref[...].astype(LOW)
+    prot_low[0] = protos_ref[...].astype(LOW)
+    prot_low[1] = teacher_protos_ref[...].astype(LOW)
+    block_rows = feat_ref.shape[0]
+    row_at = lax.broadcasted_iota(jnp.int32, (images, devices * block_rows), 0)
+    col_at = lax.broadcasted_iota(jnp.int32, (images, devices * block_rows), 1)
+    col_dev = lax.shift_right_logical(col_at, 5)
+    col_in = jnp.bitwise_and(col_at, 31)
+    lead = row_at - 3 * col_dev
+    for copy in copies:
+        copy.wait_recv()
+    rows_all = fb[...].reshape(devices * block_rows, LANES)
+
+    def features_of(model):
+        pieces = []
+        for j in range(3):
+            hit = (col_in - (16 * model + 3 * j) == lead) & (lead >= 0) & (lead < 3)
+            pieces.append(dot_nn(jnp.where(hit, 1.0, 0.0).astype(LOW), rows_all).astype(LOW))
+        return jnp.concatenate(pieces, 1)
+
+    feats = features_of(0)
+    tfeats = features_of(1)
+
+    def gather_pair(step, student, teacher, out_s, out_t):
+        own_model = jnp.where(core == 0, student, teacher)
+        half_out[step] = jnp.where(core == 0, teacher, student)
+        copy = die(2 * step, half_out.at[step], half_in.at[step])
+        copy.wait_recv()
+        got = half_in[step]
+        block = jnp.concatenate(
+            [jnp.where(core == 0, own_model, got), jnp.where(core == 0, got, own_model)], 1
+        ).astype(LOW)
+        mine_buf[step, chip] = block
+        made = cores(step, lambda peer: mine_buf.at[step, chip], mine_buf.at[step, chip])
+        for copy in made:
+            copy.wait_recv()
+        copy = die(2 * step + 1, mine_buf.at[step], other_buf.at[step])
+        copy.wait_recv()
+        for at in range(chips):
+            one, two = mine_buf[step, at], other_buf[step, at]
+            out_s[:, at * LANES : (at + 1) * LANES] = jnp.where(core == 0, one, two)
+            out_t[:, at * LANES : (at + 1) * LANES] = jnp.where(core == 0, two, one)
+
+    pre_one = dot_nt(feats, hid_low[:, :D])
+    pre1[...] = pre_one
+    tpre_one = dot_nt(tfeats, thid_low[:, :D])
+    gather_pair(0, gelu_exact(pre_one).astype(LOW).astype(FULL), gelu_exact(tpre_one).astype(LOW).astype(FULL), act_s, act_t)
+    pre_two = dot_nt(act_s[...], hid_low[:, D:])
+    pre2[...] = pre_two
+    tpre_two = dot_nt(act_t[...], thid_low[:, D:])
+    gather_pair(1, gelu_exact(pre_two).astype(LOW).astype(FULL), gelu_exact(tpre_two).astype(LOW).astype(FULL), act2_s, act2_t)
+
+    unit, inverse_norm = unit_rows(dot_nt(act2_s[...], last_ref[...]))
+    tunit, unused = unit_rows(dot_nt(act2_t[...], teacher_last_ref[...]))
+    unit_ref[...] = unit
+    inv_ref[...] = jnp.broadcast_to(inverse_norm, inv_ref.shape)
+    unit_low = unit.astype(LOW)
+    scaled = dot_nn(unit_low, prot_low[0]) / TAU_STUDENT
+    tlogits = dot_nn(tunit.astype(LOW), prot_low[1])
+    top_s = jnp.max(scaled, -1, keepdims=True)
+    grown_s = jnp.exp(scaled - top_s)
+    exp_s[...] = grown_s
+    sharp = (tlogits - centre_ref[...]) / TAU_TEACHER
+    top_t = jnp.max(sharp, -1, keepdims=True)
+    grown_t = jnp.exp(sharp - top_t)
+    exp_t[...] = grown_t
+    lane = lax.broadcasted_iota(jnp.int32, (images, LANES), 1)
+    stats = jnp.where(lane == 0, top_s, 0.0)
+    stats = jnp.where(lane == 1, jnp.sum(grown_s, -1, keepdims=True), stats)
+    stats = jnp.where(lane == 2, top_t, stats)
+    stats = jnp.where(lane == 3, jnp.sum(grown_t, -1, keepdims=True), stats)
+    stats = jnp.where(lane == 4, jnp.sum(grown_t * scaled, -1, keepdims=True), stats)
+    square = jnp.concatenate([stats, jnp.zeros((LANES - images, LANES), FULL)], 0)
+    stat_out[...] = square.T[:8]
+    stat_all[me] = stat_out[...]
+    copies = wide(1, stat_out, stat_all.at[me])
+    counted = mask_ref[...]
+    count = jnp.sum(counted)
+    centre_out_ref[...] = (
+        CENTRE_MOMENTUM * centre_ref[...]
+        + (1.0 - CENTRE_MOMENTUM) * jnp.sum(counted * tlogits, 0, keepdims=True) / count
+    )
+    for copy in copies:
+        copy.wait_recv()
+    merged = stat_all[...]
+    tops, totals = merged[:, 0], merged[:, 1]
+    ttops, ttotals, crosses = merged[:, 2], merged[:, 3], merged[:, 4]
+    peak_s = jnp.max(tops, 0, keepdims=True)
+    sum_s = jnp.sum(totals * jnp.exp(tops - peak_s), 0, keepdims=True)
+    peak_t = jnp.max(ttops, 0, keepdims=True)
+    shrink = jnp.exp(ttops - peak_t)
+    sum_t = jnp.sum(ttotals * shrink, 0, keepdims=True)
+    cross = jnp.sum(crosses * shrink, 0, keepdims=True)
+    log_total = peak_s + jnp.log(sum_s)
+    mask_row = mask_row_ref[...]
+    losses = jnp.where(mask_row > 0.0, log_total - cross / sum_t, 0.0)
+    loss = jnp.sum(losses)
+    lane8 = lax.broadcasted_iota(jnp.int32, (8, LANES), 1)
+    scalars_ref[...] = jnp.where(lane8 == 0, loss, jnp.where(lane8 == 1, count, 0.0))
+    back = jnp.concatenate(
+        [log_total, peak_t, 1.0 / sum_t, jnp.zeros((LANES - 3, LANES), FULL)], 0
+    ).T
+    share_s = jnp.exp(top_s - back[:images, 0:1])
+    share_t = jnp.exp(top_t - back[:images, 1:2]) * back[:images, 2:3]
+    grad_logits = (
+        (counted / count) * (exp_s[...] * share_s - exp_t[...] * share_t) / TAU_STUDENT
+    ).astype(LOW)
+
+    pz_ref[...] = dot_nt(grad_logits, prot_low[0]).reshape(groups, 8, unit.shape[1])
+    for group in range(groups):
+        owner = 2 * group
+
+        @pl.when(me != owner)
+        def _(group=group, owner=owner):
+            push(pz_ref.at[group], pz_all.at[me], wide_sent.at[2, group], wide_landed.at[2, me], owner)
+
+    grad_protos_ref[...] = dot_tn(unit_low, grad_logits)
+
+    @pl.when((core == 0) & (chip < groups))
+    def _():
+        pz_all[me] = pz_ref[chip]
+        for source in range(devices):
+
+            @pl.when(source != me)
+            def _(source=source):
+                pltpu.make_async_copy(pz_all.at[source], pz_all.at[source], wide_landed.at[2, source]).wait()
+
+        total = jnp.sum(pz_all[...], 0)
+        rows = pl.ds(pl.multiple_of(chip * 8, 8), 8)
+        own_unit = unit_ref[rows, :]
+        own_inv = inv_ref[rows, :][:, 0:1]
+        dz_own[...] = own_inv * (total - own_unit * jnp.sum(own_unit * total, -1, keepdims=True))
+        dz_all[chip] = dz_own[...]
+        for step in range(1, devices):
+            push(dz_own, dz_all.at[chip], wide_sent.at[3, step - 1], wide_landed.at[3, chip], lax.rem(me + step, devices))
+
+    for group in range(groups):
+
+        @pl.when(me != 2 * group)
+        def _(group=group):
+            pltpu.make_async_copy(dz_all.at[group], dz_all.at[group], wide_landed.at[3, group]).wait()
+
+    grad_bottle = dz_all[...].reshape(images, unit.shape[1]).astype(LOW)
+    chip_columns = pl.ds(pl.multiple_of(chip * LANES, LANES), LANES)
+    pair = dot_nn(grad_bottle, last_ref[:, chip_columns])
+    grad_act_two = jnp.where(core == 0, pair[:, :units], pair[:, units:])
+    grad_pre_two = (grad_act_two * gelu_slope(pre2[...])).astype(LOW)
+
+    dp_own[...] = grad_pre_two.astype(FULL)
+    copy = die(4, dp_own, dp_in)
+    width = last_ref.shape[0] // devices
+    pick_row = lax.broadcasted_iota(jnp.int32, (width, last_ref.shape[0]), 0)
+    pick_col = lax.broadcasted_iota(jnp.int32, (width, last_ref.shape[0]), 1)
+    pick = jnp.where(pick_col == pick_row + me * width, 1.0, 0.0).astype(LOW)
+    own_bottle = dot_nt(pick, grad_bottle).astype(LOW)
+    grad_last_ref[...] = dot_nn(own_bottle, act2_s[...])
+    copy.wait_recv()
+    own_dp, got_dp = dp_own[...], dp_in[...]
+    dp_cb[...] = jnp.concatenate(
+        [jnp.where(core == 0, own_dp, got_dp), jnp.where(core == 0, got_dp, own_dp)], 1
+    ).astype(LOW)
+    half = images // 2
+    my_rows = pl.ds(pl.multiple_of(core * half, 16), half)
+    their_rows = pl.ds(pl.multiple_of((1 - core) * half, 16), half)
+    dp_half[0, chip] = dp_cb[my_rows, :]
+    made = cores(2, lambda peer: dp_half.at[0, chip], dp_half.at[0, chip])
+    grad_hidden_ref[:, D:] = dot_tn(grad_pre_two, act_s[...])
+    for copy in made:
+        copy.wait_recv()
+    copy = die(5, dp_half.at[0], dp_half.at[1])
+    for at in range(chips):
+        dp_full[my_rows, at * LANES : (at + 1) * LANES] = dp_half[0, at]
+    copy.wait_recv()
+    for at in range(chips):
+        dp_full[their_rows, at * LANES : (at + 1) * LANES] = dp_half[1, at]
+    pair = dot_nn(dp_full[...], part_ref[...].reshape(devices * units, LANES))
+    grad_act_one = jnp.where(core == 0, pair[:, :units], pair[:, units:])
+    grad_pre_one = (grad_act_one * gelu_slope(pre1[...])).astype(LOW)
+
+    out_row = lax.broadcasted_iota(jnp.int32, (8 * chips, images), 0)
+    in_row = lax.broadcasted_iota(jnp.int32, (8 * chips, images), 1)
+    out_chip = lax.shift_right_logical(out_row, 3)
+    out_in = jnp.bitwise_and(out_row, 7)
+    hit = (in_row - 6 * out_chip == out_in) & (out_in < 6)
+    moved = dot_nn(jnp.where(hit, 1.0, 0.0).astype(LOW), grad_pre_one).astype(LOW)
+    df_part[...] = dot_nn(moved, hid_low[:, :D]).reshape(chips, 8, D)
+    df_all[chip] = df_part[chip]
+    made = cores(3, lambda peer: df_part.at[peer // 2], df_all.at[chip])
+    grad_hidden_ref[:, :D] = dot_tn(grad_pre_one, feats)
+    for copy in made:
+        copy.wait_recv()
+    df_sum[...] = jnp.sum(df_all[...], 0)
+    copy = die(6, df_sum, df_other)
+    copy.wait_recv()
+    whole = df_sum[...] + df_other[...]
+    grad_feat_ref[...] = whole
+    squares = jnp.sum(grad_hidden_ref[...] * grad_hidden_ref[...])
+    squares = squares + jnp.sum(grad_last_ref[...] * grad_last_ref[...])
+    squares = squares + jnp.sum(grad_protos_ref[...] * grad_protos_ref[...])
+    scalars_ref[...] = jnp.where(lane8 == 2, squares, scalars_ref[...])
+    for copy in sends:
+        copy.wait_send()
+    for group in range(groups):
+
+        @pl.when(me != 2 * group)
+        def _(group=group):
+            pltpu.make_async_copy(pz_ref.at[group], pz_ref.at[group], wide_sent.at[2, group]).wait()
+
+    @pl.when((core == 0) & (chip < groups))
+    def _():
+        for step in range(1, devices):
+            pltpu.make_async_copy(dz_own, dz_own, wide_sent.at[3, step - 1]).wait()
+
+
+def head(feat, hidden, teacher_hidden, part, last, teacher_last, protos, teacher_protos, centre, mask, mask_row, devices):
+    images = mask.shape[0]
+    units, wide = hidden.shape
+    bottle, width = protos.shape
+    hid = last.shape[1]
+    chips = devices // 2
+    groups = images // 8
+    vmem = pl.BlockSpec(memory_space=pltpu.VMEM)
+    shape = jax.ShapeDtypeStruct
+    dma = pltpu.SemaphoreType.DMA
+    return pl.pallas_call(
+        functools.partial(head_kernel, devices),
+        out_shape=(
+            shape((8, LANES), FULL),
+            shape((units, wide), FULL),
+            shape((bottle // devices, hid), FULL),
+            shape((bottle, width), FULL),
+            shape((8, D), FULL),
+            shape((1, width), FULL),
+        ),
+        in_specs=[vmem] * 11,
+        out_specs=(vmem,) * 6,
+        scratch_shapes=[
+            pltpu.VMEM((devices,) + feat.shape, LOW),
+            pltpu.VMEM((units, wide), LOW),
+            pltpu.VMEM((units, wide), LOW),
+            pltpu.VMEM((2, bottle, width), LOW),
+            pltpu.VMEM((2, images, units), FULL),
+            pltpu.VMEM((2, images, units), FULL),
+            pltpu.VMEM((2, chips, images, LANES), LOW),
+            pltpu.VMEM((2, chips, images, LANES), LOW),
+            pltpu.VMEM((images, hid), LOW),
+            pltpu.VMEM((images, hid), LOW),
+            pltpu.VMEM((images, hid), LOW),
+            pltpu.VMEM((images, hid), LOW),
+            pltpu.VMEM((images, units), FULL),
+            pltpu.VMEM((images, units), FULL),
+            pltpu.VMEM((images, bottle), FULL),
+            pltpu.VMEM((images, LANES), FULL),
+            pltpu.VMEM((images, width), FULL),
+            pltpu.VMEM((images, width), FULL),
+            pltpu.VMEM((8, LANES), FULL),
+            pltpu.VMEM((devices, 8, LANES), FULL),
+            pltpu.VMEM((groups, 8, bottle), FULL),
+            pltpu.VMEM((devices, 8, bottle), FULL),
+            pltpu.VMEM((8, bottle), FULL),
+            pltpu.VMEM((groups, 8, bottle), FULL),
+            pltpu.VMEM((images, units), FULL),
+            pltpu.VMEM((images, units), FULL),
+            pltpu.VMEM((images, LANES), LOW),
+            pltpu.VMEM((2, chips, images // 2, LANES), LOW),
+            pltpu.VMEM((images, hid), LOW),
+            pltpu.VMEM((chips, 8, D), FULL),
+            pltpu.VMEM((chips, 8, D), FULL),
+            pltpu.VMEM((8, D), FULL),
+            pltpu.VMEM((8, D), FULL),
+            dma((7,)),
+            dma((7,)),
+            dma((4, devices)),
+            dma((4, devices)),
+            dma((4, chips - 1)),
+            dma((4, chips - 1)),
+        ],
+        compiler_params=params(2),
+        name="head",
+    )(feat, hidden, teacher_hidden, part, last, teacher_last, protos, teacher_protos, centre, mask, mask_row)
+
+
+def gram_device(matrix):
+    return 2 * matrix
+
+
+def collect_kernel(
+    depth,
+    rows_layer,
+    bounds,
+    squares_ref,
+    packet_ref,
+    stats_ref,
+    bases_ref,
+    own_ref,
+    norm_ref,
+    next_stats_ref,
+    basis_ref,
+    die_buf,
+    d_buf,
+    x_buf,
+    y_buf,
+    z_buf,
+    stat_buf,
+    square_out,
+    square_all,
+    segs,
+    gram_buf,
+    die_sent,
+    die_landed,
+    near_sent,
+    near_landed,
+    z_sent,
+    z_landed,
+    stat_sent,
+    stat_landed,
+    gram_sent,
+    gram_landed,
+    square_sent,
+    square_landed,
+):
+    me = lax.axis_index("dp")
+    total = 8 * depth
+    core = lax.rem(me, 2)
+    x_at = lax.rem(me // 2, 2)
+    y_at = lax.rem(me // 4, 2)
+    z_at = me // 8
+    chip = me // 2
+    partner = me + 1 - 2 * core
+    to_x = me + 2 - 4 * x_at
+    to_y = me + 4 - 8 * y_at
+    everyone = [lax.rem(me + step, total) for step in range(1, total)]
+    matrices = stats_ref.shape[0]
+    own_rows = stats_ref.shape[1]
+    segment_rows = segs.shape[2]
+    is_gram = (core == 0) & (chip < matrices)
+    greet(everyone)
+    sends = []
+
+    def place(y_pos, x_pos, c_pos):
+        return ((y_pos * 2 + x_pos) * 2 + c_pos) * depth
+
+    relative = [(y_at, x_at), (y_at, 1 - x_at), (1 - y_at, x_at), (1 - y_at, 1 - x_at)]
+    starts = [place(y_pos, x_pos, core) for y_pos, x_pos in relative]
+    partner_starts = [place(y_pos, x_pos, 1 - core) for y_pos, x_pos in relative]
+    layers = (packet_ref.shape[1] // rows_layer)
+    chunks = [(layer * rows_layer, rows_layer) for layer in reversed(range(layers))]
+    chunks.append((layers * rows_layer, packet_ref.shape[1] - layers * rows_layer))
+    count = len(chunks)
+
+    def first_half(k):
+        return ((chunks[k][1] // 2 + 15) // 16) * 16
+
+    die_copies = {}
+    for k in range(count):
+        lower, size = chunks[k]
+        for rel in (3, 1, 2, 0):
+            copy = push(
+                packet_ref.at[pl.ds(partner_starts[rel], depth), pl.ds(lower, size)],
+                die_buf.at[pl.ds(rel * depth, depth), pl.ds(lower, size)],
+                die_sent.at[k, rel],
+                die_landed.at[k, rel],
+                partner,
+            )
+            die_copies[k, rel] = copy
+            sends.append(copy)
+
+    for matrix in range(matrices):
+        owner = gram_device(matrix)
+
+        @pl.when(me != owner)
+        def _(matrix=matrix, owner=owner):
+            push(stats_ref.at[matrix], stat_buf.at[0, me], stat_sent.at[0, matrix], stat_landed.at[0, me], owner)
+            push(bases_ref.at[matrix], stat_buf.at[1, me], stat_sent.at[1, matrix], stat_landed.at[1, me], owner)
+
+    near = {}
+
+    def pair_sum(rel, z_pos, lower, size):
+        return packet_ref[starts[rel] + z_pos, pl.ds(lower, size), :].astype(FULL) + die_buf[
+            rel * depth + z_pos, pl.ds(lower, size), :
+        ].astype(FULL)
+
+    def stage_one(k):
+        lower, size = chunks[k]
+        half = first_half(k)
+        die_copies[k, 3].wait_recv()
+        for z_pos in range(depth):
+            die_buf[3 * depth + z_pos, pl.ds(lower, size), :] = pair_sum(3, z_pos, lower, size).astype(LOW)
+        for which, (start, length, peer) in enumerate(
+            [(lower, half, to_x), (lower + half, size - half, to_y)]
+        ):
+            copy = push(
+                die_buf.at[pl.ds(3 * depth, depth), pl.ds(start, length)],
+                d_buf.at[:, pl.ds(start, length)],
+                near_sent.at[k, which],
+                near_landed.at[k, which],
+                peer,
+            )
+            near[k, which] = copy
+            sends.append(copy)
+
+    def stage_two(k):
+        lower, size = chunks[k]
+        half = first_half(k)
+        for rel, which, peer, target in ((1, 2, to_x, x_buf), (2, 3, to_y, y_buf)):
+            die_copies[k, rel].wait_recv()
+            near[k, 1 if rel == 1 else 0].wait_recv()
+            first, second = (lower, half), (lower + half, size - half)
+            helped, plain = (second, first) if rel == 1 else (first, second)
+            for z_pos in range(depth):
+                die_buf[rel * depth + z_pos, pl.ds(plain[0], plain[1]), :] = pair_sum(
+                    rel, z_pos, plain[0], plain[1]
+                ).astype(LOW)
+                die_buf[rel * depth + z_pos, pl.ds(helped[0], helped[1]), :] = (
+                    pair_sum(rel, z_pos, helped[0], helped[1])
+                    + d_buf[z_pos, pl.ds(helped[0], helped[1]), :].astype(FULL)
+                ).astype(LOW)
+            copy = push(
+                die_buf.at[pl.ds(rel * depth, depth), pl.ds(lower, size)],
+                target.at[:, pl.ds(lower, size)],
+                near_sent.at[k, which],
+                near_landed.at[k, which],
+                peer,
+            )
+            near[k, which] = copy
+            sends.append(copy)
+
+    z_copies = {}
+
+    def stage_three(k):
+        lower, size = chunks[k]
+        die_copies[k, 0].wait_recv()
+        near[k, 2].wait_recv()
+        near[k, 3].wait_recv()
+        for z_pos in range(depth):
+            die_buf[z_pos, pl.ds(lower, size), :] = (
+                pair_sum(0, z_pos, lower, size)
+                + x_buf[z_pos, pl.ds(lower, size), :].astype(FULL)
+                + y_buf[z_pos, pl.ds(lower, size), :].astype(FULL)
+            ).astype(LOW)
+        for step in range(1, depth):
+            z_to = lax.rem(z_at + step, depth)
+            copy = push(
+                die_buf.at[z_to, pl.ds(lower, size)],
+                z_buf.at[z_at, pl.ds(lower, size)],
+                z_sent.at[k, step],
+                z_landed.at[k, step],
+                lax.rem(me + 8 * step, total),
+            )
+            z_copies[k, step] = copy
+            sends.append(copy)
+
+    def stage_four(k):
+        lower, size = chunks[k]
+        for step in range(1, depth):
+            z_copies[k, step].wait_recv()
+        value = die_buf[z_at, pl.ds(lower, size), :].astype(FULL)
+        for step in range(1, depth):
+            value = value + z_buf[lax.rem(z_at + step, depth), pl.ds(lower, size), :].astype(FULL)
+        own_ref[pl.ds(lower, size), :] = value
+        if k == count - 1:
+            return
+        layer = lower // rows_layer
+        for segment, (low_row, high_row) in enumerate(bounds):
+            piece = value[low_row:high_row].astype(LOW)
+            if high_row - low_row < segment_rows:
+                blank = jnp.zeros((segment_rows - (high_row - low_row), value.shape[1]), LOW)
+                piece = jnp.concatenate([piece, blank], 0)
+            matrix = 4 * layer + segment
+            segs[layer, segment] = piece
+            owner = gram_device(matrix)
+
+            @pl.when(me != owner)
+            def _(matrix=matrix, owner=owner, layer=layer, segment=segment):
+                push(segs.at[layer, segment], gram_buf.at[me], gram_sent.at[matrix], gram_landed.at[me], owner)
+
+    stages = [stage_one, stage_two, stage_three, stage_four]
+    for step in range(count + len(stages) - 1):
+        for at, stage in enumerate(stages):
+            if 0 <= step - at < count:
+                stage(step - at)
+
+    own = own_ref[...]
+    lane8 = lax.broadcasted_iota(jnp.int32, (8, LANES), 1)
+    squares = jnp.sum(own * own) + jnp.sum(jnp.where(lane8 == 2, squares_ref[...], 0.0)) / 8.0
+    square_out[...] = jnp.full((8, LANES), squares)
+    square_all[me] = square_out[...]
+    copies = [
+        push(square_out, square_all.at[me], square_sent.at[at], square_landed.at[at], peer)
+        for at, peer in enumerate(everyone)
+    ]
+    sends.extend(copies)
+    for copy in copies:
+        copy.wait_recv()
+    squares = jnp.sum(square_all[...], 0)
+    norm = jnp.sqrt(squares)
+    norm_ref[...] = norm
+    clip = jnp.minimum(1.0, CLIP_MAX / (norm + 1e-06))[:1, :1]
+
+    @pl.when(is_gram)
+    def _():
+        for matrix in range(matrices):
+
+            @pl.when(matrix == chip)
+            def _(matrix=matrix):
+                gram_buf[me] = segs[matrix // 4, matrix % 4]
+                stat_buf[0, me] = stats_ref[matrix]
+                stat_buf[1, me] = bases_ref[matrix]
+
+        for source in range(total):
+
+            @pl.when(source != me)
+            def _(source=source):
+                for at in range(2):
+                    pltpu.make_async_copy(
+                        stat_buf.at[at, source], stat_buf.at[at, source], stat_landed.at[at, source]
+                    ).wait()
+                pltpu.make_async_copy(gram_buf.at[source], gram_buf.at[source], gram_landed.at[source]).wait()
+
+        rows = gram_buf[...].reshape(total * segment_rows, gram_buf.shape[2])
+        gram = dot_tn(rows, rows)
+        scale = (1.0 - BETA_STAT) * (clip * clip)
+        for source in range(total):
+            next_stats_ref[source] = (
+                BETA_STAT * stat_buf[0, source]
+                + scale * gram[source * own_rows : (source + 1) * own_rows]
+            )
+        basis_ref[...] = stat_buf[1]
+
+    @pl.when(jnp.logical_not(is_gram))
+    def _():
+        next_stats_ref[...] = jnp.zeros(next_stats_ref.shape, FULL)
+        basis_ref[...] = jnp.zeros(basis_ref.shape, FULL)
+
+    for copy in sends:
+        copy.wait_send()
+    for matrix in range(matrices):
+
+        @pl.when(me != gram_device(matrix))
+        def _(matrix=matrix):
+            for at, source in ((0, stats_ref), (1, bases_ref)):
+                pltpu.make_async_copy(source.at[matrix], source.at[matrix], stat_sent.at[at, matrix]).wait()
+            own_segment = segs.at[matrix // 4, matrix % 4]
+            pltpu.make_async_copy(own_segment, own_segment, gram_sent.at[matrix]).wait()
+
+
+def collect(squares, packets, stats, bases, rows_layer, bounds):
+    devices, rows, width = packets.shape
+    depth = devices // 8
+    matrices, own_rows = stats.shape[:2]
+    layers = rows // rows_layer
+    segment_rows = -(-max(high - low for low, high in bounds) // 16) * 16
+    vmem = pl.BlockSpec(memory_space=pltpu.VMEM)
+    shape = jax.ShapeDtypeStruct
+    dma = pltpu.SemaphoreType.DMA
+    count = layers + 1
+    return pl.pallas_call(
+        functools.partial(collect_kernel, depth, rows_layer, bounds),
+        out_shape=(
+            shape((rows, width), FULL),
+            shape((8, LANES), FULL),
+            shape((devices, own_rows, width), FULL),
+            shape((devices, own_rows, width), FULL),
+        ),
+        in_specs=[vmem] * 4,
+        out_specs=(vmem,) * 4,
+        scratch_shapes=[
+            pltpu.VMEM((4 * depth, rows, width), LOW),
+            pltpu.VMEM((depth, rows, width), LOW),
+            pltpu.VMEM((depth, rows, width), LOW),
+            pltpu.VMEM((depth, rows, width), LOW),
+            pltpu.VMEM((depth, rows, width), LOW),
+            pltpu.VMEM((2, devices, own_rows, width), FULL),
+            pltpu.VMEM((8, LANES), FULL),
+            pltpu.VMEM((devices, 8, LANES), FULL),
+            pltpu.VMEM((layers, 4, segment_rows, width), LOW),
+            pltpu.VMEM((devices, segment_rows, width), LOW),
+            dma((count, 4)),
+            dma((count, 4)),
+            dma((count, 4)),
+            dma((count, 4)),
+            dma((count, depth)),
+            dma((count, depth)),
+            dma((2, matrices)),
+            dma((2, devices)),
+            dma((matrices,)),
+            dma((devices,)),
+            dma((devices - 1,)),
+            dma((devices - 1,)),
+        ],
+        compiler_params=params(3, 56 << 20),
+        name="collect",
+    )(squares, packets, stats, bases)
+
+
+def dot_high(left, right, contract):
+    return lax.dot_general(
+        left,
+        right,
+        (contract, ((), ())),
+        precision=lax.Precision.HIGHEST,
+        preferred_element_type=FULL,
+    )
+
+
+def inverse_factor(block):
+    size = block.shape[0]
+    tiles = size // 8
+    sub = lax.broadcasted_iota(jnp.int32, (8, size), 0)
+    lane = lax.broadcasted_iota(jnp.int32, (8, size), 1)
+    rest = [block[8 * t : 8 * t + 8] for t in range(tiles)]
+    made = [jnp.where(lane == sub + 8 * t, 1.0, 0.0) for t in range(tiles)]
+    for k in range(size):
+        tile, row = k // 8, k % 8
+        pivot = rest[tile][row : row + 1]
+        scale = lax.rsqrt(pivot[:, k : k + 1])
+        factor_row = pivot * scale
+        made_row = made[tile][row : row + 1] * scale
+        for t in range(tile, tiles):
+            column = rest[t][:, k : k + 1] * scale
+            if t == tile:
+                column = jnp.where(sub[:, :1] > row, column, 0.0)
+            rest[t] = rest[t] - column * factor_row
+            made[t] = made[t] - column * made_row
+            if t == tile:
+                made[t] = jnp.where(sub == row, made_row, made[t])
+    return jnp.concatenate(made, 0)
+
+
+def renew_kernel(stats_ref, basis_ref, out_ref, stat, base, gram, work, done):
+    parts, rows = stats_ref.shape[:2]
+    size = parts * rows
+    blocks = size // LANES
+    for part in range(parts):
+        stat[part * rows : (part + 1) * rows] = stats_ref[part]
+        base[part * rows : (part + 1) * rows] = basis_ref[part]
+    at_row = lax.broadcasted_iota(jnp.int32, (size, size), 0)
+    at_col = lax.broadcasted_iota(jnp.int32, (size, size), 1)
+    trace = jnp.sum(jnp.where(at_row == at_col, stat[...], 0.0), axis=(0, 1), keepdims=True)
+    scaled = dot_high(stat[...], base[...], ((1,), (0,))) * (size / trace)
+    product = dot_high(scaled, scaled, ((0,), (0,)))
+    for b in range(blocks):
+        work[b] = scaled[:, b * LANES : (b + 1) * LANES]
+        for c in range(blocks):
+            gram[b, c] = product[b * LANES : (b + 1) * LANES, c * LANES : (c + 1) * LANES]
+
+    def step(b, carried):
+        inverse = inverse_factor(gram[b, b])
+        made = dot_high(work[b], inverse, ((1,), (1,)))
+        done[b] = made
+
+        def trail(c, inner):
+            panel = dot_high(inverse, gram[b, c], ((1,), (0,)))
+            work[c] = work[c] - dot_high(made, panel, ((1,), (0,)))
+
+            def against(e, innermost):
+                other = dot_high(inverse, gram[b, e], ((1,), (0,)))
+                gram[c, e] = gram[c, e] - dot_high(panel, other, ((0,), (0,)))
+                return innermost
+
+            lax.fori_loop(c, blocks, against, 0)
+            return inner
+
+        lax.fori_loop(b + 1, blocks, trail, 0)
+        return carried
+
+    lax.fori_loop(0, blocks, step, 0)
+    whole = jnp.concatenate([done[b] for b in range(blocks)], 1)
+    for part in range(parts):
+        out_ref[part] = whole[part * rows : (part + 1) * rows]
+
+
+def renew_own(stats, basis):
+    devices, rows, width = stats.shape
+    size = devices * rows
+    blocks = size // LANES
+    vmem = pl.BlockSpec(memory_space=pltpu.VMEM)
+    return pl.pallas_call(
+        renew_kernel,
+        out_shape=jax.ShapeDtypeStruct(stats.shape, FULL),
+        in_specs=[vmem] * 2,
+        out_specs=vmem,
+        scratch_shapes=[
+            pltpu.VMEM((size, width), FULL),
+            pltpu.VMEM((size, width), FULL),
+            pltpu.VMEM((blocks, blocks, LANES, LANES), FULL),
+            pltpu.VMEM((blocks, size, LANES), FULL),
+            pltpu.VMEM((blocks, size, LANES), FULL),
+        ],
+        compiler_params=pltpu.CompilerParams(vmem_limit_bytes=32 << 20),
+        name="renew",
+    )(stats, basis)
+
+
+def deal_kernel(devices, stats_ref, bases_ref, own_stats_ref, own_bases_ref, sent, landed):
+    me = lax.axis_index("dp")
+    core = lax.rem(me, 2)
+    chip = me // 2
+    matrices = own_stats_ref.shape[0]
+    is_gram = (core == 0) & (chip < matrices)
+    greet([lax.rem(me + step, devices) for step in range(1, devices)])
+
+    @pl.when(is_gram)
+    def _():
+        for step in range(1, devices):
+            peer = lax.rem(me + step, devices)
+            push(bases_ref.at[peer], own_bases_ref.at[chip], sent.at[1, step], landed.at[1, chip], peer)
+        for step in range(1, devices):
+            peer = lax.rem(me + step, devices)
+            push(stats_ref.at[peer], own_stats_ref.at[chip], sent.at[0, step], landed.at[0, chip], peer)
+        own_stats_ref[chip] = stats_ref[me]
+        own_bases_ref[chip] = bases_ref[me]
+
+    for matrix in range(matrices):
+
+        @pl.when(me != gram_device(matrix))
+        def _(matrix=matrix):
+            for at, target in ((0, own_stats_ref), (1, own_bases_ref)):
+                pltpu.make_async_copy(target.at[matrix], target.at[matrix], landed.at[at, matrix]).wait()
+
+    @pl.when(is_gram)
+    def _():
+        for step in range(1, devices):
+            for at, source in ((0, stats_ref), (1, bases_ref)):
+                pltpu.make_async_copy(source.at[0], source.at[0], sent.at[at, step]).wait()
+
+
+def deal(stats, bases, matrices):
+    devices, rows, width = stats.shape
+    vmem = pl.BlockSpec(memory_space=pltpu.VMEM)
+    dma = pltpu.SemaphoreType.DMA
+    return pl.pallas_call(
+        functools.partial(deal_kernel, devices),
+        out_shape=(jax.ShapeDtypeStruct((matrices, rows, width), FULL),) * 2,
+        in_specs=[vmem] * 2,
+        out_specs=(vmem,) * 2,
+        scratch_shapes=[dma((2, devices)), dma((2, matrices))],
+        compiler_params=params(4),
+        name="deal",
+    )(stats, bases)
+
+
+def head_slow(
+    features,
+    teacher_features,
+    valid_mask,
+    head_hidden,
+    head_last,
+    protos,
+    teacher_hidden,
+    teacher_last,
+    teacher_protos,
+    centre,
+    device_index,
+):
+    all_features, all_teacher = (
+        lax.all_gather(features, "dp", axis=0, tiled=True),
+        lax.all_gather(teacher_features, "dp", axis=0, tiled=True),
+    )
+    first_weight = head_hidden[:, :D].astype(jnp.bfloat16)
+    second_weight = head_hidden[:, D:].astype(jnp.bfloat16)
+    last_weight = head_last.astype(jnp.bfloat16)
+    proto_weight = protos.astype(jnp.bfloat16)
+    teacher_first = teacher_hidden[:, :D].astype(jnp.bfloat16)
+    teacher_second = teacher_hidden[:, D:].astype(jnp.bfloat16)
+    pre_one = matmul_low("bd,hd->bh", all_features, first_weight)
+    teacher_pre_one = matmul_low("bd,hd->bh", all_teacher, teacher_first)
+    act_one = (
+        lax.all_gather(gelu_exact(pre_one).astype(jnp.bfloat16), "dp", axis=1, tiled=True),
+        lax.all_gather(gelu_exact(teacher_pre_one).astype(jnp.bfloat16), "dp", axis=1, tiled=True),
+    )
+    pre_two = matmul_low("bh,kh->bk", act_one[0], second_weight)
+    teacher_pre_two = matmul_low("bh,kh->bk", act_one[1], teacher_second)
+    act_two = (
+        lax.all_gather(gelu_exact(pre_two).astype(jnp.bfloat16), "dp", axis=1, tiled=True),
+        lax.all_gather(gelu_exact(teacher_pre_two).astype(jnp.bfloat16), "dp", axis=1, tiled=True),
+    )
+    bottles = (
+        lax.all_gather(matmul_low("bh,hc->bc", act_two[0], last_weight), "dp", axis=1, tiled=True),
+        lax.all_gather(
+            matmul_low("bh,hc->bc", act_two[1], teacher_last.astype(jnp.bfloat16)),
+            "dp",
+            axis=1,
+            tiled=True,
+        ),
+    )
+    unit, inverse_norm = unit_rows(bottles[0])
+    teacher_unit, unused_norm = unit_rows(bottles[1])
+    unit_low = unit.astype(jnp.bfloat16)
+    logits = matmul_low("bc,cp->bp", unit_low, proto_weight)
+    teacher_logits = matmul_low(
+        "bc,cp->bp", teacher_unit.astype(jnp.bfloat16), teacher_protos.astype(jnp.bfloat16)
+    )
+    scaled = logits / TAU_STUDENT
+    student_top = jnp.max(scaled, -1)
+    student_total = jnp.sum(jnp.exp(scaled - student_top[:, None]), -1)
+    sharpened = (teacher_logits - centre) / TAU_TEACHER
+    teacher_top = jnp.max(sharpened, -1)
+    teacher_exp = jnp.exp(sharpened - teacher_top[:, None])
+    merged = joined(
+        (
+            student_top,
+            student_total,
+            teacher_top,
+            jnp.sum(teacher_exp, -1),
+            jnp.sum(teacher_exp * scaled, -1),
+        ),
+        "dp",
+        combine_parts,
+    )
+    log_total = merged[0] + jnp.log(merged[1])
+    counted = valid_mask.astype(jnp.float32)
+    loss_count = jnp.sum(counted)
+    loss_sum = jnp.sum(counted * (log_total - merged[4] / merged[3]))
+    student_prob = jnp.exp(scaled - log_total[:, None])
+    teacher_prob = jnp.exp(sharpened - merged[2][:, None]) / merged[3][:, None]
+    grad_logits = (
+        (counted / loss_count)[:, None] * (student_prob - teacher_prob) / TAU_STUDENT
+    ).astype(jnp.bfloat16)
+    grad_protos = matmul_low("bc,bp->cp", unit_low, grad_logits)
+    grad_unit = lax.psum(matmul_low("bp,cp->bc", grad_logits, proto_weight), "dp")
+    grad_bottle = inverse_norm * (grad_unit - unit * jnp.sum(unit * grad_unit, -1, keepdims=True))
+    last_width = head_last.shape[1]
+    grad_bottle_own = lax.dynamic_slice_in_dim(
+        grad_bottle, device_index * last_width, last_width, 1
+    ).astype(jnp.bfloat16)
+    grad_last = matmul_low("bh,bc->hc", act_two[0], grad_bottle_own)
+    grad_act_two = lax.psum_scatter(
+        matmul_low("bc,hc->bh", grad_bottle_own, last_weight), "dp", scatter_dimension=1, tiled=True
+    )
+    grad_pre_two = (grad_act_two * gelu_slope(pre_two)).astype(jnp.bfloat16)
+    grad_second = matmul_low("bk,bh->kh", grad_pre_two, act_one[0])
+    grad_act_one = lax.psum_scatter(
+        matmul_low("bk,kh->bh", grad_pre_two, second_weight), "dp", scatter_dimension=1, tiled=True
+    )
+    grad_pre_one = (grad_act_one * gelu_slope(pre_one)).astype(jnp.bfloat16)
+    grad_first = matmul_low("bh,bd->hd", grad_pre_one, all_features)
+    grad_features = lax.psum_scatter(
+        matmul_low("bh,hd->bd", grad_pre_one, first_weight), "dp", scatter_dimension=0, tiled=True
+    )
+    grad_hidden = jnp.concatenate([grad_first, grad_second], 1)
+    next_centre = (
+        CENTRE_MOMENTUM * centre
+        + (1.0 - CENTRE_MOMENTUM) * jnp.sum(counted[:, None] * teacher_logits, 0) / loss_count
+    )
+    return (loss_sum, loss_count, grad_hidden, grad_last, grad_protos, grad_features, next_centre)
+
+
+def pack_small(embedding, teacher_embedding, head_last, teacher_last):
+    def table(value):
+        flat = value.T.astype(LOW).reshape(-1)
+        return jnp.pad(flat, (0, -flat.size % (16 * LANES))).reshape(-1, LANES)
+
+    def last(value):
+        return value.T.astype(LOW).reshape(-1, LANES)
+
+    return jnp.concatenate(
+        [table(embedding), table(teacher_embedding), last(head_last), last(teacher_last)], 0
+    )
+
+
+def unpack_small(everything, embedding, head_last, devices):
+    depth = devices // 8
+    rows, columns = embedding.shape
+    ordered = everything.reshape(2, 2, 2, depth, -1, LANES).transpose(3, 0, 1, 2, 4, 5)
+    ordered = ordered.reshape(devices, -1, LANES)
+    size = rows * columns
+    table_rows = (size + (-size % (16 * LANES))) // LANES
+    last_rows = head_last.size // LANES
+
+    def table(at):
+        flat = ordered[:, at : at + table_rows].reshape(devices, -1)[:, :size]
+        return flat.reshape(devices * columns, rows).T
+
+    def last(at):
+        return ordered[:, at : at + last_rows].reshape(devices * head_last.shape[1], -1)
+
+    return (
+        table(0),
+        table(table_rows),
+        last(2 * table_rows),
+        last(2 * table_rows + last_rows),
+    )
+
+
+def own_feature_rows(features, teacher_features):
+    def rows(value):
+        count = value.shape[0]
+        turned = value.reshape(count, D // LANES, LANES).transpose(1, 0, 2).reshape(-1, LANES)
+        return jnp.pad(turned, ((0, 16 - turned.shape[0]), (0, 0)))
+
+    return jnp.concatenate([rows(features), rows(teacher_features)], 0)
+
+
+def head_fast(
+    features,
+    teacher_features,
+    valid_mask,
+    head_hidden,
+    protos,
+    teacher_hidden,
+    teacher_protos,
+    centre,
+    part,
+    last_full,
+    teacher_last_full,
+    devices,
+    device_index,
+):
+    counted = valid_mask.astype(FULL)
+    mask_row = jnp.pad(counted, (0, LANES - counted.size)).reshape(1, LANES)
+    scalars, grad_hidden, grad_last, grad_protos, grad_feat, next_centre = head(
+        own_feature_rows(features, teacher_features),
+        head_hidden,
+        teacher_hidden,
+        part,
+        last_full,
+        teacher_last_full,
+        protos,
+        teacher_protos,
+        centre[None],
+        counted[:, None],
+        mask_row,
+        devices,
+    )
+    count = features.shape[0]
+    grad_features = lax.dynamic_slice_in_dim(grad_feat, (device_index % 2) * count, count, 0)
+    return (
+        scalars[0, 0],
+        scalars[0, 1],
+        scalars,
+        grad_hidden,
+        grad_last.T,
+        grad_protos,
+        grad_features,
+        next_centre[0],
+    )
+
+
+def packets_of(grad_table, grad_layers, devices):
+    depth = devices // 8
+    layers = grad_layers.shape[0]
+    parts = grad_layers.reshape(layers, devices, -1, D).transpose(1, 0, 2, 3).reshape(devices, -1, D)
+    flat = grad_table.T.reshape(devices, -1)
+    flat = jnp.pad(flat, ((0, 0), (0, -flat.shape[1] % (16 * D)))).reshape(devices, -1, D)
+    joint = jnp.concatenate([parts, flat], 1).astype(LOW)
+    ordered = joint.reshape((depth, 2, 2, 2) + joint.shape[1:]).transpose(1, 2, 3, 0, 4, 5)
+    return ordered.reshape(joint.shape)
+
+
+def tail_fast(
+    squares, grad_table, grad_layers, layer_stats, layer_bases, owners, embedding, layers, devices
+):
+    own_rows = layer_stats.shape[2]
+    matrices = owners.shape[0]
+    rows_layer = layers.shape[1]
+    own, norm, full_stats, full_bases = collect(
+        squares,
+        packets_of(grad_table, grad_layers, devices),
+        layer_stats.reshape(matrices, own_rows, D),
+        layer_bases.reshape(matrices, own_rows, D),
+        rows_layer,
+        layer_bounds(devices),
+    )
+    count = layers.shape[0] * rows_layer
+    grad_layers_own = own[:count].reshape(layers.shape)
+    rows, columns = embedding.shape
+    grad_embed = own[count:].reshape(-1)[: rows * columns].reshape(columns, rows).T
+    renewed = renew_own(full_stats, full_bases)
+    stats_own, bases_own = deal(full_stats, renewed, matrices)
+    bases_own = jnp.where(
+        owners[:, None, None] >= 0, bases_own, layer_bases.reshape(matrices, own_rows, D)
+    )
+    return (
+        norm[0, 0],
+        grad_embed,
+        grad_layers_own,
+        stats_own.reshape(layer_stats.shape),
+        bases_own.reshape(layer_bases.shape),
+    )
+
+
 def per_device(
     patches,
     valid_mask,
@@ -353,153 +1571,138 @@
 ):
     devices = lax.axis_size("dp")
     device_index = lax.axis_index("dp")
-    fetched = (
-        lax.all_gather(embedding.astype(jnp.bfloat16), "dp", axis=1, tiled=True),
-        lax.all_gather(layers.astype(jnp.bfloat16), "dp", axis=1, tiled=True),
-        lax.all_gather(teacher_embedding.astype(jnp.bfloat16), "dp", axis=1, tiled=True),
-        lax.all_gather(teacher_layers.astype(jnp.bfloat16), "dp", axis=1, tiled=True),
-    )
-    stats_full, bases_full = (
-        lax.all_gather(layer_stats.astype(jnp.bfloat16), "dp", axis=2, tiled=True).astype(
+    fast = 2 * head_hidden.shape[0] == LANES
+    if fast:
+        small, part = spread(
+            pack_small(embedding, teacher_embedding, head_last, teacher_last),
+            head_hidden[:, D:].astype(LOW),
+            devices,
+        )
+        embed_table, teacher_table, last_full, teacher_last_full = unpack_small(
+            small, embedding, head_last, devices
+        )
+    else:
+        embed_table, teacher_table = (
+            lax.all_gather(embedding.astype(LOW), "dp", axis=1, tiled=True),
+            lax.all_gather(teacher_embedding.astype(LOW), "dp", axis=1, tiled=True),
+        )
+    layer_full, teacher_full = (
+        lax.all_gather(layers.astype(LOW), "dp", axis=1, tiled=True),
+        lax.all_gather(teacher_layers.astype(LOW), "dp", axis=1, tiled=True),
+    )
+    bases_full = lax.all_gather(layer_bases.astype(LOW), "dp", axis=2, tiled=True).astype(
+        layer_bases.dtype
+    )
+    if not fast:
+        stats_full = lax.all_gather(layer_stats.astype(LOW), "dp", axis=2, tiled=True).astype(
             layer_stats.dtype
-        ),
-        lax.all_gather(layer_bases.astype(jnp.bfloat16), "dp", axis=2, tiled=True).astype(
-            layer_bases.dtype
-        ),
-    )
-    embed_table, layer_full = (fetched[0], fetched[1])
+        )
     features, layer_inputs, final_state = backbone(patches, embed_table, layer_full, devices)
     teacher_features, unused_inputs, unused_final = backbone(
-        patches, fetched[2], fetched[3], devices
-    )
-    all_features, all_teacher = (
-        lax.all_gather(features, "dp", axis=0, tiled=True),
-        lax.all_gather(teacher_features, "dp", axis=0, tiled=True),
-    )
-    first_weight = head_hidden[:, :D].astype(jnp.bfloat16)
-    second_weight = head_hidden[:, D:].astype(jnp.bfloat16)
-    last_weight = head_last.astype(jnp.bfloat16)
-    proto_weight = protos.astype(jnp.bfloat16)
-    teacher_first = teacher_hidden[:, :D].astype(jnp.bfloat16)
-    teacher_second = teacher_hidden[:, D:].astype(jnp.bfloat16)
-    pre_one = matmul_low("bd,hd->bh", all_features, first_weight)
-    teacher_pre_one = matmul_low("bd,hd->bh", all_teacher, teacher_first)
-    act_one = (
-        lax.all_gather(gelu_exact(pre_one).astype(jnp.bfloat16), "dp", axis=1, tiled=True),
-        lax.all_gather(gelu_exact(teacher_pre_one).astype(jnp.bfloat16), "dp", axis=1, tiled=True),
-    )
-    pre_two = matmul_low("bh,kh->bk", act_one[0], second_weight)
-    teacher_pre_two = matmul_low("bh,kh->bk", act_one[1], teacher_second)
-    act_two = (
-        lax.all_gather(gelu_exact(pre_two).astype(jnp.bfloat16), "dp", axis=1, tiled=True),
-        lax.all_gather(gelu_exact(teacher_pre_two).astype(jnp.bfloat16), "dp", axis=1, tiled=True),
-    )
-    bottles = (
-        lax.all_gather(matmul_low("bh,hc->bc", act_two[0], last_weight), "dp", axis=1, tiled=True),
-        lax.all_gather(
-            matmul_low("bh,hc->bc", act_two[1], teacher_last.astype(jnp.bfloat16)),
-            "dp",
-            axis=1,
-            tiled=True,
-        ),
-    )
-    unit, inverse_norm = unit_rows(bottles[0])
-    teacher_unit, unused_norm = unit_rows(bottles[1])
-    unit_low = unit.astype(jnp.bfloat16)
-    logits = matmul_low("bc,cp->bp", unit_low, proto_weight)
-    teacher_logits = matmul_low(
-        "bc,cp->bp", teacher_unit.astype(jnp.bfloat16), teacher_protos.astype(jnp.bfloat16)
-    )
-    scaled = logits / TAU_STUDENT
-    student_top = jnp.max(scaled, -1)
-    student_total = jnp.sum(jnp.exp(scaled - student_top[:, None]), -1)
-    sharpened = (teacher_logits - centre) / TAU_TEACHER
-    teacher_top = jnp.max(sharpened, -1)
-    teacher_exp = jnp.exp(sharpened - teacher_top[:, None])
-    merged = joined(
+        patches, teacher_table, teacher_full, devices
+    )
+    if fast:
         (
-            student_top,
-            student_total,
-            teacher_top,
-            jnp.sum(teacher_exp, -1),
-            jnp.sum(teacher_exp * scaled, -1),
-        ),
-        "dp",
-        combine_parts,
-    )
-    log_total = merged[0] + jnp.log(merged[1])
-    counted = valid_mask.astype(jnp.float32)
-    loss_count = jnp.sum(counted)
-    loss_sum = jnp.sum(counted * (log_total - merged[4] / merged[3]))
-    student_prob = jnp.exp(scaled - log_total[:, None])
-    teacher_prob = jnp.exp(sharpened - merged[2][:, None]) / merged[3][:, None]
-    grad_logits = (
-        (counted / loss_count)[:, None] * (student_prob - teacher_prob) / TAU_STUDENT
-    ).astype(jnp.bfloat16)
-    grad_protos = matmul_low("bc,bp->cp", unit_low, grad_logits)
-    grad_unit = lax.psum(matmul_low("bp,cp->bc", grad_logits, proto_weight), "dp")
-    grad_bottle = inverse_norm * (grad_unit - unit * jnp.sum(unit * grad_unit, -1, keepdims=True))
-    last_width = head_last.shape[1]
-    grad_bottle_own = lax.dynamic_slice_in_dim(
-        grad_bottle, device_index * last_width, last_width, 1
-    ).astype(jnp.bfloat16)
-    grad_last = matmul_low("bh,bc->hc", act_two[0], grad_bottle_own)
-    grad_act_two = lax.psum_scatter(
-        matmul_low("bc,hc->bh", grad_bottle_own, last_weight), "dp", scatter_dimension=1, tiled=True
-    )
-    grad_pre_two = (grad_act_two * gelu_slope(pre_two)).astype(jnp.bfloat16)
-    grad_second = matmul_low("bk,bh->kh", grad_pre_two, act_one[0])
-    grad_act_one = lax.psum_scatter(
-        matmul_low("bk,kh->bh", grad_pre_two, second_weight), "dp", scatter_dimension=1, tiled=True
-    )
-    grad_pre_one = (grad_act_one * gelu_slope(pre_one)).astype(jnp.bfloat16)
-    grad_first = matmul_low("bh,bd->hd", grad_pre_one, all_features)
-    grad_features = lax.psum_scatter(
-        matmul_low("bh,hd->bd", grad_pre_one, first_weight), "dp", scatter_dimension=0, tiled=True
-    )
-    layer_again = lax.all_gather(layers.astype(jnp.bfloat16), "dp", axis=1, tiled=True)
+            loss_sum,
+            loss_count,
+            squares,
+            grad_hidden,
+            grad_last,
+            grad_protos,
+            grad_features,
+            next_centre,
+        ) = head_fast(
+            features,
+            teacher_features,
+            valid_mask,
+            head_hidden,
+            protos,
+            teacher_hidden,
+            teacher_protos,
+            centre,
+            part,
+            last_full,
+            teacher_last_full,
+            devices,
+            device_index,
+        )
+    else:
+        (
+            loss_sum,
+            loss_count,
+            grad_hidden,
+            grad_last,
+            grad_protos,
+            grad_features,
+            next_centre,
+        ) = head_slow(
+            features,
+            teacher_features,
+            valid_mask,
+            head_hidden,
+            head_last,
+            protos,
+            teacher_hidden,
+            teacher_last,
+            teacher_protos,
+            centre,
+            device_index,
+        )
     grad_table, grad_layers = backbone_back(
         patches,
         embed_table,
-        layer_again,
+        layer_full,
         layer_inputs,
         final_state,
         grad_features,
         devices,
         unchanged,
     )
-    summed = (
-        lax.psum_scatter(grad_table, "dp", scatter_dimension=1, tiled=True),
-        lax.psum_scatter(grad_layers, "dp", scatter_dimension=1, tiled=True),
-    )
-    grad_embed = summed[0]
-    grad_layers_own = summed[1]
-    grad_hidden = jnp.concatenate([grad_first, grad_second], 1)
     bounds = layer_bounds(devices)
-    grams = jnp.stack(
-        [
-            matmul_high(
-                "lcd,lce->lde",
-                grad_layers_own[:, lower_row:upper_row],
-                grad_layers_own[:, lower_row:upper_row],
-            )
-            for lower_row, upper_row in bounds
-        ],
-        1,
-    )
-    squares = (
-        jnp.sum(grad_embed * grad_embed)
-        + jnp.sum(grad_layers_own * grad_layers_own)
-        + jnp.sum(grad_hidden * grad_hidden)
-        + jnp.sum(grad_last * grad_last)
-        + jnp.sum(grad_protos * grad_protos)
-    )
-    totals = lax.psum((squares, grams), "dp")
-    grad_norm = jnp.sqrt(totals[0])
+    if fast:
+        grad_norm, grad_embed, grad_layers_own, stats_own, bases_own = tail_fast(
+            squares,
+            grad_table,
+            grad_layers,
+            layer_stats,
+            layer_bases,
+            owners,
+            embedding,
+            layers,
+            devices,
+        )
+    else:
+        summed = (
+            lax.psum_scatter(grad_table, "dp", scatter_dimension=1, tiled=True),
+            lax.psum_scatter(grad_layers, "dp", scatter_dimension=1, tiled=True),
+        )
+        grad_embed = summed[0]
+        grad_layers_own = summed[1]
+        grams = jnp.stack(
+            [
+                matmul_high(
+                    "lcd,lce->lde",
+                    grad_layers_own[:, lower_row:upper_row],
+                    grad_layers_own[:, lower_row:upper_row],
+                )
+                for lower_row, upper_row in bounds
+            ],
+            1,
+        )
+        squares = (
+            jnp.sum(grad_embed * grad_embed)
+            + jnp.sum(grad_layers_own * grad_layers_own)
+            + jnp.sum(grad_hidden * grad_hidden)
+            + jnp.sum(grad_last * grad_last)
+            + jnp.sum(grad_protos * grad_protos)
+        )
+        totals = lax.psum((squares, grams), "dp")
+        grad_norm = jnp.sqrt(totals[0])
+        clip_factor = jnp.minimum(1.0, CLIP_MAX / (grad_norm + 1e-06))
+        next_stats = (
+            BETA_STAT * stats_full + (1.0 - BETA_STAT) * (clip_factor * clip_factor) * totals[1]
+        )
     clip_factor = jnp.minimum(1.0, CLIP_MAX / (grad_norm + 1e-06))
-    next_stats = (
-        BETA_STAT * stats_full + (1.0 - BETA_STAT) * (clip_factor * clip_factor) * totals[1]
-    )
     rows = jnp.arange(embedding.shape[0])[:, None]
     is_matrix = rows < PIX + SEQ
     embed_out = adam_step(
@@ -545,23 +1748,20 @@
         seconds.append(second_new)
         weights_new.append(weight_block - RATE_MATRIX * (update + WEIGHT_DECAY * weight_block))
     next_layers = jnp.concatenate(weights_new, 1)
-    flat_stats = next_stats.reshape(-1, D, D)
-    flat_bases = bases_full.reshape(-1, D, D)
-
-    def renew_owned(operands):
-        return lax.cond(operands[2] == device_index, renew, nothing, operands[0], operands[1])
-
-    renewed = lax.psum(lax.map(renew_owned, (flat_stats, flat_bases, owners)), "dp")
-    next_bases = jnp.where(owners[:, None, None] >= 0, renewed, flat_bases).reshape(
-        bases_full.shape
-    )
-    own_rows = layer_stats.shape[2]
-    stats_own = lax.dynamic_slice_in_dim(next_stats, device_index * own_rows, own_rows, 2)
-    bases_own = lax.dynamic_slice_in_dim(next_bases, device_index * own_rows, own_rows, 2)
-    next_centre = (
-        CENTRE_MOMENTUM * centre
-        + (1.0 - CENTRE_MOMENTUM) * jnp.sum(counted[:, None] * teacher_logits, 0) / loss_count
-    )
+    if not fast:
+        flat_stats = next_stats.reshape(-1, D, D)
+        flat_bases = bases_full.reshape(-1, D, D)
+
+        def renew_owned(operands):
+            return lax.cond(operands[2] == device_index, renew, nothing, operands[0], operands[1])
+
+        renewed = lax.psum(lax.map(renew_owned, (flat_stats, flat_bases, owners)), "dp")
+        next_bases = jnp.where(owners[:, None, None] >= 0, renewed, flat_bases).reshape(
+            bases_full.shape
+        )
+        own_rows = layer_stats.shape[2]
+        stats_own = lax.dynamic_slice_in_dim(next_stats, device_index * own_rows, own_rows, 2)
+        bases_own = lax.dynamic_slice_in_dim(next_bases, device_index * own_rows, own_rows, 2)
     return (
         loss_sum,
         loss_count,

time: 2520 us -> 1070 us (0.42)
  waiting for transfers between devices: 1140 us -> 138 us
  blocking collectives: 474 us -> 0 us
  Pallas kernels: 0 us -> 282 us
  other arithmetic: 366 us -> 189 us
  matrix products: 269 us -> 231 us
    reduce_scatter x3 -> x0, waiting for transfers between devices: 463 us -> none  [the longest x1 203 us: per_device(): lax.psum_scatter(grad_layers, 'dp', scatter_dimension=1, tiled=True)]
    all_gather x10 -> x0, blocking collectives: 395 us -> none  [the longest x1 45.1 us: per_device(): lax.all_gather(teacher_embedding.astype(jnp.bfloat16), 'dp', axis=1, tile...]
    unnamed x13 -> x3, waiting for transfers between devices: 287 us -> 0.05 us
    pallas_call x0 -> x5, Pallas kernels: none -> 282 us  [the longest x1 90.9 us: collect(): pl.pallas_call(functools.partial(collect_kernel, depth, rows_layer, bound...]
    psum x2 -> x0, waiting for transfers between devices: 249 us -> none  [the longest x1 125 us: per_device(): lax.psum(lax.map(renew_owned, (flat_stats, flat_bases, owners)), 'dp')]
    another operation x16 -> x0, other arithmetic: 90.4 us -> none  [the longest x10 56.1 us: renew(): lower_factor = jnp.linalg.cholesky(gram)]
    add x66 -> x1, other arithmetic: 84.3 us -> 1.02 us  [backbone(): current = jnp.concatenate([leading, projected + position[1:]], 1)]
    unnamed x1 -> x0, blocking collectives: 39.7 us -> none
  transfers between devices with their start and end apart: 11 -> 3, of which waited for: 10 -> 2; matrix products, arithmetic and copies ran while one was open for 5% -> 6% of each run, Pallas kernels for 0% -> 4%
where the time goes in v1:
time: 1070 us; the launch traced here: 1050 us
  Pallas kernels  282 us (26%)
  matrix products  231 us (22%)
  local copies, waits for them, and re-layouts  195 us (18%)
  other arithmetic  189 us (18%)
  waiting for transfers between devices  138 us (13%)
  between operations  18.6 us (2%)
    dot_general x72, matrix products, matmul_low(): return jnp.einsum(form, left, right, preferred_element_type=jnp.float32)  217 us
    pallas_call x1, Pallas kernels, collect(): pl.pallas_call(functools.partial(collect_kernel, depth, rows_layer, bound...  90.9 us
    pallas_call x1, Pallas kernels, head(): pl.pallas_call(functools.partial(head_kernel, devices), out_shape=(shape(...  81.6 us
    all_gather x1, waiting for transfers between devices, per_device(): lax.all_gather(layers.astype(LOW), 'dp', axis=1, tiled=True)  73.7 us
    all_gather x1, waiting for transfers between devices, per_device(): lax.all_gather(teacher_layers.astype(LOW), 'dp', axis=1, tiled=True)  64.1 us
    reduce_sum x7, other arithmetic, norm_back(): jnp.sum(grad_out * normed, leading)  46.7 us
    pallas_call x1, Pallas kernels, spread(): pl.pallas_call(functools.partial(spread_kernel, depth), out_shape=(jax.Sh...  41.8 us
    unnamed x569, local copies, waits for them, and re-layouts  41 us
  transfers between devices with their start and end apart: 3, of which 2 were waited for; matrix products, arithmetic and copies ran while one was open for 6% of the time, Pallas kernels for 4%

profile of v1, /device:TPU:31, one launch (start us, length us, event | category | flops | bytes accessed | tf_op | source)
XLA Modules:
  0.0 1053.4 jit_solution(12349725049391428904)
XLA Ops:
  14.1 41.8 %spread.1 = (bf16[32,448,128]{2,1,0:T(8,128)(2,1)S(1)}, bf16[32,64,128]{2,1,0:T(8,128)(2,1)S(1)}) custom-call(bf16[448,128]{1,0:T(8,128)(2,1)S(1)} %pad_maximum_fusion.6.small_ref, bf16[64,2048]{1,0:T(8,128)(2,1)S(1)} %slice.943.columns_ref), custom_call_target="tpu_custom_call" | custom-call | tf_op jit(solution)/shard_map/spread/pallas_call | solution.py:446
  91.4 13.3 %fusion.307 = (bf16[3,1,384,384]{3,1,0,2:T(2,128)(2,1)}, bf16[3,1,384,384]{3,1,0,2:T(2,128)(2,1)}, bf16[3,1,384,384]{3,1,0,2:T(2,128)(2,1)}, bf16[3,1,384,384]{3,1,0,2:T(2,128)(2,1)}) fusion(bf16[3,4,384,384]{3,1,0,2:T(4,128)(2,1)} %all-gather.8.cloned.1.call-done), kind=kLoop, calls=%fused_computation.606 | loop fusion | bytes 7077888 | tf_op jit(solution)/shard_map/slice | solution.py:1732
  104.7 64.1 %all-gather.6.cloned.1.call-done = bf16[3,4608,384]{2,1,0:T(8,128)(2,1)} async-done(((bf16[3,144,384]{2,1,0:T(8,128)(2,1)}), bf16[3,4608,384]{2,1,0:T(8,128)(2,1)}) %all-gather.6.cloned.1.call-update) | async-done | bytes 10616848 | tf_op jit(solution)/shard_map/all_gather | solution.py:1591
  184.2 73.7 %all-gather.4.cloned.1.call-done = bf16[3,4608,384]{2,1,0:T(8,128)(2,1)} async-done(((bf16[3,144,384]{2,1,0:T(8,128)(2,1)}), bf16[3,4608,384]{2,1,0:T(8,128)(2,1)}) %all-gather.4.cloned.1.call-update) | async-done | bytes 10616848 | tf_op jit(solution)/shard_map/all_gather | solution.py:1590
  303.6 6.8 fusion.318
  340.7 6.8 fusion.321
  376.0 5.8 fusion.119
  509.2 81.6 %head.1 = (f32[8,128]{1,0:T(8,128)S(1)}, f32[64,2432]{1,0:T(8,128)S(1)}, f32[8,2048]{1,0:T(8,128)S(1)}, f32[256,2048]{1,0:T(8,128)}, f32[8,384]{1,0:T(8,128)S(1)}, /*index=5*/f32[1,2048]{1,0:T(1,128)S(1)}) custom-call(bf16[32,128]{1,0:T(8,128)(2,1)S(1)} %fusion.246.feat_ref, f32[64,2432]{1,0:T(8,128)S(1)} %copy-done.1, f32[64,2432]{1,0:T(8,128)S(1)} %copy-done.4, ...), custom_call_target="tpu_custom_call" | custom-call | tf_op jit(solution)/shard_map/head/pallas_call | solution.py:786
  599.9 7.8 multiply_reduce_fusion.10
  619.9 7.9 multiply_reduce_fusion.2
  640.7 7.8 multiply_reduce_fusion.11
  658.3 7.8 multiply_reduce_fusion.14
  677.7 7.9 multiply_reduce_fusion.1
  698.5 7.8 multiply_reduce_fusion.15
  716.1 7.8 multiply_reduce_fusion.18
  729.8 5.7 fusion.72
  735.5 8.6 multiply_reduce_fusion
  756.7 7.2 multiply_reduce_fusion.19
  825.5 5.9 dot_general.355
  846.2 5.8 copy.760
  852.0 90.9 %collect.1 = (f32[464,384]{1,0:T(8,128)}, f32[8,128]{1,0:T(8,128)}, f32[32,12,384]{2,1,0:T(8,128)}, f32[32,12,384]{2,1,0:T(8,128)}) custom-call(f32[8,128]{1,0:T(8,128)} %copy-done.13, bf16[32,464,384]{2,1,0:T(8,128)(2,1)} %bitcast.537, f32[12,12,384]{2,1,0:T(8,128)} %bitcast.622, f32[12,12,384]{2,1,0:T(8,128)} %bitcast.613), custom_call_target="tpu_custom_call" | custom-call | tf_op jit(solution)/shard_map/collect/pallas_call | solution.py:1118
  963.7 39.7 %renew.1.bases_ref = f32[32,12,384]{2,1,0:T(8,128)S(1)} custom-call(f32[32,12,384]{2,1,0:T(8,128)S(1)} %copy-done.3, f32[32,12,384]{2,1,0:T(8,128)S(1)} %copy-done.6), custom_call_target="tpu_custom_call" | custom-call | tf_op jit(solution)/shard_map/renew/pallas_call | solution.py:1239
  1003.5 28.3 %deal.1 = (f32[12,12,384]{2,1,0:T(8,128)S(1)}, f32[12,12,384]{2,1,0:T(8,128)S(1)}) custom-call(f32[32,12,384]{2,1,0:T(8,128)S(1)} %copy-done.3, f32[32,12,384]{2,1,0:T(8,128)S(1)} %renew.1.bases_ref), custom_call_target="tpu_custom_call" | custom-call | tf_op jit(solution)/shard_map/deal/pallas_call | solution.py:1293
  1037.3 6.7 multiply_add_fusion
  (912 shorter events, 487.6 us)
Async XLA Ops:
  7.2 69.3 %copy-start = (bf16[3,256,588]{1,2,0:T(8,128)(2,1)S(1)}, bf16[3,256,588]{1,2,0:T(8,128)(2,1)}, u32[]{:S(2)}) copy-start(bf16[3,256,588]{1,2,0:T(8,128)(2,1)} %param.26) | copy-start | bytes 2709508
  7.2 84.2 %all-gather.8.cloned.1.call-start = ((), (), s32[]{:S(2)}) async-start(), calls=%async_computation.2 | async-start | bytes 3649536 | tf_op jit(solution)/shard_map/all_gather | solution.py:1593
  9.1 159.7 %all-gather.6.cloned.1.call-start = ((), (), s32[]{:S(2)}) async-start(), calls=%async_computation.1 | async-start | bytes 10948608 | tf_op jit(solution)/shard_map/all_gather | solution.py:1591
  11.0 246.9 %all-gather.4.cloned.1.call-start = ((), (), s32[]{:S(2)}) async-start(), calls=%async_computation | async-start | bytes 10948608 | tf_op jit(solution)/shard_map/all_gather | solution.py:1590
  82.1 329.1 %copy-start.174 = (f32[3,1,384]{2,0,1:T(4,128)}, f32[3,1,384]{2,0,1:T(4,128)S(1)}, u32[]{:S(2)}) copy-start(f32[3,1,384]{2,0,1:T(4,128)S(1)} %broadcast_in_dim.25) | copy-start | bytes 13828
  85.3 342.2 %copy-start.198 = (f32[384]{0:T(512)}, f32[384]{0:T(512)S(1)}, u32[]{:S(2)}) copy-start(f32[384]{0:T(512)S(1)} %get-tuple-element.212) | copy-start | bytes 4612
  509.2 81.7 %copy-start.190 = (f32[3,1,384]{2,0,1:T(4,128)S(1)}, f32[3,1,384]{2,0,1:T(4,128)}, u32[]{:S(2)}) copy-start(f32[3,1,384]{2,0,1:T(4,128)} %copy-done.189) | copy-start | bytes 13828
  509.2 81.7 %copy-start.217 = (f32[384]{0:T(512)S(1)}, f32[384]{0:T(512)}, u32[]{:S(2)}) copy-start(f32[384]{0:T(512)} %get-tuple-element.242) | copy-start | bytes 4612
  509.2 81.7 %copy-start.240 = (f32[3]{0:T(128)S(1)}, f32[3]{0:T(128)}, u32[]{:S(2)}) copy-start(f32[3]{0:T(128)} %copy-done.239) | copy-start | bytes 40
  509.2 81.7 %copy-start.242 = (f32[3]{0:T(128)S(1)}, f32[3]{0:T(128)}, u32[]{:S(2)}) copy-start(f32[3]{0:T(128)} %copy-done.241) | copy-start | bytes 40
  509.2 82.6 %copy-start.230 = (f32[384]{0:T(512)S(1)}, f32[384]{0:T(512)}, u32[]{:S(2)}) copy-start(f32[384]{0:T(512)} %get-tuple-element.202) | copy-start | bytes 4612
  509.2 83.7 %copy-start.147 = (bf16[32,48,384]{2,1,0:T(8,128)(2,1)S(1)}, bf16[32,48,384]{2,1,0:T(8,128)(2,1)}, u32[]{:S(2)}) copy-start(bf16[32,48,384]{2,1,0:T(8,128)(2,1)} %get-tuple-element.309) | copy-start | bytes 3538948
  590.9 203.2 %copy-start.13 = (f32[8,128]{1,0:T(8,128)}, f32[8,128]{1,0:T(8,128)S(1)}, u32[]{:S(2)}) copy-start(f32[8,128]{1,0:T(8,128)S(1)} %get-tuple-element.42.squares_ref) | copy-start | bytes 12292
  961.0 71.6 %copy-start.261 = (pred[12]{0:T(512)(128)(4,1)S(1)}, pred[12]{0:T(512)(128)(4,1)}, u32[]{:S(2)}) copy-start(pred[12]{0:T(512)(128)(4,1)} %broadcast_compare_fusion) | copy-start | bytes 40
  963.7 68.9 %copy-start.103 = (f32[3,4,12,384]{3,2,1,0:T(8,128)S(1)}, f32[3,4,12,384]{3,2,1,0:T(8,128)}, u32[]{:S(2)}) copy-start(f32[3,4,12,384]{3,2,1,0:T(8,128)} %copy.762) | copy-start | bytes 663556
  963.7 71.7 %copy-start.177 = (f32[2048,8]{0,1:T(8,128)S(1)}, f32[2048,8]{0,1:T(8,128)}, u32[]{:S(2)}) copy-start(f32[2048,8]{0,1:T(8,128)} %param.49) | copy-start | bytes 196612
  963.7 71.6 %copy-start.179 = (f32[2048,8]{0,1:T(8,128)S(1)}, f32[2048,8]{0,1:T(8,128)}, u32[]{:S(2)}) copy-start(f32[2048,8]{0,1:T(8,128)} %param.40) | copy-start | bytes 196612
  963.7 71.6 %copy-start.195 = (f32[2048,8]{0,1:T(8,128)S(1)}, f32[2048,8]{0,1:T(8,128)}, u32[]{:S(2)}) copy-start(f32[2048,8]{0,1:T(8,128)} %param.42) | copy-start | bytes 196612
  963.7 73.5 %copy-start.122 = (f32[256,2048]{1,0:T(8,128)S(1)}, f32[256,2048]{1,0:T(8,128)}, u32[]{:S(2)}) copy-start(f32[256,2048]{1,0:T(8,128)} %param.44) | copy-start | bytes 6291460
  1003.5 30.0 %copy-start.2 = (f32[64,2432]{1,0:T(8,128)S(1)}, f32[64,2432]{1,0:T(8,128)}, u32[]{:S(2)}) copy-start(f32[64,2432]{1,0:T(8,128)} %hidden_ref.1) | copy-start | bytes 1867780
  1003.5 30.0 %copy-start.5 = (f32[64,2432]{1,0:T(8,128)S(1)}, f32[64,2432]{1,0:T(8,128)}, u32[]{:S(2)}) copy-start(f32[64,2432]{1,0:T(8,128)} %teacher_hidden_ref.1) | copy-start | bytes 1867780
  1003.5 30.0 %copy-start.8 = (f32[64,2432]{1,0:T(8,128)S(1)}, f32[64,2432]{1,0:T(8,128)}, u32[]{:S(2)}) copy-start(f32[64,2432]{1,0:T(8,128)} %copy-done.7) | copy-start | bytes 1867780
  1003.5 30.0 %copy-start.172 = (f32[64,2432]{1,0:T(8,128)S(1)}, f32[64,2432]{1,0:T(8,128)}, u32[]{:S(2)}) copy-start(f32[64,2432]{1,0:T(8,128)} %param.39) | copy-start | bytes 1867780
  1003.5 30.0 %copy-start.173 = (f32[64,2432]{1,0:T(8,128)S(1)}, f32[64,2432]{1,0:T(8,128)}, u32[]{:S(2)}) copy-start(f32[64,2432]{1,0:T(8,128)} %param.38) | copy-start | bytes 1867780
  (259 other events, 788.1 us)
Sparse Core Ops, SparseCore 0:
  11.5 68.1 all-gather.7
  83.2 85.5 all-gather.5
  172.3 85.5 all-gather.3

commit v2 on v1

--- a/solution.py
+++ b/solution.py
@@ -1498,26 +1498,472 @@
     )
 
 
-def packets_of(grad_table, grad_layers, devices):
+TOKENS = 272
+HALF_ROW = 256
+SAVED = ("inputs", "normed", "joint", "mixed", "attended", "middle", "normed_two", "activated", "slope", "outer")
+
+
+def saved_widths():
+    return {
+        "inputs": (D, FULL),
+        "normed": (D, LOW),
+        "joint": (3 * D, LOW),
+        "mixed": (D, LOW),
+        "attended": (D, LOW),
+        "middle": (D, FULL),
+        "normed_two": (D, LOW),
+        "activated": (MLP, LOW),
+        "slope": (MLP, LOW),
+        "outer": (D, LOW),
+    }
+
+
+def unpack_blocks(weights, joint_out, output_out, cuts):
+    devices = weights.shape[0]
+    joint_rows, output_rows = cuts[0], cuts[1] - cuts[0]
+    group = 4
+    for at in range(0, devices, group):
+        blocks = [weights[at + t, 0 : cuts[1]].astype(FULL) for t in range(group)]
+        joint = jnp.concatenate([block[:joint_rows] for block in blocks], 0)
+        output = jnp.concatenate([block[joint_rows:] for block in blocks], 0)
+        joint_out[at * joint_rows : (at + group) * joint_rows] = joint.astype(LOW)
+        output_out[at * output_rows : (at + group) * output_rows] = output.astype(LOW)
+
+
+def weight_rows(weights, cuts, which, part, parts):
+    per = weights.shape[0] // parts
+    block = weights[part * per : (part + 1) * per, cuts[which] : cuts[which + 1]]
+    return block.reshape(-1, block.shape[-1])
+
+
+def chance(keys_half, queries, live):
+    scores = jnp.where(live, dot_nt(keys_half, queries), -jnp.inf)
+    grown = jnp.exp(scores - jnp.max(scores, 0, keepdims=True))
+    return grown * (1.0 / jnp.sum(grown, 0, keepdims=True))
+
+
+def forward_kernel(
+    cuts,
+    save,
+    patches_ref,
+    table_ref,
+    start_ref,
+    weights_ref,
+    vectors_ref,
+    tail_ref,
+    feat_ref,
+    last_ref,
+    *rest,
+):
+    layer, image = pl.program_id(0), pl.program_id(1)
+    if save:
+        outs = dict(zip(SAVED, rest[: len(SAVED)]))
+        rest = rest[len(SAVED) :]
+    current, joint_weight, output_weight = rest
+
+    def keep(name, value):
+        if save:
+            outs[name][0, 0] = value
+
+    weights = weights_ref.at[0]
+
+    @pl.when(image == 0)
+    def _():
+        unpack_blocks(weights, joint_weight, output_weight, cuts)
+
+    @pl.when(layer == 0)
+    def _():
+        current[image, :HALF_ROW] = start_ref[:HALF_ROW] + dot_nn(patches_ref[0], table_ref[...])
+        current[image, HALF_ROW:] = start_ref[HALF_ROW:]
+
+    inputs = current[image]
+    vectors = vectors_ref[0]
+    keep("inputs", inputs)
+    normed = layer_norm(inputs, vectors[0:1], vectors[1:2]).astype(LOW)
+    keep("normed", normed)
+    lane = lax.broadcasted_iota(jnp.int32, (TOKENS, LANES), 1)
+    live = lax.broadcasted_iota(jnp.int32, (TOKENS, TOKENS), 0) < SEQ
+    mixed = []
+    for pair in range(D // LANES):
+        lower = pair * LANES
+        parts = [
+            dot_nt(normed, joint_weight[third * D + lower : third * D + lower + LANES])
+            for third in range(3)
+        ]
+        rounded = [part.astype(LOW) for part in parts]
+        if save:
+            for third in range(3):
+                outs["joint"][0, 0, :, third * D + lower : third * D + lower + LANES] = rounded[third]
+        queries = (rounded[0].astype(FULL) * HEAD_DIM ** (-0.5)).astype(LOW)
+        values = parts[2].T.astype(LOW)
+        turned = []
+        for half in range(2):
+            keys_half = jnp.where((lane >= HEAD_DIM) == bool(half), rounded[1].astype(FULL), 0.0).astype(LOW)
+            share = chance(keys_half, queries, live).astype(LOW)
+            turned.append(dot_nn(values[half * HEAD_DIM : (half + 1) * HEAD_DIM], share))
+        mixed.append(jnp.concatenate(turned, 0).T.astype(LOW))
+    mixed = jnp.concatenate(mixed, 1)
+    keep("mixed", mixed)
+    attended = dot_nt(mixed, output_weight[...])
+    keep("attended", attended.astype(LOW))
+    middle = inputs + vectors[4:5] * attended
+    keep("middle", middle)
+    normed_two = layer_norm(middle, vectors[2:3], vectors[3:4]).astype(LOW)
+    keep("normed_two", normed_two)
+    outer = jnp.zeros((TOKENS, D), FULL)
+    parts = MLP // D
+    for part in range(parts):
+        inner = dot_nt(normed_two, weight_rows(weights, cuts, 1, part, parts))
+        spread_half = 0.5 * (1.0 + lax.erf(inner * ROOT_HALF))
+        activated = (inner * spread_half).astype(LOW)
+        if save:
+            outs["activated"][0, 0, :, part * D : (part + 1) * D] = activated
+            slope = spread_half + inner * jnp.exp(-0.5 * inner * inner) * DENSITY_SCALE
+            outs["slope"][0, 0, :, part * D : (part + 1) * D] = slope.astype(LOW)
+        outer = outer + dot_nn(activated, weight_rows(weights, cuts, 2, part, parts))
+    keep("outer", outer.astype(LOW))
+    result = middle + vectors[5:6] * outer
+    current[image] = result
+    final = result[HALF_ROW : HALF_ROW + 8]
+    last_ref[0] = final
+    feat_ref[0] = layer_norm(final, tail_ref[2:3], tail_ref[3:4])
+
+
+def start_rows(embed_table):
+    tail_rows = table_tail(embed_table)
+    position = embed_table[PIX : PIX + SEQ].astype(FULL)
+    return jnp.concatenate(
+        [
+            position[1:] + tail_rows[0],
+            (position[0] + tail_rows[1])[None],
+            jnp.zeros((TOKENS - SEQ, D), FULL),
+        ],
+        0,
+    )
+
+
+def padded_vectors(embed_table):
+    return jnp.pad(table_vectors(embed_table), ((0, 0), (0, 2), (0, 0)))
+
+
+def padded_tail(embed_table):
+    return jnp.pad(table_tail(embed_table), ((0, 4), (0, 0)))
+
+
+def forward(patches, embed_table, layer_full, devices, save):
+    images = patches.shape[0]
+    blocks = layer_full.reshape(LAYERS, devices, -1, D)
+    cuts = [lower for lower, upper in layer_bounds(devices)][1:] + [blocks.shape[2]]
+    shape = jax.ShapeDtypeStruct
+
+    def whole(*dims):
+        return pl.BlockSpec(dims, lambda layer, image: (0,) * len(dims))
+
+    outs = [shape((images, 8, D), FULL)] * 2
+    specs = [pl.BlockSpec((1, 8, D), lambda layer, image: (image, 0, 0))] * 2
+    if save:
+        for name in SAVED:
+            width, kind = saved_widths()[name]
+            outs.append(shape((LAYERS, images, TOKENS, width), kind))
+            specs.append(
+                pl.BlockSpec((1, 1, TOKENS, width), lambda layer, image: (layer, image, 0, 0))
+            )
+    return pl.pallas_call(
+        functools.partial(forward_kernel, cuts, save),
+        grid=(LAYERS, images),
+        out_shape=outs,
+        in_specs=[
+            pl.BlockSpec(
+                (1,) + patches.shape[1:], lambda layer, image: (jnp.where(layer == 0, image, 0), 0, 0)
+            ),
+            whole(PIX, D),
+            whole(TOKENS, D),
+            pl.BlockSpec((1,) + blocks.shape[1:], lambda layer, image: (layer, 0, 0, 0)),
+            pl.BlockSpec((1, 8, D), lambda layer, image: (layer, 0, 0)),
+            whole(8, D),
+        ],
+        out_specs=specs,
+        scratch_shapes=[
+            pltpu.VMEM((images, TOKENS, D), FULL),
+            pltpu.VMEM((3 * D, D), LOW),
+            pltpu.VMEM((D, D), LOW),
+        ],
+        compiler_params=pltpu.CompilerParams(vmem_limit_bytes=56 << 20),
+        name="forward_save" if save else "forward",
+    )(
+        patches,
+        embed_table[:PIX],
+        start_rows(embed_table),
+        blocks,
+        padded_vectors(embed_table),
+        padded_tail(embed_table),
+    )
+
+
+def backward_kernel(cuts, depth, *refs):
+    (patches_ref, weights_ref, vectors_ref, tail_ref, final_ref, grad_feat_ref) = refs[:6]
+    saved = dict(zip(SAVED, refs[6 : 6 + len(SAVED)]))
+    (
+        packet_ref,
+        grad_patch_ref,
+        grad_start_ref,
+        grad_vectors_ref,
+        grad_tail_ref,
+        grad_now,
+        joint_weight,
+        output_weight,
+        grad_outer_all,
+        grad_inner_all,
+        grad_attended_all,
+        grad_joint_all,
+    ) = refs[6 + len(SAVED) :]
+    step, image = pl.program_id(0), pl.program_id(1)
+    images = pl.num_programs(1)
+    weights = weights_ref.at[0]
+    vectors = vectors_ref[0]
+
+    @pl.when(image == 0)
+    def _():
+        unpack_blocks(weights, joint_weight, output_weight, cuts)
+        grad_vectors_ref[...] = jnp.zeros(grad_vectors_ref.shape, FULL)
+
+    @pl.when((step == 0) & (image == 0))
+    def _():
+        grad_tail_ref[...] = jnp.zeros(grad_tail_ref.shape, FULL)
+
+    @pl.when(step == 0)
+    def _():
+        first = lax.broadcasted_iota(jnp.int32, (8, D), 0) == 0
+        given = jnp.where(first, grad_feat_ref[image], 0.0)
+        grad_class, grad_gain, grad_shift = norm_back(final_ref[image], tail_ref[2:3], given)
+        grad_tail_ref[2:3] += grad_gain[None]
+        grad_tail_ref[3:4] += grad_shift[None]
+        grad_now[image] = jnp.zeros((TOKENS, D), FULL)
+        grad_now[image, HALF_ROW : HALF_ROW + 8] = jnp.where(first, grad_class, 0.0)
+
+    rows = pl.ds(pl.multiple_of(image * TOKENS, 16), TOKENS)
+    grad_result = grad_now[image]
+    grad_outer = (vectors[5:6] * grad_result).astype(LOW)
+    grad_outer_all[rows, :] = grad_outer
+    grad_scale_two = jnp.sum(grad_result * saved["outer"][0, image].astype(FULL), 0, keepdims=True)
+    parts = MLP // D
+    grad_normed_two = jnp.zeros((TOKENS, D), FULL)
+    for part in range(parts):
+        columns = slice(part * D, (part + 1) * D)
+        grad_activated = dot_nt(grad_outer, weight_rows(weights, cuts, 2, part, parts))
+        grad_inner = (grad_activated * saved["slope"][0, image, :, columns].astype(FULL)).astype(LOW)
+        grad_inner_all[rows, columns] = grad_inner
+        grad_normed_two = grad_normed_two + dot_nn(grad_inner, weight_rows(weights, cuts, 1, part, parts))
+    grad_middle_norm, grad_gain_two, grad_shift_two = norm_back(
+        saved["middle"][0, image], vectors[2:3], grad_normed_two
+    )
+    grad_middle = grad_result + grad_middle_norm
+    grad_attended = (vectors[4:5] * grad_middle).astype(LOW)
+    grad_attended_all[rows, :] = grad_attended
+    grad_scale_one = jnp.sum(grad_middle * saved["attended"][0, image].astype(FULL), 0, keepdims=True)
+    grad_mixed = dot_nn(grad_attended, output_weight[...]).astype(LOW)
+    lane = lax.broadcasted_iota(jnp.int32, (TOKENS, LANES), 1)
+    live = lax.broadcasted_iota(jnp.int32, (TOKENS, TOKENS), 0) < SEQ
+    for pair in range(D // LANES):
+        lower = pair * LANES
+        queries, keys_in, values_in = [
+            saved["joint"][0, image, :, third * D + lower : third * D + lower + LANES]
+            for third in range(3)
+        ]
+        queries = (queries.astype(FULL) * HEAD_DIM ** (-0.5)).astype(LOW)
+        keys_wide = keys_in.astype(FULL)
+        values_wide = values_in.astype(FULL)
+        keys_turned = keys_wide.T.astype(LOW)
+        grad_head = grad_mixed[:, lower : lower + LANES]
+        turned, grad_keys, grad_values = [], [], []
+        for half in range(2):
+            mine = (lane >= HEAD_DIM) == bool(half)
+            share = chance(jnp.where(mine, keys_wide, 0.0).astype(LOW), queries, live)
+            grad_share = dot_nt(jnp.where(mine, values_wide, 0.0).astype(LOW), grad_head)
+            grad_values.append(dot_nn(share.astype(LOW), grad_head))
+            grad_scores = (
+                share * (grad_share - jnp.sum(share * grad_share, 0, keepdims=True))
+            ).astype(LOW)
+            grad_keys.append(dot_nn(grad_scores, queries))
+            turned.append(dot_nn(keys_turned[half * HEAD_DIM : (half + 1) * HEAD_DIM], grad_scores))
+        grad_queries = jnp.concatenate(turned, 0).T * HEAD_DIM ** (-0.5)
+        low_half = lane < HEAD_DIM
+        for third, value in enumerate(
+            (
+                grad_queries,
+                jnp.where(low_half, grad_keys[0], grad_keys[1]),
+                jnp.where(low_half, grad_values[0], grad_values[1]),
+            )
+        ):
+            grad_joint_all[rows, third * D + lower : third * D + lower + LANES] = value.astype(LOW)
+    grad_normed = dot_nn(grad_joint_all[rows, :], joint_weight[...])
+    grad_input_norm, grad_gain_one, grad_shift_one = norm_back(
+        saved["inputs"][0, image], vectors[0:1], grad_normed
+    )
+    grad_input = grad_middle + grad_input_norm
+    grad_now[image] = grad_input
+    for at, value in enumerate(
+        (
+            grad_gain_one[None],
+            grad_shift_one[None],
+            grad_gain_two[None],
+            grad_shift_two[None],
+            grad_scale_one,
+            grad_scale_two,
+        )
+    ):
+        grad_vectors_ref[0, at : at + 1] += value
+
+    @pl.when(image == images - 1)
+    def _():
+        devices = packet_ref.shape[0]
+
+        def flat(name):
+            value = saved[name][0]
+            return value.reshape(-1, value.shape[-1])
+
+        per = cuts[0], cuts[1] - cuts[0], cuts[2] - cuts[1], cuts[3] - cuts[2]
+
+        def slot(device):
+            return (device % 8) * depth + device // 8
+
+        groups = 4
+        each = devices // groups
+        for at in range(groups):
+            first = at * each
+            joint_rows = dot_tn(grad_joint_all[:, first * per[0] : (first + each) * per[0]], flat("normed"))
+            output_rows = dot_tn(
+                grad_attended_all[:, first * per[1] : (first + each) * per[1]], flat("mixed")
+            )
+            inner_rows = dot_tn(
+                grad_inner_all[:, first * per[2] : (first + each) * per[2]], flat("normed_two")
+            ).astype(LOW)
+            outer_rows = dot_tn(
+                saved["activated"][0, :, :, first * per[3] : (first + each) * per[3]].reshape(
+                    -1, each * per[3]
+                ),
+                grad_outer_all[...],
+            ).astype(LOW)
+            for t in range(each):
+                joined_rows = jnp.concatenate(
+                    [
+                        joint_rows[t * per[0] : (t + 1) * per[0]],
+                        output_rows[t * per[1] : (t + 1) * per[1]],
+                    ],
+                    0,
+                )
+                place = slot(first + t)
+                packet_ref[place, : cuts[1]] = joined_rows.astype(LOW)
+                packet_ref[place, cuts[1] : cuts[2]] = inner_rows[t * per[2] : (t + 1) * per[2]]
+                packet_ref[place, cuts[2] : cuts[3]] = outer_rows[t * per[3] : (t + 1) * per[3]]
+
+    @pl.when(step == pl.num_programs(0) - 1)
+    def _():
+        @pl.when(image == 0)
+        def _():
+            grad_patch_ref[...] = jnp.zeros(grad_patch_ref.shape, FULL)
+            grad_start_ref[...] = jnp.zeros(grad_start_ref.shape, FULL)
+
+        grad_patch_ref[...] += dot_tn(patches_ref[image], grad_input[:HALF_ROW].astype(LOW))
+        grad_start_ref[...] += grad_input
+        grad_tail_ref[0:1] += jnp.sum(grad_input[:HALF_ROW], 0, keepdims=True)
+        grad_tail_ref[1:2] += grad_input[HALF_ROW : HALF_ROW + 1]
+
+
+def backward(patches, embed_table, layer_full, final, grad_feat, saved, devices):
+    images = patches.shape[0]
     depth = devices // 8
-    layers = grad_layers.shape[0]
-    parts = grad_layers.reshape(layers, devices, -1, D).transpose(1, 0, 2, 3).reshape(devices, -1, D)
+    blocks = layer_full.reshape(LAYERS, devices, -1, D)
+    cuts = [lower for lower, upper in layer_bounds(devices)][1:] + [blocks.shape[2]]
+    shape = jax.ShapeDtypeStruct
+
+    def whole(*dims):
+        return pl.BlockSpec(dims, lambda step, image: (0,) * len(dims))
+
+    def of_layer(*dims):
+        return pl.BlockSpec(
+            (1,) + dims, lambda step, image: (LAYERS - 1 - step,) + (0,) * len(dims)
+        )
+
+    all_rows = images * TOKENS
+    packets, grad_patch, grad_start, grad_vectors, grad_tail = pl.pallas_call(
+        functools.partial(backward_kernel, cuts, depth),
+        grid=(LAYERS, images),
+        out_shape=(
+            shape((devices, LAYERS * blocks.shape[2], D), LOW),
+            shape((PIX, D), FULL),
+            shape((TOKENS, D), FULL),
+            shape((LAYERS, 8, D), FULL),
+            shape((8, D), FULL),
+        ),
+        in_specs=[
+            whole(*patches.shape),
+            of_layer(*blocks.shape[1:]),
+            of_layer(8, D),
+            whole(8, D),
+            whole(images, 8, D),
+            whole(images, 8, D),
+        ]
+        + [of_layer(images, TOKENS, saved_widths()[name][0]) for name in SAVED],
+        out_specs=(
+            pl.BlockSpec(
+                (devices, blocks.shape[2], D), lambda step, image: (0, LAYERS - 1 - step, 0)
+            ),
+            whole(PIX, D),
+            whole(TOKENS, D),
+            of_layer(8, D),
+            whole(8, D),
+        ),
+        scratch_shapes=[
+            pltpu.VMEM((images, TOKENS, D), FULL),
+            pltpu.VMEM((3 * D, D), LOW),
+            pltpu.VMEM((D, D), LOW),
+            pltpu.VMEM((all_rows, D), LOW),
+            pltpu.VMEM((all_rows, MLP), LOW),
+            pltpu.VMEM((all_rows, D), LOW),
+            pltpu.VMEM((all_rows, 3 * D), LOW),
+        ],
+        compiler_params=pltpu.CompilerParams(vmem_limit_bytes=62 << 20),
+        name="backward",
+    )(
+        patches,
+        blocks,
+        padded_vectors(embed_table),
+        padded_tail(embed_table),
+        final,
+        grad_feat,
+        *saved,
+    )
+    grad_table = jnp.concatenate(
+        [
+            grad_patch,
+            grad_start[SEQ - 1 : SEQ],
+            grad_start[: SEQ - 1],
+            grad_vectors[:, :6].reshape(-1, D),
+            grad_tail[:4],
+        ],
+        0,
+    )
+    return packets, grad_table
+
+
+def embedding_packet(grad_table, devices):
+    depth = devices // 8
     flat = grad_table.T.reshape(devices, -1)
     flat = jnp.pad(flat, ((0, 0), (0, -flat.shape[1] % (16 * D)))).reshape(devices, -1, D)
-    joint = jnp.concatenate([parts, flat], 1).astype(LOW)
-    ordered = joint.reshape((depth, 2, 2, 2) + joint.shape[1:]).transpose(1, 2, 3, 0, 4, 5)
-    return ordered.reshape(joint.shape)
+    ordered = flat.astype(LOW).reshape((depth, 2, 2, 2) + flat.shape[1:]).transpose(1, 2, 3, 0, 4, 5)
+    return ordered.reshape(flat.shape)
 
 
 def tail_fast(
-    squares, grad_table, grad_layers, layer_stats, layer_bases, owners, embedding, layers, devices
+    squares, grad_table, layer_packets, layer_stats, layer_bases, owners, embedding, layers, devices
 ):
     own_rows = layer_stats.shape[2]
     matrices = owners.shape[0]
     rows_layer = layers.shape[1]
     own, norm, full_stats, full_bases = collect(
         squares,
-        packets_of(grad_table, grad_layers, devices),
+        jnp.concatenate([layer_packets, embedding_packet(grad_table, devices)], 1),
         layer_stats.reshape(matrices, own_rows, D),
         layer_bases.reshape(matrices, own_rows, D),
         rows_layer,
@@ -1597,10 +2043,16 @@
         stats_full = lax.all_gather(layer_stats.astype(LOW), "dp", axis=2, tiled=True).astype(
             layer_stats.dtype
         )
-    features, layer_inputs, final_state = backbone(patches, embed_table, layer_full, devices)
-    teacher_features, unused_inputs, unused_final = backbone(
-        patches, teacher_table, teacher_full, devices
-    )
+    if fast:
+        feature_rows, final_rows, *saved = forward(patches, embed_table, layer_full, devices, True)
+        teacher_rows, unused_rows = forward(patches, teacher_table, teacher_full, devices, False)
+        features = feature_rows[:, 0].astype(LOW)
+        teacher_features = teacher_rows[:, 0].astype(LOW)
+    else:
+        features, layer_inputs, final_state = backbone(patches, embed_table, layer_full, devices)
+        teacher_features, unused_inputs, unused_final = backbone(
+            patches, teacher_table, teacher_full, devices
+        )
     if fast:
         (
             loss_sum,
@@ -1648,16 +2100,22 @@
             centre,
             device_index,
         )
-    grad_table, grad_layers = backbone_back(
-        patches,
-        embed_table,
-        layer_full,
-        layer_inputs,
-        final_state,
-        grad_features,
-        devices,
-        unchanged,
-    )
+    if fast:
+        grad_rows = jnp.pad(grad_features[:, None], ((0, 0), (0, 7), (0, 0)))
+        grad_layers, grad_table = backward(
+            patches, embed_table, layer_full, final_rows, grad_rows, saved, devices
+        )
+    else:
+        grad_table, grad_layers = backbone_back(
+            patches,
+            embed_table,
+            layer_full,
+            layer_inputs,
+            final_state,
+            grad_features,
+            devices,
+            unchanged,
+        )
     bounds = layer_bounds(devices)
     if fast:
         grad_norm, grad_embed, grad_layers_own, stats_own, bases_own = tail_fast(

time: 1070 us -> 701 us (0.66)
  matrix products: 231 us -> 12 us
  Pallas kernels: 282 us -> 472 us
  other arithmetic: 189 us -> 33 us
  local copies, waits for them, and re-layouts: 195 us -> 51.1 us
  waiting for transfers between devices: 138 us -> 109 us
    dot_general x72 -> x0, matrix products: 217 us -> none  [matmul_low(): return jnp.einsum(form, left, right, preferred_element_type=jnp.float32)]
    pallas_call x0 -> x3, Pallas kernels: none -> 189 us  [the longest x2 112 us: forward(): pl.pallas_call(functools.partial(forward_kernel, cuts, save), grid=(LAYER...]
    reduce_sum x38 -> x0, other arithmetic: 83.7 us -> none  [the longest x7 46.7 us: norm_back(): jnp.sum(grad_out * normed, leading)]
    all_gather x1, waiting for transfers between devices: 73.7 us -> 34.9 us  [per_device(): lax.all_gather(layers.astype(LOW), 'dp', axis=1, tiled=True)]
    sub x6 -> x0, other arithmetic: 33 us -> none  [layer_parts(): attention = jax.nn.softmax(scores, axis=-1)]
    convert_element_type x25 -> x2, other arithmetic: 32.8 us -> 1.95 us  [start_rows(): position = embed_table[PIX:PIX + SEQ].astype(FULL)]
    slice x25 -> x10, local copies, waits for them, and re-layouts: 34.1 us -> 4.12 us  [the longest x2 1.77 us: forward(): embed_table[:PIX]]
    convert_element_type x12 -> x2, local copies, waits for them, and re-layouts: 28.1 us -> 0.04 us  [the longest x1 0.02 us: per_device(): teacher_features = teacher_rows[:, 0].astype(LOW)]
  transfers between devices with their start and end apart: 3 -> 3, of which waited for: 2 -> 2; matrix products, arithmetic and copies ran while one was open for 6% -> 6% of each run, Pallas kernels for 4% -> 14%
where the time goes in v2:
time: 701 us; the launch traced here: 693 us
  Pallas kernels  472 us (67%)
  waiting for transfers between devices  109 us (16%)
  local copies, waits for them, and re-layouts  51.1 us (7%)
  other arithmetic  33 us (5%)
  between operations  15.8 us (2%)
  matrix products  12 us (2%)
    pallas_call x2, Pallas kernels, forward(): pl.pallas_call(functools.partial(forward_kernel, cuts, save), grid=(LAYER...  112 us
    pallas_call x1, Pallas kernels, collect(): pl.pallas_call(functools.partial(collect_kernel, depth, rows_layer, bound...  90.7 us
    pallas_call x1, Pallas kernels, head(): pl.pallas_call(functools.partial(head_kernel, devices), out_shape=(shape(...  81.7 us
    pallas_call x1, Pallas kernels, backward(): pl.pallas_call(functools.partial(backward_kernel, cuts, depth), grid=(LAY...  77 us
    all_gather x1, waiting for transfers between devices, per_device(): lax.all_gather(teacher_layers.astype(LOW), 'dp', axis=1, tiled=True)  74.4 us
    pallas_call x1, Pallas kernels, spread(): pl.pallas_call(functools.partial(spread_kernel, depth), out_shape=(jax.Sh...  42.1 us
    pallas_call x1, Pallas kernels, renew_own(): pl.pallas_call(renew_kernel, out_shape=jax.ShapeDtypeStruct(stats.shape,...  39.7 us
    all_gather x1, waiting for transfers between devices, per_device(): lax.all_gather(layers.astype(LOW), 'dp', axis=1, tiled=True)  34.9 us
  transfers between devices with their start and end apart: 3, of which 2 were waited for; matrix products, arithmetic and copies ran while one was open for 6% of the time, Pallas kernels for 14%

profile of v2, /device:TPU:31, one launch (start us, length us, event | category | flops | bytes accessed | tf_op | source)
XLA Modules:
  0.0 693.4 jit_solution(9360257663504703764)
XLA Ops:
  7.3 1.7 copy.123
  9.1 1.9 convert_element_type.105
  12.3 42.1 %spread.1 = (bf16[32,448,128]{2,1,0:T(8,128)(2,1)S(1)}, bf16[32,64,128]{2,1,0:T(8,128)(2,1)S(1)}) custom-call(bf16[448,128]{1,0:T(8,128)(2,1)S(1)} %pad_maximum_fusion.4.small_ref, bf16[64,2048]{1,0:T(8,128)(2,1)S(1)} %slice.311.columns_ref), custom_call_target="tpu_custom_call" | custom-call | tf_op jit(solution)/shard_map/spread/pallas_call | solution.py:446
  55.2 1.8 copy-done.10
  60.9 2.1 reshape.183
  65.1 2.2 copy.82.patches_ref.refs_0_
  68.6 2.7 fusion.83
  79.2 12.9 %fusion.85 = (bf16[3,1,384,384]{3,1,0,2:T(2,128)(2,1)}, bf16[3,1,384,384]{3,1,0,2:T(2,128)(2,1)}, bf16[3,1,384,384]{3,1,0,2:T(2,128)(2,1)}, bf16[3,1,384,384]{3,1,0,2:T(2,128)(2,1)}) fusion(bf16[3,4,384,384]{3,1,0,2:T(4,128)(2,1)} %all-gather.8.cloned.1.call-done), kind=kLoop, calls=%fused_computation.158 | loop fusion | bytes 7077888 | tf_op jit(solution)/shard_map/slice | solution.py:2190
  92.1 74.4 %all-gather.6.cloned.1.call-done = bf16[3,4608,384]{2,1,0:T(8,128)(2,1)} async-done(((bf16[3,144,384]{2,1,0:T(8,128)(2,1)}), bf16[3,4608,384]{2,1,0:T(8,128)(2,1)}) %all-gather.6.cloned.1.call-update) | async-done | bytes 10616848 | tf_op jit(solution)/shard_map/all_gather | solution.py:2037
  166.5 53.7 %forward.1 = (f32[3,8,384]{2,1,0:T(8,128)}, f32[3,8,384]{2,1,0:T(8,128)}) custom-call(bf16[3,256,588]{2,1,0:T(8,128)(2,1)} %copy.82.patches_ref.refs_0_, bf16[588,384]{1,0:T(8,128)(2,1)} %slice.245.table_ref, f32[272,384]{1,0:T(8,128)} %get-tuple-element.211.start_ref, bf16[3,32,144,384]{3,2,1,0:T(8,128)(2,1)} %bitcast.98, ...), custom_call_target="tpu_custom_call" | custom-call | tf_op jit(solution)/shard_map/forward/pallas_call | solution.py:1671
  221.1 34.9 %all-gather.4.cloned.1.call-done = bf16[3,4608,384]{2,1,0:T(8,128)(2,1)} async-done(((bf16[3,144,384]{2,1,0:T(8,128)(2,1)}), bf16[3,4608,384]{2,1,0:T(8,128)(2,1)}) %all-gather.4.cloned.1.call-update) | async-done | bytes 10616848 | tf_op jit(solution)/shard_map/all_gather | solution.py:2036
  256.0 58.6 %forward_save.1 = (f32[3,8,384]{2,1,0:T(8,128)}, f32[3,8,384]{2,1,0:T(8,128)}, f32[3,3,272,384]{3,2,1,0:T(8,128)}, bf16[3,3,272,384]{3,2,1,0:T(8,128)(2,1)}, bf1...) custom-call(bf16[3,256,588]{2,1,0:T(8,128)(2,1)} %copy.82.patches_re, ...), custom_call_target="tpu_custom_call" | custom-call | tf_op jit(solution)/shard_map/forward_save/pallas_call | solution.py:1671
  316.6 81.7 %head.1 = (f32[8,128]{1,0:T(8,128)S(1)}, f32[64,2432]{1,0:T(8,128)S(1)}, f32[8,2048]{1,0:T(8,128)S(1)}, f32[256,2048]{1,0:T(8,128)}, f32[8,384]{1,0:T(8,128)S(1)}, /*index=5*/f32[1,2048]{1,0:T(1,128)S(1)}) custom-call(bf16[32,128]{1,0:T(8,128)(2,1)S(1)} %fusion.60.feat_ref, f32[64,2432]{1,0:T(8,128)S(1)} %copy-done, f32[64,2432]{1,0:T(8,128)S(1)} %copy-done.2, ...), custom_call_target="tpu_custom_call" | custom-call | tf_op jit(solution)/shard_map/head/pallas_call | solution.py:786
  399.7 77.0 %backward.1 = (bf16[32,432,384]{2,1,0:T(8,128)(2,1)}, f32[588,384]{1,0:T(8,128)}, f32[272,384]{1,0:T(8,128)}, f32[3,8,384]{2,1,0:T(8,128)}, f32[8,384]{1,0:T(8,128)}) custom-call(bf16[3,256,588]{2,1,0:T(8,128)(2,1)} %copy.82.patches_ref.refs_0_, bf16[3,32,144,384]{3,2,1,0:T(8,128)(2,1)} %bitcast.95, f32[3,8,384]{2,1,0:T(8,128)} %pad_convert_fusion.1.vectors_ref.refs_2_, ...), custom_call_target="tpu_custom_call" | custom-call | tf_op jit(solution)/shard_map/backward/pallas_call | solution.py:1889
  483.3 9.9 %pad_maximum_fusion.packet_ref = bf16[32,464,384]{2,1,0:T(8,128)(2,1)} fusion(bf16[32,32,384]{2,1,0:T(8,128)(2,1)S(1)} %bitcast.99, bf16[32,432,384]{2,1,0:T(8,128)(2,1)} %get-tuple-element.75), kind=kLoop, calls=%fused_computation | loop fusion | flops 22806528 | bytes 22806528 | tf_op jit(solution)/shard_map/concatenate | solution.py:1966
  493.2 90.7 %collect.1 = (f32[464,384]{1,0:T(8,128)}, f32[8,128]{1,0:T(8,128)}, f32[32,12,384]{2,1,0:T(8,128)}, f32[32,12,384]{2,1,0:T(8,128)}) custom-call(f32[8,128]{1,0:T(8,128)} %copy-done.9, bf16[32,464,384]{2,1,0:T(8,128)(2,1)} %pad_maximum_fusion.packet_ref, f32[12,12,384]{2,1,0:T(8,128)} %bitcast.119, f32[12,12,384]{2,1,0:T(8,128)} %bitcast.114), custom_call_target="tpu_custom_call" | custom-call | tf_op jit(solution)/shard_map/collect/pallas_call | solution.py:1118
  584.8 2.0 slice.211
  588.7 2.3 fusion.13
  591.0 2.1 fusion.44
  596.4 1.7 fusion.4
  604.4 39.7 %renew.1.bases_ref = f32[32,12,384]{2,1,0:T(8,128)S(1)} custom-call(f32[32,12,384]{2,1,0:T(8,128)S(1)} %copy-done.1, f32[32,12,384]{2,1,0:T(8,128)S(1)} %copy-done.3), custom_call_target="tpu_custom_call" | custom-call | tf_op jit(solution)/shard_map/renew/pallas_call | solution.py:1239
  644.2 28.3 %deal.1 = (f32[12,12,384]{2,1,0:T(8,128)S(1)}, f32[12,12,384]{2,1,0:T(8,128)S(1)}) custom-call(f32[32,12,384]{2,1,0:T(8,128)S(1)} %copy-done.1, f32[32,12,384]{2,1,0:T(8,128)S(1)} %renew.1.bases_ref), custom_call_target="tpu_custom_call" | custom-call | tf_op jit(solution)/shard_map/deal/pallas_call | solution.py:1293
  674.1 3.0 multiply_add_fusion.3
  678.8 5.0 multiply_add_fusion
  (203 shorter events, 45.1 us)
Async XLA Ops:
  7.3 4.9 copy-start
  7.3 72.0 %all-gather.8.cloned.1.call-start = ((), (), s32[]{:S(2)}) async-start(), calls=%async_computation.2 | async-start | bytes 3649536 | tf_op jit(solution)/shard_map/all_gather | solution.py:2039
  9.1 157.4 %all-gather.6.cloned.1.call-start = ((), (), s32[]{:S(2)}) async-start(), calls=%async_computation.1 | async-start | bytes 10948608 | tf_op jit(solution)/shard_map/all_gather | solution.py:2037
  11.0 245.0 %all-gather.4.cloned.1.call-start = ((), (), s32[]{:S(2)}) async-start(), calls=%async_computation | async-start | bytes 10948608 | tf_op jit(solution)/shard_map/all_gather | solution.py:2036
  58.8 8.5 %copy-start.17 = (bf16[384,867]{0,1:T(8,128)(2,1)}, bf16[384,867]{0,1:T(8,128)(2,1)S(1)}, u32[]{:S(2)}) copy-start(bf16[384,867]{0,1:T(8,128)(2,1)S(1)} %copy.84) | copy-start | bytes 1997572
  256.0 59.5 %copy-start.2 = (f32[64,2432]{1,0:T(8,128)S(1)}, f32[64,2432]{1,0:T(8,128)}, u32[]{:S(2)}) copy-start(f32[64,2432]{1,0:T(8,128)} %teacher_hidden_ref.1) | copy-start | bytes 1867780
  256.0 59.5 %copy-start.8 = (f32[2048]{0:T(1024)S(1)}, f32[2048]{0:T(1024)}, u32[]{:S(2)}) copy-start(f32[2048]{0:T(1024)} %param.51) | copy-start | bytes 24580
  399.1 78.8 %copy-start.9 = (f32[8,128]{1,0:T(8,128)}, f32[8,128]{1,0:T(8,128)S(1)}, u32[]{:S(2)}) copy-start(f32[8,128]{1,0:T(8,128)S(1)} %get-tuple-element.62.squares_ref) | copy-start | bytes 12292
  583.9 9.2 %copy-start.13 = (bf16[3,1,384,384]{3,1,0,2:T(2,128)(2,1)S(1)}, bf16[3,1,384,384]{3,1,0,2:T(2,128)(2,1)}, u32[]{:S(2)}) copy-start(bf16[3,1,384,384]{3,1,0,2:T(2,128)(2,1)} %get-tuple-element.190) | copy-start | bytes 2654212
  588.7 4.9 copy-start.15
  601.5 75.7 %copy-start.32 = (f32[2048,8]{0,1:T(8,128)S(1)}, f32[2048,8]{0,1:T(8,128)}, u32[]{:S(2)}) copy-start(f32[2048,8]{0,1:T(8,128)} %param.40) | copy-start | bytes 196612
  601.5 75.7 %copy-start.44 = (f32[2048,8]{0,1:T(8,128)S(1)}, f32[2048,8]{0,1:T(8,128)}, u32[]{:S(2)}) copy-start(f32[2048,8]{0,1:T(8,128)} %param.42) | copy-start | bytes 196612
  604.4 68.8 %copy-start.19 = (f32[3,4,12,384]{3,2,1,0:T(8,128)S(1)}, f32[3,4,12,384]{3,2,1,0:T(8,128)}, u32[]{:S(2)}) copy-start(f32[3,4,12,384]{3,2,1,0:T(8,128)} %copy.92) | copy-start | bytes 663556
  604.4 68.8 %copy-start.48 = (pred[12]{0:T(512)(128)(4,1)S(1)}, pred[12]{0:T(512)(128)(4,1)}, u32[]{:S(2)}) copy-start(pred[12]{0:T(512)(128)(4,1)} %broadcast_compare_fusion) | copy-start | bytes 40
  604.4 74.4 %copy-start.24 = (f32[256,2048]{1,0:T(8,128)S(1)}, f32[256,2048]{1,0:T(8,128)}, u32[]{:S(2)}) copy-start(f32[256,2048]{1,0:T(8,128)} %get-tuple-element.88) | copy-start | bytes 6291460
  644.1 30.0 %copy-start.5 = (f32[64,2432]{1,0:T(8,128)S(1)}, f32[64,2432]{1,0:T(8,128)}, u32[]{:S(2)}) copy-start(f32[64,2432]{1,0:T(8,128)} %copy-done.4) | copy-start | bytes 1867780
  644.2 30.0 %copy-start.29 = (f32[64,2432]{1,0:T(8,128)S(1)}, f32[64,2432]{1,0:T(8,128)}, u32[]{:S(2)}) copy-start(f32[64,2432]{1,0:T(8,128)} %param.39) | copy-start | bytes 1867780
  644.2 34.6 %copy-start.23 = (f32[256,2048]{1,0:T(8,128)S(1)}, f32[256,2048]{1,0:T(8,128)}, u32[]{:S(2)}) copy-start(f32[256,2048]{1,0:T(8,128)} %param.44) | copy-start | bytes 6291460
  673.3 5.4 copy-start.22
  678.8 5.0 copy-start.20
  678.8 5.0 copy-start.40
  678.8 5.0 copy-start.41
  678.8 5.0 copy-start.42
  678.8 5.0 copy-start.43
  (30 other events, 86.8 us)
Sparse Core Ops, SparseCore 0:
  11.6 65.7 all-gather.7
  80.9 85.5 all-gather.5
  170.0 85.9 all-gather.3

commit v3 on v1

--- a/solution.py
+++ b/solution.py
@@ -371,96 +371,124 @@
     return lax.dot_general(left, right, (((0,), (0,)), ((), ())), preferred_element_type=FULL)
 
 
-def spread_kernel(depth, small_ref, columns_ref, all_ref, part_ref, own_sem, sent, landed, csent, clanded):
-    me = lax.axis_index("dp")
-    total = 8 * depth
-    core = lax.rem(me, 2)
-    x_at = lax.rem(me // 2, 2)
-    y_at = lax.rem(me // 4, 2)
-    z_at = me // 8
-    peers = [lax.rem(me + step, total) for step in range(1, total)]
-    greet(peers)
-
-    def place(y_pos, x_pos, c_pos):
-        return ((y_pos * 2 + x_pos) * 2 + c_pos) * depth
-
-    mine = place(y_at, x_at, core)
-    across_x = place(y_at, 1 - x_at, core)
-    across_y = place(1 - y_at, x_at, core)
-    across_d = place(1 - y_at, 1 - x_at, core)
-    partner = me + 1 - 2 * core
-    to_x = me + 2 - 4 * x_at
-    to_y = me + 4 - 8 * y_at
-    own = pltpu.make_async_copy(small_ref, all_ref.at[mine + z_at], own_sem.at[0])
-    own.start()
-    copies = []
-    z_copies = []
-    for step in range(1, depth):
-        peer = lax.rem(me + 8 * step, total)
-        z_copies.append(
-            push(small_ref, all_ref.at[mine + z_at], sent.at[step], landed.at[step], peer)
-        )
-    hid_rows = columns_ref.shape[0]
-    c_copies = []
-    for step, peer in enumerate(peers):
-        block = columns_ref.at[:, pl.ds(pl.multiple_of((peer // 2) * LANES, LANES), LANES)]
-        c_copies.append(push(block, part_ref.at[me], csent.at[step], clanded.at[step], peer))
-    own_block = columns_ref.at[:, pl.ds(pl.multiple_of((me // 2) * LANES, LANES), LANES)]
-    own_part = pltpu.make_async_copy(own_block, part_ref.at[me], own_sem.at[1])
-    own_part.start()
-    own.wait()
-    for copy in z_copies:
-        copy.wait_recv()
-    base = depth
-
-    def column(start, where, device):
-        view = all_ref.at[pl.ds(start, depth)]
-        return push(view, view, sent.at[where], landed.at[where], device)
-
-    x_copy = column(mine, base, to_x)
-    y_copy = column(mine, base + 1, to_y)
-    die_own = column(mine, base + 2, partner)
-    half = small_ref.shape[0] // 2
-    x_copy.wait_recv()
-    from_x = all_ref.at[pl.ds(across_x, depth), pl.ds(0, half)]
-    d_one = push(from_x, from_x, sent.at[base + 3], landed.at[base + 3], to_y)
-    die_x = column(across_x, base + 5, partner)
-    y_copy.wait_recv()
-    from_y = all_ref.at[pl.ds(across_y, depth), pl.ds(half, half)]
-    d_two = push(from_y, from_y, sent.at[base + 4], landed.at[base + 4], to_x)
-    die_y = column(across_y, base + 6, partner)
-    d_one.wait_recv()
-    d_two.wait_recv()
-    die_d = column(across_d, base + 7, partner)
-    for copy in (die_own, die_x, die_y, die_d):
-        copy.wait_recv()
-    for copy in c_copies:
-        copy.wait_recv()
-    own_part.wait()
-    for copy in z_copies + c_copies + [x_copy, y_copy, die_own, d_one, d_two, die_x, die_y, die_d]:
-        copy.wait_send()
-
-
-def spread(small, columns, devices):
-    depth = devices // 8
-    return pl.pallas_call(
-        functools.partial(spread_kernel, depth),
-        out_shape=(
-            jax.ShapeDtypeStruct((devices,) + small.shape, small.dtype),
-            jax.ShapeDtypeStruct((devices, columns.shape[0], LANES), columns.dtype),
-        ),
-        in_specs=[pl.BlockSpec(memory_space=pltpu.VMEM)] * 2,
-        out_specs=(pl.BlockSpec(memory_space=pltpu.VMEM),) * 2,
-        scratch_shapes=[
-            pltpu.SemaphoreType.DMA((2,)),
-            pltpu.SemaphoreType.DMA((depth + 8,)),
-            pltpu.SemaphoreType.DMA((depth + 8,)),
-            pltpu.SemaphoreType.DMA((devices - 1,)),
-            pltpu.SemaphoreType.DMA((devices - 1,)),
-        ],
-        compiler_params=params(1),
-        name="spread",
-    )(small, columns)
+def slot_of(device, depth):
+    return (device % 8) * depth + device // 8
+
+
+class Route:
+    def __init__(self, depth, items, own_sem, z_sent, z_landed, near_sent, near_landed, die_sent, die_landed):
+        self.depth = depth
+        self.items = items
+        self.sems = (own_sem, z_sent, z_landed, near_sent, near_landed, die_sent, die_landed)
+        me = lax.axis_index("dp")
+        self.me = me
+        self.total = 8 * depth
+        self.core = lax.rem(me, 2)
+        x_at = lax.rem(me // 2, 2)
+        y_at = lax.rem(me // 4, 2)
+        self.z_at = me // 8
+        self.partner = me + 1 - 2 * self.core
+        self.to_x = me + 2 - 4 * x_at
+        self.to_y = me + 4 - 8 * y_at
+        places = [(y_at, x_at), (y_at, 1 - x_at), (1 - y_at, x_at), (1 - y_at, 1 - x_at)]
+        self.starts = [((y * 2 + x) * 2 + self.core) * depth for y, x in places]
+
+    def copy(self, source, target, sent, landed, device):
+        return pltpu.make_async_remote_copy(
+            src_ref=source,
+            dst_ref=target,
+            send_sem=sent,
+            recv_sem=landed,
+            device_id=(device,),
+            device_id_type=MESH,
+        )
+
+    def half(self, at):
+        size = self.items[at][3]
+        return (size // 2 + 15) // 16 * 16
+
+    def own(self, at):
+        source, target, lower, size = self.items[at]
+        return pltpu.make_async_copy(
+            source.at[pl.ds(lower, size)],
+            target.at[self.starts[0] + self.z_at, pl.ds(lower, size)],
+            self.sems[0].at[at],
+        )
+
+    def deep(self, at, step):
+        source, target, lower, size = self.items[at]
+        return self.copy(
+            source.at[pl.ds(lower, size)],
+            target.at[self.starts[0] + self.z_at, pl.ds(lower, size)],
+            self.sems[1].at[at, step],
+            self.sems[2].at[at, step],
+            lax.rem(self.me + 8 * step, self.total),
+        )
+
+    def near(self, at, which):
+        source, target, lower, size = self.items[at]
+        half = self.half(at)
+        column, first, length, device = [
+            (0, lower, size, self.to_x),
+            (0, lower, size, self.to_y),
+            (1, lower, half, self.to_y),
+            (2, lower + half, size - half, self.to_x),
+        ][which]
+        view = target.at[pl.ds(self.starts[column], self.depth), pl.ds(first, length)]
+        return self.copy(view, view, self.sems[3].at[at, which], self.sems[4].at[at, which], device)
+
+    def die(self, at, column):
+        source, target, lower, size = self.items[at]
+        view = target.at[pl.ds(self.starts[column], self.depth), pl.ds(lower, size)]
+        return self.copy(
+            view, view, self.sems[5].at[at, column], self.sems[6].at[at, column], self.partner
+        )
+
+    def act(self, stage, at):
+        if stage == "A":
+            self.own(at).start()
+            for step in range(1, self.depth):
+                self.deep(at, step).start()
+        elif stage == "B":
+            self.own(at).wait()
+            for step in range(1, self.depth):
+                self.deep(at, step).wait_recv()
+            self.near(at, 0).start()
+            self.near(at, 1).start()
+            self.die(at, 0).start()
+        elif stage == "C":
+            self.near(at, 0).wait_recv()
+            self.near(at, 2).start()
+            self.die(at, 1).start()
+            self.near(at, 1).wait_recv()
+            self.near(at, 3).start()
+            self.die(at, 2).start()
+        elif stage == "D":
+            self.near(at, 2).wait_recv()
+            self.near(at, 3).wait_recv()
+            self.die(at, 3).start()
+        elif stage == "E":
+            for column in range(4):
+                self.die(at, column).wait_recv()
+        else:
+            for step in range(1, self.depth):
+                self.deep(at, step).wait_send()
+            for which in range(4):
+                self.near(at, which).wait_send()
+                self.die(at, which).wait_send()
+
+
+def route_sems(count, depth):
+    dma = pltpu.SemaphoreType.DMA
+    return [
+        dma((count,)),
+        dma((count, depth)),
+        dma((count, depth)),
+        dma((count, 4)),
+        dma((count, 4)),
+        dma((count, 4)),
+        dma((count, 4)),
+    ]
 
 
 def head_kernel(
@@ -476,12 +504,14 @@
     centre_ref,
     mask_ref,
     mask_row_ref,
+    bases_ref,
     scalars_ref,
     grad_hidden_ref,
     grad_last_ref,
     grad_protos_ref,
     grad_feat_ref,
     centre_out_ref,
+    bases_all_ref,
     fb,
     hid_low,
     thid_low,
@@ -521,6 +551,7 @@
     wide_landed,
     core_sent,
     core_landed,
+    *sems,
 ):
     me = lax.axis_index("dp")
     core = lax.rem(me, 2)
@@ -533,6 +564,14 @@
     units = hidden_ref.shape[0]
     groups = images // 8
     greet(everyone)
+    layer_part = bases_ref.shape[0] // LAYERS
+    items = [(bases_ref, bases_all_ref, at * layer_part, layer_part) for at in range(LAYERS)]
+    route = Route(devices // 8, items, *sems)
+
+    def beside(*words):
+        for word in words:
+            route.act(word[0], int(word[1:]))
+
     sends = []
 
     def die(step, source, target):
@@ -570,6 +609,7 @@
     lead = row_at - 3 * col_dev
     for copy in copies:
         copy.wait_recv()
+    beside("A0")
     rows_all = fb[...].reshape(devices * block_rows, LANES)
 
     def features_of(model):
@@ -606,11 +646,13 @@
     pre1[...] = pre_one
     tpre_one = dot_nt(tfeats, thid_low[:, :D])
     gather_pair(0, gelu_exact(pre_one).astype(LOW).astype(FULL), gelu_exact(tpre_one).astype(LOW).astype(FULL), act_s, act_t)
+    beside("B0", "A1")
     pre_two = dot_nt(act_s[...], hid_low[:, D:])
     pre2[...] = pre_two
     tpre_two = dot_nt(act_t[...], thid_low[:, D:])
     gather_pair(1, gelu_exact(pre_two).astype(LOW).astype(FULL), gelu_exact(tpre_two).astype(LOW).astype(FULL), act2_s, act2_t)
 
+    beside("C0", "B1", "A2")
     unit, inverse_norm = unit_rows(dot_nt(act2_s[...], last_ref[...]))
     tunit, unused = unit_rows(dot_nt(act2_t[...], teacher_last_ref[...]))
     unit_ref[...] = unit
@@ -643,6 +685,7 @@
     )
     for copy in copies:
         copy.wait_recv()
+    beside("D0", "C1", "B2")
     merged = stat_all[...]
     tops, totals = merged[:, 0], merged[:, 1]
     ttops, ttotals, crosses = merged[:, 2], merged[:, 3], merged[:, 4]
@@ -701,6 +744,7 @@
         def _(group=group):
             pltpu.make_async_copy(dz_all.at[group], dz_all.at[group], wide_landed.at[3, group]).wait()
 
+    beside("E0", "D1", "C2")
     grad_bottle = dz_all[...].reshape(images, unit.shape[1]).astype(LOW)
     chip_columns = pl.ds(pl.multiple_of(chip * LANES, LANES), LANES)
     pair = dot_nn(grad_bottle, last_ref[:, chip_columns])
@@ -734,7 +778,9 @@
     copy.wait_recv()
     for at in range(chips):
         dp_full[their_rows, at * LANES : (at + 1) * LANES] = dp_half[1, at]
-    pair = dot_nn(dp_full[...], part_ref[...].reshape(devices * units, LANES))
+    beside("E1", "D2")
+    part = jnp.concatenate([part_ref[at % 2, at // 2] for at in range(devices)], 0)
+    pair = dot_nn(dp_full[...], part)
     grad_act_one = jnp.where(core == 0, pair[:, :units], pair[:, units:])
     grad_pre_one = (grad_act_one * gelu_slope(pre1[...])).astype(LOW)
 
@@ -755,6 +801,7 @@
     copy.wait_recv()
     whole = df_sum[...] + df_other[...]
     grad_feat_ref[...] = whole
+    beside("E2", "F0", "F1", "F2")
     squares = jnp.sum(grad_hidden_ref[...] * grad_hidden_ref[...])
     squares = squares + jnp.sum(grad_last_ref[...] * grad_last_ref[...])
     squares = squares + jnp.sum(grad_protos_ref[...] * grad_protos_ref[...])
@@ -773,7 +820,7 @@
             pltpu.make_async_copy(dz_own, dz_own, wide_sent.at[3, step - 1]).wait()
 
 
-def head(feat, hidden, teacher_hidden, part, last, teacher_last, protos, teacher_protos, centre, mask, mask_row, devices):
+def head(feat, hidden, teacher_hidden, part, last, teacher_last, protos, teacher_protos, centre, mask, mask_row, bases, devices):
     images = mask.shape[0]
     units, wide = hidden.shape
     bottle, width = protos.shape
@@ -792,9 +839,10 @@
             shape((bottle, width), FULL),
             shape((8, D), FULL),
             shape((1, width), FULL),
+            shape((devices,) + bases.shape, LOW),
         ),
-        in_specs=[vmem] * 11,
-        out_specs=(vmem,) * 6,
+        in_specs=[vmem] * 12,
+        out_specs=(vmem,) * 6 + (pl.BlockSpec(memory_space=pl.ANY),),
         scratch_shapes=[
             pltpu.VMEM((devices,) + feat.shape, LOW),
             pltpu.VMEM((units, wide), LOW),
@@ -835,323 +883,15 @@
             dma((4, devices)),
             dma((4, chips - 1)),
             dma((4, chips - 1)),
-        ],
+        ]
+        + route_sems(LAYERS, devices // 8),
         compiler_params=params(2),
         name="head",
-    )(feat, hidden, teacher_hidden, part, last, teacher_last, protos, teacher_protos, centre, mask, mask_row)
+    )(feat, hidden, teacher_hidden, part, last, teacher_last, protos, teacher_protos, centre, mask, mask_row, bases)
 
 
 def gram_device(matrix):
     return 2 * matrix
-
-
-def collect_kernel(
-    depth,
-    rows_layer,
-    bounds,
-    squares_ref,
-    packet_ref,
-    stats_ref,
-    bases_ref,
-    own_ref,
-    norm_ref,
-    next_stats_ref,
-    basis_ref,
-    die_buf,
-    d_buf,
-    x_buf,
-    y_buf,
-    z_buf,
-    stat_buf,
-    square_out,
-    square_all,
-    segs,
-    gram_buf,
-    die_sent,
-    die_landed,
-    near_sent,
-    near_landed,
-    z_sent,
-    z_landed,
-    stat_sent,
-    stat_landed,
-    gram_sent,
-    gram_landed,
-    square_sent,
-    square_landed,
-):
-    me = lax.axis_index("dp")
-    total = 8 * depth
-    core = lax.rem(me, 2)
-    x_at = lax.rem(me // 2, 2)
-    y_at = lax.rem(me // 4, 2)
-    z_at = me // 8
-    chip = me // 2
-    partner = me + 1 - 2 * core
-    to_x = me + 2 - 4 * x_at
-    to_y = me + 4 - 8 * y_at
-    everyone = [lax.rem(me + step, total) for step in range(1, total)]
-    matrices = stats_ref.shape[0]
-    own_rows = stats_ref.shape[1]
-    segment_rows = segs.shape[2]
-    is_gram = (core == 0) & (chip < matrices)
-    greet(everyone)
-    sends = []
-
-    def place(y_pos, x_pos, c_pos):
-        return ((y_pos * 2 + x_pos) * 2 + c_pos) * depth
-
-    relative = [(y_at, x_at), (y_at, 1 - x_at), (1 - y_at, x_at), (1 - y_at, 1 - x_at)]
-    starts = [place(y_pos, x_pos, core) for y_pos, x_pos in relative]
-    partner_starts = [place(y_pos, x_pos, 1 - core) for y_pos, x_pos in relative]
-    layers = (packet_ref.shape[1] // rows_layer)
-    chunks = [(layer * rows_layer, rows_layer) for layer in reversed(range(layers))]
-    chunks.append((layers * rows_layer, packet_ref.shape[1] - layers * rows_layer))
-    count = len(chunks)
-
-    def first_half(k):
-        return ((chunks[k][1] // 2 + 15) // 16) * 16
-
-    die_copies = {}
-    for k in range(count):
-        lower, size = chunks[k]
-        for rel in (3, 1, 2, 0):
-            copy = push(
-                packet_ref.at[pl.ds(partner_starts[rel], depth), pl.ds(lower, size)],
-                die_buf.at[pl.ds(rel * depth, depth), pl.ds(lower, size)],
-                die_sent.at[k, rel],
-                die_landed.at[k, rel],
-                partner,
-            )
-            die_copies[k, rel] = copy
-            sends.append(copy)
-
-    for matrix in range(matrices):
-        owner = gram_device(matrix)
-
-        @pl.when(me != owner)
-        def _(matrix=matrix, owner=owner):
-            push(stats_ref.at[matrix], stat_buf.at[0, me], stat_sent.at[0, matrix], stat_landed.at[0, me], owner)
-            push(bases_ref.at[matrix], stat_buf.at[1, me], stat_sent.at[1, matrix], stat_landed.at[1, me], owner)
-
-    near = {}
-
-    def pair_sum(rel, z_pos, lower, size):
-        return packet_ref[starts[rel] + z_pos, pl.ds(lower, size), :].astype(FULL) + die_buf[
-            rel * depth + z_pos, pl.ds(lower, size), :
-        ].astype(FULL)
-
-    def stage_one(k):
-        lower, size = chunks[k]
-        half = first_half(k)
-        die_copies[k, 3].wait_recv()
-        for z_pos in range(depth):
-            die_buf[3 * depth + z_pos, pl.ds(lower, size), :] = pair_sum(3, z_pos, lower, size).astype(LOW)
-        for which, (start, length, peer) in enumerate(
-            [(lower, half, to_x), (lower + half, size - half, to_y)]
-        ):
-            copy = push(
-                die_buf.at[pl.ds(3 * depth, depth), pl.ds(start, length)],
-                d_buf.at[:, pl.ds(start, length)],
-                near_sent.at[k, which],
-                near_landed.at[k, which],
-                peer,
-            )
-            near[k, which] = copy
-            sends.append(copy)
-
-    def stage_two(k):
-        lower, size = chunks[k]
-        half = first_half(k)
-        for rel, which, peer, target in ((1, 2, to_x, x_buf), (2, 3, to_y, y_buf)):
-            die_copies[k, rel].wait_recv()
-            near[k, 1 if rel == 1 else 0].wait_recv()
-            first, second = (lower, half), (lower + half, size - half)
-            helped, plain = (second, first) if rel == 1 else (first, second)
-            for z_pos in range(depth):
-                die_buf[rel * depth + z_pos, pl.ds(plain[0], plain[1]), :] = pair_sum(
-                    rel, z_pos, plain[0], plain[1]
-                ).astype(LOW)
-                die_buf[rel * depth + z_pos, pl.ds(helped[0], helped[1]), :] = (
-                    pair_sum(rel, z_pos, helped[0], helped[1])
-                    + d_buf[z_pos, pl.ds(helped[0], helped[1]), :].astype(FULL)
-                ).astype(LOW)
-            copy = push(
-                die_buf.at[pl.ds(rel * depth, depth), pl.ds(lower, size)],
-                target.at[:, pl.ds(lower, size)],
-                near_sent.at[k, which],
-                near_landed.at[k, which],
-                peer,
-            )
-            near[k, which] = copy
-            sends.append(copy)
-
-    z_copies = {}
-
-    def stage_three(k):
-        lower, size = chunks[k]
-        die_copies[k, 0].wait_recv()
-        near[k, 2].wait_recv()
-        near[k, 3].wait_recv()
-        for z_pos in range(depth):
-            die_buf[z_pos, pl.ds(lower, size), :] = (
-                pair_sum(0, z_pos, lower, size)
-                + x_buf[z_pos, pl.ds(lower, size), :].astype(FULL)
-                + y_buf[z_pos, pl.ds(lower, size), :].astype(FULL)
-            ).astype(LOW)
-        for step in range(1, depth):
-            z_to = lax.rem(z_at + step, depth)
-            copy = push(
-                die_buf.at[z_to, pl.ds(lower, size)],
-                z_buf.at[z_at, pl.ds(lower, size)],
-                z_sent.at[k, step],
-                z_landed.at[k, step],
-                lax.rem(me + 8 * step, total),
-            )
-            z_copies[k, step] = copy
-            sends.append(copy)
-
-    def stage_four(k):
-        lower, size = chunks[k]
-        for step in range(1, depth):
-            z_copies[k, step].wait_recv()
-        value = die_buf[z_at, pl.ds(lower, size), :].astype(FULL)
-        for step in range(1, depth):
-            value = value + z_buf[lax.rem(z_at + step, depth), pl.ds(lower, size), :].astype(FULL)
-        own_ref[pl.ds(lower, size), :] = value
-        if k == count - 1:
-            return
-        layer = lower // rows_layer
-        for segment, (low_row, high_row) in enumerate(bounds):
-            piece = value[low_row:high_row].astype(LOW)
-            if high_row - low_row < segment_rows:
-                blank = jnp.zeros((segment_rows - (high_row - low_row), value.shape[1]), LOW)
-                piece = jnp.concatenate([piece, blank], 0)
-            matrix = 4 * layer + segment
-            segs[layer, segment] = piece
-            owner = gram_device(matrix)
-
-            @pl.when(me != owner)
-            def _(matrix=matrix, owner=owner, layer=layer, segment=segment):
-                push(segs.at[layer, segment], gram_buf.at[me], gram_sent.at[matrix], gram_landed.at[me], owner)
-
-    stages = [stage_one, stage_two, stage_three, stage_four]
-    for step in range(count + len(stages) - 1):
-        for at, stage in enumerate(stages):
-            if 0 <= step - at < count:
-                stage(step - at)
-
-    own = own_ref[...]
-    lane8 = lax.broadcasted_iota(jnp.int32, (8, LANES), 1)
-    squares = jnp.sum(own * own) + jnp.sum(jnp.where(lane8 == 2, squares_ref[...], 0.0)) / 8.0
-    square_out[...] = jnp.full((8, LANES), squares)
-    square_all[me] = square_out[...]
-    copies = [
-        push(square_out, square_all.at[me], square_sent.at[at], square_landed.at[at], peer)
-        for at, peer in enumerate(everyone)
-    ]
-    sends.extend(copies)
-    for copy in copies:
-        copy.wait_recv()
-    squares = jnp.sum(square_all[...], 0)
-    norm = jnp.sqrt(squares)
-    norm_ref[...] = norm
-    clip = jnp.minimum(1.0, CLIP_MAX / (norm + 1e-06))[:1, :1]
-
-    @pl.when(is_gram)
-    def _():
-        for matrix in range(matrices):
-
-            @pl.when(matrix == chip)
-            def _(matrix=matrix):
-                gram_buf[me] = segs[matrix // 4, matrix % 4]
-                stat_buf[0, me] = stats_ref[matrix]
-                stat_buf[1, me] = bases_ref[matrix]
-
-        for source in range(total):
-
-            @pl.when(source != me)
-            def _(source=source):
-                for at in range(2):
-                    pltpu.make_async_copy(
-                        stat_buf.at[at, source], stat_buf.at[at, source], stat_landed.at[at, source]
-                    ).wait()
-                pltpu.make_async_copy(gram_buf.at[source], gram_buf.at[source], gram_landed.at[source]).wait()
-
-        rows = gram_buf[...].reshape(total * segment_rows, gram_buf.shape[2])
-        gram = dot_tn(rows, rows)
-        scale = (1.0 - BETA_STAT) * (clip * clip)
-        for source in range(total):
-            next_stats_ref[source] = (
-                BETA_STAT * stat_buf[0, source]
-                + scale * gram[source * own_rows : (source + 1) * own_rows]
-            )
-        basis_ref[...] = stat_buf[1]
-
-    @pl.when(jnp.logical_not(is_gram))
-    def _():
-        next_stats_ref[...] = jnp.zeros(next_stats_ref.shape, FULL)
-        basis_ref[...] = jnp.zeros(basis_ref.shape, FULL)
-
-    for copy in sends:
-        copy.wait_send()
-    for matrix in range(matrices):
-
-        @pl.when(me != gram_device(matrix))
-        def _(matrix=matrix):
-            for at, source in ((0, stats_ref), (1, bases_ref)):
-                pltpu.make_async_copy(source.at[matrix], source.at[matrix], stat_sent.at[at, matrix]).wait()
-            own_segment = segs.at[matrix // 4, matrix % 4]
-            pltpu.make_async_copy(own_segment, own_segment, gram_sent.at[matrix]).wait()
-
-
-def collect(squares, packets, stats, bases, rows_layer, bounds):
-    devices, rows, width = packets.shape
-    depth = devices // 8
-    matrices, own_rows = stats.shape[:2]
-    layers = rows // rows_layer
-    segment_rows = -(-max(high - low for low, high in bounds) // 16) * 16
-    vmem = pl.BlockSpec(memory_space=pltpu.VMEM)
-    shape = jax.ShapeDtypeStruct
-    dma = pltpu.SemaphoreType.DMA
-    count = layers + 1
-    return pl.pallas_call(
-        functools.partial(collect_kernel, depth, rows_layer, bounds),
-        out_shape=(
-            shape((rows, width), FULL),
-            shape((8, LANES), FULL),
-            shape((devices, own_rows, width), FULL),
-            shape((devices, own_rows, width), FULL),
-        ),
-        in_specs=[vmem] * 4,
-        out_specs=(vmem,) * 4,
-        scratch_shapes=[
-            pltpu.VMEM((4 * depth, rows, width), LOW),
-            pltpu.VMEM((depth, rows, width), LOW),
-            pltpu.VMEM((depth, rows, width), LOW),
-            pltpu.VMEM((depth, rows, width), LOW),
-            pltpu.VMEM((depth, rows, width), LOW),
-            pltpu.VMEM((2, devices, own_rows, width), FULL),
-            pltpu.VMEM((8, LANES), FULL),
-            pltpu.VMEM((devices, 8, LANES), FULL),
-            pltpu.VMEM((layers, 4, segment_rows, width), LOW),
-            pltpu.VMEM((devices, segment_rows, width), LOW),
-            dma((count, 4)),
-            dma((count, 4)),
-            dma((count, 4)),
-            dma((count, 4)),
-            dma((count, depth)),
-            dma((count, depth)),
-            dma((2, matrices)),
-            dma((2, devices)),
-            dma((matrices,)),
-            dma((devices,)),
-            dma((devices - 1,)),
-            dma((devices - 1,)),
-        ],
-        compiler_params=params(3, 56 << 20),
-        name="collect",
-    )(squares, packets, stats, bases)
 
 
 def dot_high(left, right, contract):
@@ -1407,43 +1147,6 @@
     return (loss_sum, loss_count, grad_hidden, grad_last, grad_protos, grad_features, next_centre)
 
 
-def pack_small(embedding, teacher_embedding, head_last, teacher_last):
-    def table(value):
-        flat = value.T.astype(LOW).reshape(-1)
-        return jnp.pad(flat, (0, -flat.size % (16 * LANES))).reshape(-1, LANES)
-
-    def last(value):
-        return value.T.astype(LOW).reshape(-1, LANES)
-
-    return jnp.concatenate(
-        [table(embedding), table(teacher_embedding), last(head_last), last(teacher_last)], 0
-    )
-
-
-def unpack_small(everything, embedding, head_last, devices):
-    depth = devices // 8
-    rows, columns = embedding.shape
-    ordered = everything.reshape(2, 2, 2, depth, -1, LANES).transpose(3, 0, 1, 2, 4, 5)
-    ordered = ordered.reshape(devices, -1, LANES)
-    size = rows * columns
-    table_rows = (size + (-size % (16 * LANES))) // LANES
-    last_rows = head_last.size // LANES
-
-    def table(at):
-        flat = ordered[:, at : at + table_rows].reshape(devices, -1)[:, :size]
-        return flat.reshape(devices * columns, rows).T
-
-    def last(at):
-        return ordered[:, at : at + last_rows].reshape(devices * head_last.shape[1], -1)
-
-    return (
-        table(0),
-        table(table_rows),
-        last(2 * table_rows),
-        last(2 * table_rows + last_rows),
-    )
-
-
 def own_feature_rows(features, teacher_features):
     def rows(value):
         count = value.shape[0]
@@ -1465,12 +1168,13 @@
     part,
     last_full,
     teacher_last_full,
+    layer_bases,
     devices,
     device_index,
 ):
     counted = valid_mask.astype(FULL)
     mask_row = jnp.pad(counted, (0, LANES - counted.size)).reshape(1, LANES)
-    scalars, grad_hidden, grad_last, grad_protos, grad_feat, next_centre = head(
+    scalars, grad_hidden, grad_last, grad_protos, grad_feat, next_centre, bases_all = head(
         own_feature_rows(features, teacher_features),
         head_hidden,
         teacher_hidden,
@@ -1482,6 +1186,7 @@
         centre[None],
         counted[:, None],
         mask_row,
+        layer_bases.reshape(-1, D).astype(LOW),
         devices,
     )
     count = features.shape[0]
@@ -1495,38 +1200,1125 @@
         grad_protos,
         grad_features,
         next_centre[0],
-    )
-
-
-def packets_of(grad_table, grad_layers, devices):
+        bases_all,
+    )
+
+
+TOKENS = 272
+HALF_ROW = 256
+SAVED = ("inputs", "normed", "joint", "mixed", "attended", "middle", "normed_two", "activated", "slope", "outer")
+
+
+def saved_widths():
+    return {
+        "inputs": (D, FULL),
+        "normed": (D, LOW),
+        "joint": (3 * D, LOW),
+        "mixed": (D, LOW),
+        "attended": (D, LOW),
+        "middle": (D, FULL),
+        "normed_two": (D, LOW),
+        "activated": (MLP, LOW),
+        "slope": (MLP, LOW),
+        "outer": (D, LOW),
+    }
+
+
+def unpack_blocks(weights, joint_out, output_out, cuts, depth):
+    devices = weights.shape[0]
+    joint_rows, output_rows = cuts[0], cuts[1] - cuts[0]
+    group = 4
+    for at in range(0, devices, group):
+        blocks = [
+            weights[slot_of(at + t, depth), 0 : cuts[1]].astype(FULL) for t in range(group)
+        ]
+        joint = jnp.concatenate([block[:joint_rows] for block in blocks], 0)
+        output = jnp.concatenate([block[joint_rows:] for block in blocks], 0)
+        joint_out[at * joint_rows : (at + group) * joint_rows] = joint.astype(LOW)
+        output_out[at * output_rows : (at + group) * output_rows] = output.astype(LOW)
+
+
+def weight_rows(weights, cuts, which, part, parts):
+    per = weights.shape[0] // parts
+    block = weights[part * per : (part + 1) * per, cuts[which] : cuts[which + 1]]
+    return block.reshape(-1, block.shape[-1])
+
+
+def chance(keys_half, queries, live):
+    scores = jnp.where(live, dot_nt(keys_half, queries), -jnp.inf)
+    grown = jnp.exp(scores - jnp.max(scores, 0, keepdims=True))
+    return grown * (1.0 / jnp.sum(grown, 0, keepdims=True))
+
+
+WIDE_TABLE = 1152
+POSITION_AT = 640
+VECTORS_AT = 1024
+
+
+def table_rows(embedding):
+    turned = embedding.T
+    columns = turned.shape[0]
+    patch = jnp.pad(turned[:, :PIX], ((0, 0), (0, POSITION_AT - PIX)))
+    position = jnp.concatenate([turned[:, PIX + 1 : PIX + SEQ], turned[:, PIX : PIX + 1]], 1)
+    position = jnp.pad(position, ((0, 0), (0, VECTORS_AT - POSITION_AT - SEQ)))
+    layer_rows = turned[:, PIX + SEQ : PIX + SEQ + 6 * LAYERS].reshape(columns, LAYERS, 6)
+    layer_rows = jnp.pad(layer_rows, ((0, 0), (0, 0), (0, 2))).reshape(columns, -1)
+    tail_rows = turned[:, PIX + SEQ + 6 * LAYERS :]
+    joint = jnp.concatenate([patch, position, layer_rows, tail_rows], 1)
+    rows = -(-columns // 16) * 16
+    joint = jnp.pad(joint, ((0, rows - columns), (0, WIDE_TABLE - joint.shape[1]))).astype(LOW)
+    return jnp.concatenate([joint[:, at : at + D] for at in range(0, WIDE_TABLE, D)], 0)
+
+
+PLAN = {
+    "start": ("A0", "A1", "A2", "B0", "B1", "A3", "C0", "B2", "A4", "C1", "D0", "E0", "D1", "B3", "C2", "E1"),
+    0: ("B4", "A5"),
+    "middle": ("C3", "D2", "E2"),
+    1: ("C4", "D3"),
+    2: ("E3", "D4", "B5", "A6"),
+    3: ("E4",),
+    4: ("C5",),
+    5: ("D5", "B6", "A7"),
+    6: ("E5",),
+    7: ("C6",),
+    8: ("D6", "B7", "A8"),
+    9: ("E6",),
+    10: ("C7",),
+    11: ("D7", "B8", "A9"),
+    12: ("E7",),
+    13: ("C8",),
+    14: ("D8", "B9"),
+    15: ("E8",),
+    16: ("C9",),
+    17: ("D9",),
+    "end": ("E9",),
+}
+
+
+def fetch_kernel(
+    cuts,
+    depth,
+    patches_ref,
+    table_ref,
+    teacher_table_ref,
+    layers_ref,
+    teacher_layers_ref,
+    last_ref,
+    columns_ref,
+    feat_ref,
+    final_ref,
+    vectors_out_ref,
+    weights_out_ref,
+    last_out_ref,
+    part_ref,
+    *rest,
+):
+    layer, model, image = (pl.program_id(at) for at in range(3))
+    images = pl.num_programs(2)
+    step = (layer * 2 + model) * images + image
+    outs = dict(zip(SAVED, rest[: len(SAVED)]))
+    (
+        current,
+        joint_weight,
+        output_weight,
+        weights_all,
+        tables,
+        turned,
+        vectors_all,
+        out_sem,
+        part_own,
+        part_sent,
+        part_landed,
+        part_die,
+        *sems,
+    ) = rest[len(SAVED) :]
+    sources = (layers_ref, teacher_layers_ref)
+    rows = layers_ref.shape[1]
+    first = cuts[1]
+
+    def layer_item(which, at, lower, size):
+        return (sources[which].at[at], weights_all.at[which, at], lower, size)
+
+    items = [
+        (table_ref, tables.at[0], 0, table_ref.shape[0]),
+        layer_item(0, 0, 0, first),
+        layer_item(0, 0, first, rows - first),
+        (teacher_table_ref, tables.at[1], 0, table_ref.shape[0]),
+        layer_item(1, 0, 0, rows),
+        layer_item(0, 1, 0, rows),
+        layer_item(1, 1, 0, rows),
+        layer_item(0, 2, 0, rows),
+        layer_item(1, 2, 0, rows),
+        (last_ref, last_out_ref, 0, last_ref.shape[0]),
+    ]
+    route = Route(depth, items, *sems)
+    total = 8 * depth
+    chips = total // 2
+    chip = route.me // 2
+    core = route.core
+
+    def part_copy(at):
+        peer = lax.rem(route.me + 2 * at, total)
+        block = columns_ref.at[:, pl.ds(pl.multiple_of((peer // 2) * LANES, LANES), LANES)]
+        return route.copy(
+            block, part_ref.at[core, chip], part_sent.at[at], part_landed.at[at], peer
+        )
+
+    def part_mine():
+        block = columns_ref.at[:, pl.ds(pl.multiple_of(chip * LANES, LANES), LANES)]
+        return pltpu.make_async_copy(block, part_ref.at[core, chip], part_own.at[0])
+
+    def part_across():
+        return route.copy(
+            part_ref.at[core], part_ref.at[core], part_die.at[0], part_die.at[1], route.partner
+        )
+
+    def out_copy(at):
+        return pltpu.make_async_copy(weights_all.at[0, at], weights_out_ref.at[at], out_sem.at[at])
+
+    def run(name):
+        for word in PLAN[name]:
+            route.act(word[0], int(word[1:]))
+
+    @pl.when(step == 0)
+    def _():
+        greet([lax.rem(route.me + 2 * at, total) for at in range(1, chips)] + [route.partner])
+        run("start")
+
+    def set_up(which):
+        columns = D // total
+        block_rows = table_ref.shape[0] // (WIDE_TABLE // D)
+        group = 4
+        for at in range(0, total, group):
+            for block in range(WIDE_TABLE // D):
+                lower = block * block_rows
+                pieces = [
+                    tables[which, slot_of(at + t, depth), lower : lower + block_rows].astype(FULL)[
+                        :columns
+                    ]
+                    for t in range(group)
+                ]
+                turned[at * columns : (at + group) * columns, block * D : (block + 1) * D] = (
+                    jnp.concatenate(pieces, 0).astype(LOW)
+                )
+        vectors = turned[:, VECTORS_AT:WIDE_TABLE].astype(FULL).T
+        vectors_all[which] = vectors[:32]
+        position = turned[:, POSITION_AT:VECTORS_AT].astype(FULL).T[:TOKENS]
+        row = lax.broadcasted_iota(jnp.int32, (TOKENS, D), 0)
+        tail = 8 * LAYERS
+        extra = jnp.where(
+            row < HALF_ROW,
+            vectors[tail : tail + 1],
+            jnp.where(row == HALF_ROW, vectors[tail + 1 : tail + 2], 0.0),
+        )
+        start = position + extra
+        for at in range(feat_images):
+            current[which, at, :HALF_ROW] = start[:HALF_ROW] + dot_nt(
+                patches_ref[at], turned[:, :PIX]
+            )
+            current[which, at, HALF_ROW:] = start[HALF_ROW:]
+
+    feat_images = patches_ref.shape[0]
+    for at in range(18):
+
+        @pl.when(step == at)
+        def _(at=at):
+            run(at)
+            if at == 0:
+                set_up(0)
+                vectors_out_ref[...] = vectors_all[0]
+            if at == 3:
+                set_up(1)
+            if at == 3:
+                out_copy(0).start()
+            if at == 6:
+                out_copy(1).start()
+            if at == 11:
+                part_mine().start()
+                for other in range(1, chips):
+                    part_copy(other).start()
+            if at == 12:
+                out_copy(2).start()
+            if at == 16:
+                part_mine().wait()
+                for other in range(1, chips):
+                    part_copy(other).wait_recv()
+                part_across().start()
+
+    weights = weights_all.at[model, layer]
+
+    @pl.when(image == 0)
+    def _():
+        unpack_blocks(weights, joint_weight, output_weight, cuts, depth)
+
+    vectors = vectors_all[model, pl.ds(pl.multiple_of(layer * 8, 8), 8), :]
+    lane = lax.broadcasted_iota(jnp.int32, (TOKENS, LANES), 1)
+    live = lax.broadcasted_iota(jnp.int32, (TOKENS, TOKENS), 0) < SEQ
+
+    def attend(save):
+        def keep(name, value):
+            if save:
+                outs[name][0, 0] = value
+
+        inputs = current[model, image]
+        keep("inputs", inputs)
+        normed = layer_norm(inputs, vectors[0:1], vectors[1:2]).astype(LOW)
+        keep("normed", normed)
+        mixed = []
+        for pair in range(D // LANES):
+            lower = pair * LANES
+            parts = [
+                dot_nt(normed, joint_weight[third * D + lower : third * D + lower + LANES])
+                for third in range(3)
+            ]
+            rounded = [part.astype(LOW) for part in parts]
+            if save:
+                for third in range(3):
+                    outs["joint"][0, 0, :, third * D + lower : third * D + lower + LANES] = rounded[
+                        third
+                    ]
+            queries = (rounded[0].astype(FULL) * HEAD_DIM ** (-0.5)).astype(LOW)
+            values = parts[2].T.astype(LOW)
+            turned_heads = []
+            for half in range(2):
+                keys_half = jnp.where(
+                    (lane >= HEAD_DIM) == bool(half), rounded[1].astype(FULL), 0.0
+                ).astype(LOW)
+                share = chance(keys_half, queries, live).astype(LOW)
+                turned_heads.append(dot_nn(values[half * HEAD_DIM : (half + 1) * HEAD_DIM], share))
+            mixed.append(jnp.concatenate(turned_heads, 0).T.astype(LOW))
+        mixed = jnp.concatenate(mixed, 1)
+        keep("mixed", mixed)
+        attended = dot_nt(mixed, output_weight[...])
+        keep("attended", attended.astype(LOW))
+        middle = inputs + vectors[4:5] * attended
+        keep("middle", middle)
+        current[model, image] = middle
+
+    def perceive(save):
+        def keep(name, value):
+            if save:
+                outs[name][0, 0] = value
+
+        middle = current[model, image]
+        normed_two = layer_norm(middle, vectors[2:3], vectors[3:4]).astype(LOW)
+        keep("normed_two", normed_two)
+        outer = jnp.zeros((TOKENS, D), FULL)
+        parts = MLP // D
+        for part in range(parts):
+            inner = dot_nt(normed_two, weight_rows(weights, cuts, 1, part, parts))
+            spread_half = 0.5 * (1.0 + lax.erf(inner * ROOT_HALF))
+            activated = (inner * spread_half).astype(LOW)
+            if save:
+                outs["activated"][0, 0, :, part * D : (part + 1) * D] = activated
+                slope = spread_half + inner * jnp.exp(-0.5 * inner * inner) * DENSITY_SCALE
+                outs["slope"][0, 0, :, part * D : (part + 1) * D] = slope.astype(LOW)
+            outer = outer + dot_nn(activated, weight_rows(weights, cuts, 2, part, parts))
+        keep("outer", outer.astype(LOW))
+        result = middle + vectors[5:6] * outer
+        current[model, image] = result
+        final = result[HALF_ROW : HALF_ROW + 8]
+        final_ref[model, image] = final
+        tail = 8 * LAYERS
+        feat_ref[model, image] = layer_norm(
+            final, vectors_all[model, tail + 2 : tail + 3], vectors_all[model, tail + 3 : tail + 4]
+        )
+
+    @pl.when(model == 0)
+    def _():
+        attend(True)
+
+    @pl.when(model == 1)
+    def _():
+        attend(False)
+
+    @pl.when(step == 0)
+    def _():
+        run("middle")
+
+    @pl.when(model == 0)
+    def _():
+        perceive(True)
+
+    @pl.when(model == 1)
+    def _():
+        perceive(False)
+
+    @pl.when(step == 17)
+    def _():
+        run("end")
+        for at in range(len(items)):
+            route.act("F", at)
+        for at in range(LAYERS):
+            out_copy(at).wait()
+        across = part_across()
+        across.wait_recv()
+        across.wait_send()
+        for other in range(1, chips):
+            part_copy(other).wait_send()
+
+
+def fetch_forward(patches, embedding, teacher_embedding, layers, teacher_layers, head_last, teacher_last, head_hidden, devices):
+    images = patches.shape[0]
     depth = devices // 8
-    layers = grad_layers.shape[0]
-    parts = grad_layers.reshape(layers, devices, -1, D).transpose(1, 0, 2, 3).reshape(devices, -1, D)
-    flat = grad_table.T.reshape(devices, -1)
-    flat = jnp.pad(flat, ((0, 0), (0, -flat.shape[1] % (16 * D)))).reshape(devices, -1, D)
-    joint = jnp.concatenate([parts, flat], 1).astype(LOW)
-    ordered = joint.reshape((depth, 2, 2, 2) + joint.shape[1:]).transpose(1, 2, 3, 0, 4, 5)
-    return ordered.reshape(joint.shape)
+    rows = layers.shape[1]
+    cuts = [lower for lower, upper in layer_bounds(devices)][1:] + [rows]
+    shape = jax.ShapeDtypeStruct
+    vmem = pl.BlockSpec(memory_space=pltpu.VMEM)
+    anywhere = pl.BlockSpec(memory_space=pl.ANY)
+
+    def last_rows(value):
+        return value.T.astype(LOW).reshape(-1, LANES)
+
+    table = table_rows(embedding)
+    last = jnp.concatenate([last_rows(head_last), last_rows(teacher_last)], 0)
+    columns = head_hidden[:, D:].astype(LOW)
+    outs = [shape((2, images, 8, D), FULL)] * 2
+    specs = [vmem] * 2
+    outs += [
+        shape((32, D), FULL),
+        shape((LAYERS, devices, rows, D), LOW),
+        shape((devices,) + last.shape, LOW),
+        shape((2, devices // 2, columns.shape[0], LANES), LOW),
+    ]
+    specs += [vmem, anywhere, anywhere, anywhere]
+    for name in SAVED:
+        width, kind = saved_widths()[name]
+        outs.append(shape((LAYERS, images, TOKENS, width), kind))
+        specs.append(
+            pl.BlockSpec(
+                (1, 1, TOKENS, width),
+                lambda layer, model, image: (layer, jnp.where(model == 0, image, images - 1), 0, 0),
+            )
+        )
+    count = 10
+    dma = pltpu.SemaphoreType.DMA
+    return pl.pallas_call(
+        functools.partial(fetch_kernel, cuts, depth),
+        grid=(LAYERS, 2, images),
+        out_shape=outs,
+        in_specs=[vmem] + [anywhere] * 6,
+        out_specs=specs,
+        scratch_shapes=[
+            pltpu.VMEM((2, images, TOKENS, D), FULL),
+            pltpu.VMEM((3 * D, D), LOW),
+            pltpu.VMEM((D, D), LOW),
+            pltpu.VMEM((2, LAYERS, devices, rows, D), LOW),
+            pltpu.VMEM((2, devices) + table.shape, LOW),
+            pltpu.VMEM((D, WIDE_TABLE), LOW),
+            pltpu.VMEM((2, 32, D), FULL),
+            dma((LAYERS,)),
+            dma((1,)),
+            dma((devices // 2,)),
+            dma((devices // 2,)),
+            dma((2,)),
+        ]
+        + route_sems(count, depth),
+        compiler_params=params(1, 60 << 20),
+        name="fetch_forward",
+    )(
+        patches,
+        table,
+        table_rows(teacher_embedding),
+        layers.astype(LOW),
+        teacher_layers.astype(LOW),
+        last,
+        columns,
+    )
+
+
+def last_tables(last_all, width, devices):
+    ordered = last_all.reshape(8, devices // 8, 2, -1, LANES).transpose(2, 1, 0, 3, 4)
+    return ordered.reshape(2, width, -1)
+
+
+class Reduce:
+    def __init__(self, depth, chunks, sources, buffers, sems):
+        self.depth, self.chunks, self.sources = depth, chunks, sources
+        self.die_buf, self.d_buf, self.x_buf, self.y_buf, self.z_buf = buffers
+        self.die_sent, self.die_landed, self.near_sent, self.near_landed, self.z_sent, self.z_landed = sems
+        me = lax.axis_index("dp")
+        self.me = me
+        self.total = 8 * depth
+        core = lax.rem(me, 2)
+        x_at = lax.rem(me // 2, 2)
+        y_at = lax.rem(me // 4, 2)
+        self.z_at = me // 8
+        self.partner = me + 1 - 2 * core
+        self.to_x = me + 2 - 4 * x_at
+        self.to_y = me + 4 - 8 * y_at
+        places = [(y_at, x_at), (y_at, 1 - x_at), (1 - y_at, x_at), (1 - y_at, 1 - x_at)]
+        self.starts = [((y * 2 + x) * 2 + core) * depth for y, x in places]
+        self.partner_starts = [((y * 2 + x) * 2 + 1 - core) * depth for y, x in places]
+
+    def copy(self, source, target, sent, landed, device):
+        return pltpu.make_async_remote_copy(
+            src_ref=source,
+            dst_ref=target,
+            send_sem=sent,
+            recv_sem=landed,
+            device_id=(device,),
+            device_id_type=MESH,
+        )
+
+    def half(self, k):
+        return ((self.chunks[k][1] // 2 + 15) // 16) * 16
+
+    def die(self, k, rel):
+        lower, size = self.chunks[k]
+        return self.copy(
+            self.sources[k].at[pl.ds(self.partner_starts[rel], self.depth)],
+            self.die_buf.at[pl.ds(rel * self.depth, self.depth), pl.ds(lower, size)],
+            self.die_sent.at[k, rel],
+            self.die_landed.at[k, rel],
+            self.partner,
+        )
+
+    def near(self, k, which):
+        lower, size = self.chunks[k]
+        half = self.half(k)
+        rel, start, length, target, device = [
+            (3, lower, half, self.d_buf, self.to_x),
+            (3, lower + half, size - half, self.d_buf, self.to_y),
+            (1, lower, size, self.x_buf, self.to_x),
+            (2, lower, size, self.y_buf, self.to_y),
+        ][which]
+        return self.copy(
+            self.die_buf.at[pl.ds(rel * self.depth, self.depth), pl.ds(start, length)],
+            target.at[:, pl.ds(start, length)],
+            self.near_sent.at[k, which],
+            self.near_landed.at[k, which],
+            device,
+        )
+
+    def deep(self, k, step):
+        lower, size = self.chunks[k]
+        return self.copy(
+            self.die_buf.at[lax.rem(self.z_at + step, self.depth), pl.ds(lower, size)],
+            self.z_buf.at[self.z_at, pl.ds(lower, size)],
+            self.z_sent.at[k, step],
+            self.z_landed.at[k, step],
+            lax.rem(self.me + 8 * step, self.total),
+        )
+
+    def pair_sum(self, k, rel, z_pos, first, length):
+        lower, size = self.chunks[k]
+        return self.sources[k][
+            self.starts[rel] + z_pos, first - lower : first - lower + length
+        ].astype(FULL) + self.die_buf[rel * self.depth + z_pos, first : first + length].astype(FULL)
+
+    def begin(self, k):
+        for rel in (3, 1, 2, 0):
+            self.die(k, rel).start()
+
+    def one(self, k):
+        lower, size = self.chunks[k]
+        self.die(k, 3).wait_recv()
+        for z_pos in range(self.depth):
+            self.die_buf[3 * self.depth + z_pos, lower : lower + size] = self.pair_sum(
+                k, 3, z_pos, lower, size
+            ).astype(LOW)
+        self.near(k, 0).start()
+        self.near(k, 1).start()
+
+    def two(self, k):
+        lower, size = self.chunks[k]
+        half = self.half(k)
+        first, second = (lower, half), (lower + half, size - half)
+        for rel, which, arrived, helped, plain in ((1, 2, 1, second, first), (2, 3, 0, first, second)):
+            self.die(k, rel).wait_recv()
+            self.near(k, arrived).wait_recv()
+            for z_pos in range(self.depth):
+                at = rel * self.depth + z_pos
+                self.die_buf[at, plain[0] : plain[0] + plain[1]] = self.pair_sum(
+                    k, rel, z_pos, *plain
+                ).astype(LOW)
+                self.die_buf[at, helped[0] : helped[0] + helped[1]] = (
+                    self.pair_sum(k, rel, z_pos, *helped)
+                    + self.d_buf[z_pos, helped[0] : helped[0] + helped[1]].astype(FULL)
+                ).astype(LOW)
+            self.near(k, which).start()
+
+    def three(self, k):
+        lower, size = self.chunks[k]
+        self.die(k, 0).wait_recv()
+        self.near(k, 2).wait_recv()
+        self.near(k, 3).wait_recv()
+        for z_pos in range(self.depth):
+            self.die_buf[z_pos, lower : lower + size] = (
+                self.pair_sum(k, 0, z_pos, lower, size)
+                + self.x_buf[z_pos, lower : lower + size].astype(FULL)
+                + self.y_buf[z_pos, lower : lower + size].astype(FULL)
+            ).astype(LOW)
+        for step in range(1, self.depth):
+            self.deep(k, step).start()
+
+    def four(self, k):
+        lower, size = self.chunks[k]
+        for step in range(1, self.depth):
+            self.deep(k, step).wait_recv()
+        value = self.die_buf[self.z_at, lower : lower + size].astype(FULL)
+        for step in range(1, self.depth):
+            value = value + self.z_buf[
+                lax.rem(self.z_at + step, self.depth), lower : lower + size
+            ].astype(FULL)
+        return value
+
+    def sent(self, k, die_too):
+        if die_too:
+            for rel in range(4):
+                self.die(k, rel).wait_send()
+        for which in range(4):
+            self.near(k, which).wait_send()
+        for step in range(1, self.depth):
+            self.deep(k, step).wait_send()
+
+
+PER_LAYER = ("normed", "mixed", "normed_two", "activated")
+
+
+def backward_kernel(cuts, bounds, depth, *refs):
+    (
+        squares_ref,
+        stats_ref,
+        bases_ref,
+        patches_ref,
+        weights_ref,
+        vectors_ref,
+        final_ref,
+        grad_feat_ref,
+    ) = refs[:8]
+    saved = dict(zip(SAVED, refs[8 : 8 + len(SAVED)]))
+    (
+        own_ref,
+        norm_ref,
+        next_stats_ref,
+        basis_ref,
+        grad_now,
+        joint_weight,
+        output_weight,
+        grad_outer_all,
+        grad_inner_all,
+        grad_attended_all,
+        grad_joint_all,
+        grad_patch,
+        grad_start,
+        grad_rows,
+        packets,
+        table_packet,
+        die_buf,
+        d_buf,
+        x_buf,
+        y_buf,
+        z_buf,
+        stat_buf,
+        square_out,
+        square_all,
+        segs,
+        gram_buf,
+        die_sent,
+        die_landed,
+        near_sent,
+        near_landed,
+        z_sent,
+        z_landed,
+        stat_sent,
+        stat_landed,
+        gram_sent,
+        gram_landed,
+        square_sent,
+        square_landed,
+    ) = refs[8 + len(SAVED) :]
+    step, image = pl.program_id(0), pl.program_id(1)
+    images = final_ref.shape[0]
+    now = step * images + image
+    layer_rows = cuts[3]
+    chunks = [(layer * layer_rows, layer_rows) for layer in reversed(range(LAYERS))]
+    chunks.append((LAYERS * layer_rows, table_packet.shape[1]))
+    count = len(chunks)
+    sources = [packets.at[k % 2] for k in range(LAYERS)] + [table_packet]
+    ring = Reduce(
+        depth,
+        chunks,
+        sources,
+        (die_buf, d_buf, x_buf, y_buf, z_buf),
+        (die_sent, die_landed, near_sent, near_landed, z_sent, z_landed),
+    )
+    me = ring.me
+    total = ring.total
+    core = lax.rem(me, 2)
+    chip = me // 2
+    matrices = stats_ref.shape[0]
+    own_rows = stats_ref.shape[1]
+    segment_rows = segs.shape[2]
+    is_gram = (core == 0) & (chip < matrices)
+    everyone = [lax.rem(me + at, total) for at in range(1, total)]
+
+    def stat_copy(at, matrix):
+        source = (stats_ref, bases_ref)[at]
+        return ring.copy(
+            source.at[matrix],
+            stat_buf.at[at, me],
+            stat_sent.at[at, matrix],
+            stat_landed.at[at, me],
+            gram_device(matrix),
+        )
+
+    def stat_own(at, matrix):
+        source = (stats_ref, bases_ref)[at]
+        return pltpu.make_async_copy(source.at[matrix], stat_buf.at[at, me], stat_landed.at[at, me])
+
+    def gram_copy(matrix):
+        return ring.copy(
+            segs.at[matrix // 4, matrix % 4],
+            gram_buf.at[me],
+            gram_sent.at[matrix],
+            gram_landed.at[me],
+            gram_device(matrix),
+        )
+
+    def finish(k):
+        lower, size = chunks[k]
+        value = ring.four(k)
+        own_ref[lower : lower + size] = value
+        if k == count - 1:
+            return
+        layer = lower // layer_rows
+        for segment, (low_row, high_row) in enumerate(bounds):
+            piece = value[low_row:high_row].astype(LOW)
+            if high_row - low_row < segment_rows:
+                blank = jnp.zeros((segment_rows - (high_row - low_row), value.shape[1]), LOW)
+                piece = jnp.concatenate([piece, blank], 0)
+            matrix = 4 * layer + segment
+            segs[layer, segment] = piece
+
+            @pl.when(me != gram_device(matrix))
+            def _(matrix=matrix):
+                gram_copy(matrix).start()
+
+    @pl.when(now == 0)
+    def _():
+        greet(everyone)
+        for matrix in range(matrices):
+
+            @pl.when(me != gram_device(matrix))
+            def _(matrix=matrix):
+                stat_copy(0, matrix).start()
+                stat_copy(1, matrix).start()
+
+            @pl.when(me == gram_device(matrix))
+            def _(matrix=matrix):
+                stat_own(0, matrix).start()
+                stat_own(1, matrix).start()
+
+        grad_rows[...] = jnp.zeros(grad_rows.shape, FULL)
+        grad_patch[...] = jnp.zeros(grad_patch.shape, FULL)
+        grad_start[...] = jnp.zeros(grad_start.shape, FULL)
+
+    @pl.when(now == images)
+    def _():
+        ring.one(0)
+
+    @pl.when(now == images + 1)
+    def _():
+        ring.two(0)
+
+    @pl.when(now == 2 * images)
+    def _():
+        ring.one(1)
+        ring.three(0)
+
+    @pl.when(now == 2 * images + 1)
+    def _():
+        ring.two(1)
+        finish(0)
+
+    weights = weights_ref.at[0]
+    vectors = vectors_ref[pl.ds(pl.multiple_of((LAYERS - 1 - step) * 8, 8), 8), :]
+    tail = 8 * LAYERS
+
+    @pl.when(image == 0)
+    def _():
+        unpack_blocks(weights, joint_weight, output_weight, cuts, depth)
+
+    @pl.when(step == 0)
+    def _():
+        first = lax.broadcasted_iota(jnp.int32, (8, D), 0) == 0
+        given = jnp.where(first, grad_feat_ref[image], 0.0)
+        grad_class, grad_gain, grad_shift = norm_back(
+            final_ref[image], vectors_ref[tail + 2 : tail + 3], given
+        )
+        grad_rows[tail + 2 : tail + 3] += grad_gain[None]
+        grad_rows[tail + 3 : tail + 4] += grad_shift[None]
+        grad_now[image] = jnp.zeros((TOKENS, D), FULL)
+        grad_now[image, HALF_ROW : HALF_ROW + 8] = jnp.where(first, grad_class, 0.0)
+
+    rows = pl.ds(pl.multiple_of(image * TOKENS, 16), TOKENS)
+    grad_result = grad_now[image]
+    grad_outer = (vectors[5:6] * grad_result).astype(LOW)
+    grad_outer_all[rows, :] = grad_outer
+    grad_scale_two = jnp.sum(grad_result * saved["outer"][0, 0].astype(FULL), 0, keepdims=True)
+    parts = MLP // D
+    grad_normed_two = jnp.zeros((TOKENS, D), FULL)
+    for part in range(parts):
+        columns = slice(part * D, (part + 1) * D)
+        grad_activated = dot_nt(grad_outer, weight_rows(weights, cuts, 2, part, parts))
+        grad_inner = (grad_activated * saved["slope"][0, 0, :, columns].astype(FULL)).astype(LOW)
+        grad_inner_all[rows, columns] = grad_inner
+        grad_normed_two = grad_normed_two + dot_nn(
+            grad_inner, weight_rows(weights, cuts, 1, part, parts)
+        )
+    grad_middle_norm, grad_gain_two, grad_shift_two = norm_back(
+        saved["middle"][0, 0], vectors[2:3], grad_normed_two
+    )
+    grad_middle = grad_result + grad_middle_norm
+    grad_attended = (vectors[4:5] * grad_middle).astype(LOW)
+    grad_attended_all[rows, :] = grad_attended
+    grad_scale_one = jnp.sum(grad_middle * saved["attended"][0, 0].astype(FULL), 0, keepdims=True)
+    grad_mixed = dot_nn(grad_attended, output_weight[...]).astype(LOW)
+    lane = lax.broadcasted_iota(jnp.int32, (TOKENS, LANES), 1)
+    live = lax.broadcasted_iota(jnp.int32, (TOKENS, TOKENS), 0) < SEQ
+    for pair in range(D // LANES):
+        lower = pair * LANES
+        queries, keys_in, values_in = [
+            saved["joint"][0, 0, :, third * D + lower : third * D + lower + LANES]
+            for third in range(3)
+        ]
+        queries = (queries.astype(FULL) * HEAD_DIM ** (-0.5)).astype(LOW)
+        keys_wide = keys_in.astype(FULL)
+        values_wide = values_in.astype(FULL)
+        keys_turned = keys_wide.T.astype(LOW)
+        grad_head = grad_mixed[:, lower : lower + LANES]
+        turned, grad_keys, grad_values = [], [], []
+        for half in range(2):
+            mine = (lane >= HEAD_DIM) == bool(half)
+            share = chance(jnp.where(mine, keys_wide, 0.0).astype(LOW), queries, live)
+            grad_share = dot_nt(jnp.where(mine, values_wide, 0.0).astype(LOW), grad_head)
+            grad_values.append(dot_nn(share.astype(LOW), grad_head))
+            grad_scores = (
+                share * (grad_share - jnp.sum(share * grad_share, 0, keepdims=True))
+            ).astype(LOW)
+            grad_keys.append(dot_nn(grad_scores, queries))
+            turned.append(dot_nn(keys_turned[half * HEAD_DIM : (half + 1) * HEAD_DIM], grad_scores))
+        grad_queries = jnp.concatenate(turned, 0).T * HEAD_DIM ** (-0.5)
+        low_half = lane < HEAD_DIM
+        for third, value in enumerate(
+            (
+                grad_queries,
+                jnp.where(low_half, grad_keys[0], grad_keys[1]),
+                jnp.where(low_half, grad_values[0], grad_values[1]),
+            )
+        ):
+            grad_joint_all[rows, third * D + lower : third * D + lower + LANES] = value.astype(LOW)
+    grad_normed = dot_nn(grad_joint_all[rows, :], joint_weight[...])
+    grad_input_norm, grad_gain_one, grad_shift_one = norm_back(
+        saved["inputs"][0, 0], vectors[0:1], grad_normed
+    )
+    grad_input = grad_middle + grad_input_norm
+    grad_now[image] = grad_input
+    added = jnp.concatenate(
+        [
+            grad_gain_one[None],
+            grad_shift_one[None],
+            grad_gain_two[None],
+            grad_shift_two[None],
+            grad_scale_one,
+            grad_scale_two,
+            jnp.zeros((2, D), FULL),
+        ],
+        0,
+    )
+    grad_rows[pl.ds(pl.multiple_of((LAYERS - 1 - step) * 8, 8), 8), :] += added
+
+    @pl.when(step == LAYERS - 1)
+    def _():
+        grad_patch[:, :PIX] += dot_tn(grad_input[:HALF_ROW].astype(LOW), patches_ref[image])
+        grad_start[:TOKENS] += grad_input
+        grad_rows[tail : tail + 1] += jnp.sum(grad_input[:HALF_ROW], 0, keepdims=True)
+        grad_rows[tail + 1 : tail + 2] += grad_input[HALF_ROW : HALF_ROW + 1]
+
+    def pack(packet):
+        def flat(name):
+            value = saved[name][0]
+            return value.reshape(-1, value.shape[-1])
+
+        per = cuts[0], cuts[1] - cuts[0], cuts[2] - cuts[1], cuts[3] - cuts[2]
+        groups = 4
+        each = total // groups
+        for at in range(groups):
+            first = at * each
+            joint_rows = dot_tn(
+                grad_joint_all[:, first * per[0] : (first + each) * per[0]], flat("normed")
+            )
+            output_rows = dot_tn(
+                grad_attended_all[:, first * per[1] : (first + each) * per[1]], flat("mixed")
+            )
+            inner_rows = dot_tn(
+                grad_inner_all[:, first * per[2] : (first + each) * per[2]], flat("normed_two")
+            ).astype(LOW)
+            outer_rows = dot_tn(
+                saved["activated"][0, :, :, first * per[3] : (first + each) * per[3]].reshape(
+                    -1, each * per[3]
+                ),
+                grad_outer_all[...],
+            ).astype(LOW)
+            for t in range(each):
+                joined_rows = jnp.concatenate(
+                    [
+                        joint_rows[t * per[0] : (t + 1) * per[0]],
+                        output_rows[t * per[1] : (t + 1) * per[1]],
+                    ],
+                    0,
+                )
+                packet[slot_of(first + t, depth), : cuts[1]] = joined_rows.astype(LOW)
+                packet[first + t, cuts[1] : cuts[2]] = inner_rows[t * per[2] : (t + 1) * per[2]]
+                packet[first + t, cuts[2] : cuts[3]] = outer_rows[t * per[3] : (t + 1) * per[3]]
+
+    @pl.when((image == images - 1) & (step == LAYERS - 1))
+    def _():
+        ring.three(1)
+        for rel in range(4):
+            ring.die(0, rel).wait_send()
+
+    @pl.when(image == images - 1)
+    def _():
+        pack(packets.at[lax.rem(step, 2)])
+
+    for k in range(LAYERS - 1):
+
+        @pl.when((image == images - 1) & (step == k))
+        def _(k=k):
+            ring.begin(k)
+
+    @pl.when((image == images - 1) & (step == LAYERS - 1))
+    def _():
+        last, table = LAYERS - 1, LAYERS
+        ring.begin(last)
+        ring.one(last)
+        blank = jnp.zeros((LANES - 32, D), FULL)
+        turned_rows = jnp.concatenate([grad_rows[...], blank], 0).T
+        turned = [grad_patch[:, :D], None, None]
+        turned_start = grad_start[...].T
+        left = VECTORS_AT - POSITION_AT
+        turned[1] = jnp.concatenate([grad_patch[:, D:], turned_start[:, : 2 * D - POSITION_AT]], 1)
+        turned[2] = jnp.concatenate([turned_start[:, 2 * D - POSITION_AT : left], turned_rows], 1)
+        columns = D // total
+        for block in range(3):
+            for device in range(total):
+                piece = turned[block][device * columns : (device + 1) * columns]
+                piece = jnp.concatenate([piece, jnp.zeros((16 - columns, D), FULL)], 0)
+                table_packet[slot_of(device, depth), 16 * block : 16 * block + 16] = piece.astype(LOW)
+        ring.begin(table)
+        ring.one(table)
+        ring.two(last)
+        finish(1)
+        ring.two(table)
+        ring.three(last)
+        ring.three(table)
+        finish(last)
+        finish(table)
+
+        own = own_ref[...]
+        lane8 = lax.broadcasted_iota(jnp.int32, (8, LANES), 1)
+        squares = jnp.sum(own * own) + jnp.sum(jnp.where(lane8 == 2, squares_ref[...], 0.0)) / 8.0
+        square_out[...] = jnp.full((8, LANES), squares)
+        square_all[me] = square_out[...]
+        copies = [
+            push(square_out, square_all.at[me], square_sent.at[at], square_landed.at[at], peer)
+            for at, peer in enumerate(everyone)
+        ]
+
+        @pl.when(is_gram)
+        def _():
+            for matrix in range(matrices):
+
+                @pl.when(matrix == chip)
+                def _(matrix=matrix):
+                    gram_buf[me] = segs[matrix // 4, matrix % 4]
+
+            for source in range(total):
+                for at in range(2):
+                    view = stat_buf.at[at, source]
+                    pltpu.make_async_copy(view, view, stat_landed.at[at, source]).wait()
+
+                @pl.when(source != me)
+                def _(source=source):
+                    pltpu.make_async_copy(
+                        gram_buf.at[source], gram_buf.at[source], gram_landed.at[source]
+                    ).wait()
+
+            basis_ref[...] = stat_buf[1]
+            blocks = gram_buf[...].reshape(total * segment_rows, gram_buf.shape[2])
+            gram = dot_tn(blocks, blocks)
+            for source in range(total):
+                next_stats_ref[source] = gram[source * own_rows : (source + 1) * own_rows]
+
+        @pl.when(jnp.logical_not(is_gram))
+        def _():
+            next_stats_ref[...] = jnp.zeros(next_stats_ref.shape, FULL)
+            basis_ref[...] = jnp.zeros(basis_ref.shape, FULL)
+            stat_buf[0] = jnp.zeros(stat_buf.shape[1:], FULL)
+
+        for copy in copies:
+            copy.wait_recv()
+        norm = jnp.sqrt(jnp.sum(square_all[...], 0))
+        norm_ref[...] = norm
+        clip = jnp.minimum(1.0, CLIP_MAX / (norm + 1e-06))[:1, :1]
+        scale = (1.0 - BETA_STAT) * (clip * clip)
+        for source in range(total):
+            next_stats_ref[source] = BETA_STAT * stat_buf[0, source] + scale * next_stats_ref[source]
+
+        for copy in copies:
+            copy.wait_send()
+        for k in range(count):
+            ring.sent(k, k != 0)
+        for matrix in range(matrices):
+
+            @pl.when(me != gram_device(matrix))
+            def _(matrix=matrix):
+                stat_copy(0, matrix).wait_send()
+                stat_copy(1, matrix).wait_send()
+                gram_copy(matrix).wait_send()
+
+
+def backward(
+    squares, patches, vectors, blocks, final, grad_feat, saved, stats, bases, devices
+):
+    images = patches.shape[0]
+    depth = devices // 8
+    bounds = layer_bounds(devices)
+    layer_rows = blocks.shape[2]
+    cuts = [lower for lower, upper in bounds][1:] + [layer_rows]
+    matrices, own_rows = stats.shape[:2]
+    segment_rows = -(-max(high - low for low, high in bounds) // 16) * 16
+    table_size = 3 * (-(-(D // devices) // 16) * 16)
+    rows = LAYERS * layer_rows + table_size
+    shape = jax.ShapeDtypeStruct
+    dma = pltpu.SemaphoreType.DMA
+    vmem = pl.BlockSpec(memory_space=pltpu.VMEM)
+    anywhere = pl.BlockSpec(memory_space=pl.ANY)
+
+    def of_layer(*dims):
+        return pl.BlockSpec(
+            (1,) + dims, lambda step, image: (LAYERS - 1 - step,) + (0,) * len(dims)
+        )
+
+    def of_saved(name):
+        width = saved_widths()[name][0]
+        if name in PER_LAYER:
+            return of_layer(images, TOKENS, width)
+        return pl.BlockSpec(
+            (1, 1, TOKENS, width), lambda step, image: (LAYERS - 1 - step, image, 0, 0)
+        )
+
+    all_rows = images * TOKENS
+    count = LAYERS + 1
+    return pl.pallas_call(
+        functools.partial(backward_kernel, cuts, bounds, depth),
+        grid=(LAYERS, images),
+        out_shape=(
+            shape((rows, D), FULL),
+            shape((8, LANES), FULL),
+            shape((devices, own_rows, D), FULL),
+            shape((devices, own_rows, D), FULL),
+        ),
+        in_specs=[
+            vmem,
+            anywhere,
+            anywhere,
+            vmem,
+            of_layer(*blocks.shape[1:]),
+            vmem,
+            vmem,
+            vmem,
+        ]
+        + [of_saved(name) for name in SAVED],
+        out_specs=(vmem,) * 4,
+        scratch_shapes=[
+            pltpu.VMEM((images, TOKENS, D), FULL),
+            pltpu.VMEM((3 * D, D), LOW),
+            pltpu.VMEM((D, D), LOW),
+            pltpu.VMEM((all_rows, D), LOW),
+            pltpu.VMEM((all_rows, MLP), LOW),
+            pltpu.VMEM((all_rows, D), LOW),
+            pltpu.VMEM((all_rows, 3 * D), LOW),
+            pltpu.VMEM((D, POSITION_AT), FULL),
+            pltpu.VMEM((D, D), FULL),
+            pltpu.VMEM((32, D), FULL),
+            pltpu.VMEM((2, devices, layer_rows, D), LOW),
+            pltpu.VMEM((devices, table_size, D), LOW),
+            pltpu.VMEM((4 * depth, rows, D), LOW),
+            pltpu.VMEM((depth, rows, D), LOW),
+            pltpu.VMEM((depth, rows, D), LOW),
+            pltpu.VMEM((depth, rows, D), LOW),
+            pltpu.VMEM((depth, rows, D), LOW),
+            pltpu.VMEM((2, devices, own_rows, D), FULL),
+            pltpu.VMEM((8, LANES), FULL),
+            pltpu.VMEM((devices, 8, LANES), FULL),
+            pltpu.VMEM((LAYERS, 4, segment_rows, D), LOW),
+            pltpu.VMEM((devices, segment_rows, D), LOW),
+            dma((count, 4)),
+            dma((count, 4)),
+            dma((count, 4)),
+            dma((count, 4)),
+            dma((count, depth)),
+            dma((count, depth)),
+            dma((2, matrices)),
+            dma((2, devices)),
+            dma((matrices,)),
+            dma((devices,)),
+            dma((devices - 1,)),
+            dma((devices - 1,)),
+        ],
+        compiler_params=params(3, 63 << 20),
+        name="backward",
+    )(squares, stats, bases, patches, blocks, vectors, final, grad_feat, *saved)
+
+
+def own_table(rows, columns):
+    joint = rows.reshape(3, -1, D)[:, :columns].transpose(1, 0, 2).reshape(columns, -1)
+    position = joint[:, POSITION_AT : POSITION_AT + SEQ]
+    layer_rows = joint[:, VECTORS_AT : VECTORS_AT + 8 * LAYERS].reshape(columns, LAYERS, 8)
+    return jnp.concatenate(
+        [
+            joint[:, :PIX],
+            position[:, SEQ - 1 :],
+            position[:, : SEQ - 1],
+            layer_rows[:, :, :6].reshape(columns, -1),
+            joint[:, VECTORS_AT + 8 * LAYERS : VECTORS_AT + 8 * LAYERS + 4],
+        ],
+        1,
+    ).T
 
 
 def tail_fast(
-    squares, grad_table, grad_layers, layer_stats, layer_bases, owners, embedding, layers, devices
+    gathered,
+    layer_stats,
+    layer_bases,
+    owners,
+    embedding,
+    layers,
+    layers_first,
+    layers_second,
+    teacher_layers,
+    bases_all,
+    devices,
 ):
+    own, norm, full_stats, full_bases = gathered
     own_rows = layer_stats.shape[2]
     matrices = owners.shape[0]
-    rows_layer = layers.shape[1]
-    own, norm, full_stats, full_bases = collect(
-        squares,
-        packets_of(grad_table, grad_layers, devices),
-        layer_stats.reshape(matrices, own_rows, D),
-        layer_bases.reshape(matrices, own_rows, D),
-        rows_layer,
+    count = layers.shape[0] * layers.shape[1]
+    layer_outs = soap(
+        norm,
+        own[:count],
+        bases_all,
+        layers,
+        layers_first,
+        layers_second,
+        teacher_layers,
         layer_bounds(devices),
     )
-    count = layers.shape[0] * rows_layer
-    grad_layers_own = own[:count].reshape(layers.shape)
-    rows, columns = embedding.shape
-    grad_embed = own[count:].reshape(-1)[: rows * columns].reshape(columns, rows).T
+    grad_embed = own_table(own[count:], embedding.shape[1])
     renewed = renew_own(full_stats, full_bases)
     stats_own, bases_own = deal(full_stats, renewed, matrices)
     bases_own = jnp.where(
@@ -1535,10 +2327,98 @@
     return (
         norm[0, 0],
         grad_embed,
-        grad_layers_own,
+        layer_outs,
         stats_own.reshape(layer_stats.shape),
         bases_own.reshape(layer_bases.shape),
     )
+
+
+def split_dot(left, basis, contract):
+    high = left.astype(LOW)
+    rest = (left - high.astype(FULL)).astype(LOW)
+    dims = (contract, ((), ()))
+    return lax.dot_general(high, basis, dims, preferred_element_type=FULL) + lax.dot_general(
+        rest, basis, dims, preferred_element_type=FULL
+    )
+
+
+def soap_kernel(
+    bounds,
+    depth,
+    norm_ref,
+    grads_ref,
+    bases_ref,
+    weights_ref,
+    first_ref,
+    second_ref,
+    teacher_ref,
+    first_out_ref,
+    second_out_ref,
+    weights_out_ref,
+    teacher_out_ref,
+    basis,
+):
+    layer = pl.program_id(0)
+    devices = bases_ref.shape[0]
+    own_rows = bases_ref.shape[1] // 4
+    clip = jnp.minimum(1.0, CLIP_MAX / (norm_ref[0:1, 0:1] + 1e-06))
+    grads = grads_ref[...] * clip
+    group = 4
+    firsts, seconds, updates = [], [], []
+    for segment, (low_row, high_row) in enumerate(bounds):
+        for at in range(0, devices, group):
+            pieces = [
+                bases_ref[slot_of(at + t, depth)][segment * own_rows : (segment + 1) * own_rows]
+                for t in range(group)
+            ]
+            basis[at * own_rows : (at + group) * own_rows] = jnp.concatenate(
+                [piece.astype(FULL) for piece in pieces], 0
+            ).astype(LOW)
+        rotated = split_dot(grads[low_row:high_row], basis[...], ((1,), (0,)))
+        first_new = BETA_ONE * first_ref[0, low_row:high_row] + (1.0 - BETA_ONE) * rotated
+        second_new = (
+            BETA_TWO * second_ref[0, low_row:high_row] + (1.0 - BETA_TWO) * rotated * rotated
+        )
+        direction = (
+            first_new
+            / (1.0 - BETA_ONE**STEP)
+            / (jnp.sqrt(second_new / (1.0 - BETA_TWO**STEP)) + ADAM_EPSILON)
+        )
+        firsts.append(first_new)
+        seconds.append(second_new)
+        updates.append(split_dot(direction, basis[...], ((1,), (1,))))
+    first_out_ref[0] = jnp.concatenate(firsts, 0)
+    second_out_ref[0] = jnp.concatenate(seconds, 0)
+    weight = weights_ref[0]
+    fresh = weight - RATE_MATRIX * (jnp.concatenate(updates, 0) + WEIGHT_DECAY * weight)
+    weights_out_ref[0] = fresh
+    teacher_out_ref[0] = follow(teacher_ref[0], fresh)
+
+
+def soap(norm, grads, bases_all, weights, first, second, teacher, bounds):
+    devices = bases_all.shape[0]
+    rows = weights.shape[1]
+    own_rows = bases_all.shape[1] // LAYERS
+    vmem = pl.BlockSpec(memory_space=pltpu.VMEM)
+    block = pl.BlockSpec((1, rows, D), lambda layer: (layer, 0, 0))
+    return pl.pallas_call(
+        functools.partial(soap_kernel, bounds, devices // 8),
+        grid=(LAYERS,),
+        out_shape=[jax.ShapeDtypeStruct(weights.shape, FULL)] * 4,
+        in_specs=[
+            vmem,
+            pl.BlockSpec((rows, D), lambda layer: (layer, 0)),
+            pl.BlockSpec((devices, own_rows, D), lambda layer: (0, layer, 0)),
+            block,
+            block,
+            block,
+            block,
+        ],
+        out_specs=[block] * 4,
+        scratch_shapes=[pltpu.VMEM((D, D), LOW)],
+        compiler_params=pltpu.CompilerParams(vmem_limit_bytes=32 << 20),
+        name="soap",
+    )(norm, grads, bases_all, weights, first, second, teacher)
 
 
 def per_device(
@@ -1572,35 +2452,44 @@
     devices = lax.axis_size("dp")
     device_index = lax.axis_index("dp")
     fast = 2 * head_hidden.shape[0] == LANES
-    if fast:
-        small, part = spread(
-            pack_small(embedding, teacher_embedding, head_last, teacher_last),
-            head_hidden[:, D:].astype(LOW),
-            devices,
-        )
-        embed_table, teacher_table, last_full, teacher_last_full = unpack_small(
-            small, embedding, head_last, devices
-        )
-    else:
+    if not fast:
         embed_table, teacher_table = (
             lax.all_gather(embedding.astype(LOW), "dp", axis=1, tiled=True),
             lax.all_gather(teacher_embedding.astype(LOW), "dp", axis=1, tiled=True),
         )
-    layer_full, teacher_full = (
-        lax.all_gather(layers.astype(LOW), "dp", axis=1, tiled=True),
-        lax.all_gather(teacher_layers.astype(LOW), "dp", axis=1, tiled=True),
-    )
-    bases_full = lax.all_gather(layer_bases.astype(LOW), "dp", axis=2, tiled=True).astype(
-        layer_bases.dtype
-    )
+        layer_full, teacher_full = (
+            lax.all_gather(layers.astype(LOW), "dp", axis=1, tiled=True),
+            lax.all_gather(teacher_layers.astype(LOW), "dp", axis=1, tiled=True),
+        )
     if not fast:
+        bases_full = lax.all_gather(layer_bases.astype(LOW), "dp", axis=2, tiled=True).astype(
+            layer_bases.dtype
+        )
         stats_full = lax.all_gather(layer_stats.astype(LOW), "dp", axis=2, tiled=True).astype(
             layer_stats.dtype
         )
-    features, layer_inputs, final_state = backbone(patches, embed_table, layer_full, devices)
-    teacher_features, unused_inputs, unused_final = backbone(
-        patches, teacher_table, teacher_full, devices
-    )
+    if fast:
+        feature_rows, final_rows, vectors, layer_full, last_all, part, *saved = fetch_forward(
+            patches,
+            embedding,
+            teacher_embedding,
+            layers,
+            teacher_layers,
+            head_last,
+            teacher_last,
+            head_hidden,
+            devices,
+        )
+        features = feature_rows[0, :, 0].astype(LOW)
+        teacher_features = feature_rows[1, :, 0].astype(LOW)
+        last_full, teacher_last_full = last_tables(
+            last_all, head_last.shape[1] * devices, devices
+        )
+    else:
+        features, layer_inputs, final_state = backbone(patches, embed_table, layer_full, devices)
+        teacher_features, unused_inputs, unused_final = backbone(
+            patches, teacher_table, teacher_full, devices
+        )
     if fast:
         (
             loss_sum,
@@ -1611,6 +2500,7 @@
             grad_protos,
             grad_features,
             next_centre,
+            bases_all,
         ) = head_fast(
             features,
             teacher_features,
@@ -1623,6 +2513,7 @@
             part,
             last_full,
             teacher_last_full,
+            layer_bases,
             devices,
             device_index,
         )
@@ -1648,27 +2539,45 @@
             centre,
             device_index,
         )
-    grad_table, grad_layers = backbone_back(
-        patches,
-        embed_table,
-        layer_full,
-        layer_inputs,
-        final_state,
-        grad_features,
-        devices,
-        unchanged,
-    )
+    if fast:
+        grad_rows = jnp.pad(grad_features[:, None], ((0, 0), (0, 7), (0, 0)))
+        matrices, own_rows = owners.shape[0], layer_stats.shape[2]
+        gathered = backward(
+            squares,
+            patches,
+            vectors,
+            layer_full,
+            final_rows[0],
+            grad_rows,
+            saved,
+            layer_stats.reshape(matrices, own_rows, D),
+            layer_bases.reshape(matrices, own_rows, D),
+            devices,
+        )
+    else:
+        grad_table, grad_layers = backbone_back(
+            patches,
+            embed_table,
+            layer_full,
+            layer_inputs,
+            final_state,
+            grad_features,
+            devices,
+            unchanged,
+        )
     bounds = layer_bounds(devices)
     if fast:
-        grad_norm, grad_embed, grad_layers_own, stats_own, bases_own = tail_fast(
-            squares,
-            grad_table,
-            grad_layers,
+        grad_norm, grad_embed, layer_outs, stats_own, bases_own = tail_fast(
+            gathered,
             layer_stats,
             layer_bases,
             owners,
             embedding,
             layers,
+            layers_first,
+            layers_second,
+            teacher_layers,
+            bases_all,
             devices,
         )
     else:
@@ -1727,27 +2636,32 @@
     protos_out = adam_step(
         protos, clip_factor * grad_protos, protos_first, protos_second, RATE_MATRIX, WEIGHT_DECAY
     )
-    firsts, seconds, weights_new = ([], [], [])
-    for segment, (lower_row, upper_row) in enumerate(bounds):
-        basis = bases_full[:, segment]
-        weight_block = layers[:, lower_row:upper_row]
-        rotated = matmul_high(
-            "lcd,ldk->lck", clip_factor * grad_layers_own[:, lower_row:upper_row], basis
-        )
-        first_new = BETA_ONE * layers_first[:, lower_row:upper_row] + (1.0 - BETA_ONE) * rotated
-        second_new = (
-            BETA_TWO * layers_second[:, lower_row:upper_row] + (1.0 - BETA_TWO) * rotated * rotated
-        )
-        direction = (
-            first_new
-            / (1.0 - BETA_ONE**STEP)
-            / (jnp.sqrt(second_new / (1.0 - BETA_TWO**STEP)) + ADAM_EPSILON)
-        )
-        update = matmul_high("lck,ldk->lcd", direction, basis)
-        firsts.append(first_new)
-        seconds.append(second_new)
-        weights_new.append(weight_block - RATE_MATRIX * (update + WEIGHT_DECAY * weight_block))
-    next_layers = jnp.concatenate(weights_new, 1)
+    if fast:
+        next_layers_first, next_layers_second, next_layers, next_teacher_layers = layer_outs
+    else:
+        firsts, seconds, weights_new = ([], [], [])
+        for segment, (lower_row, upper_row) in enumerate(bounds):
+            basis = bases_full[:, segment]
+            weight_block = layers[:, lower_row:upper_row]
+            rotated = matmul_high(
+                "lcd,ldk->lck", clip_factor * grad_layers_own[:, lower_row:upper_row], basis
+            )
+            first_new = BETA_ONE * layers_first[:, lower_row:upper_row] + (1.0 - BETA_ONE) * rotated
+            second_new = (
+                BETA_TWO * layers_second[:, lower_row:upper_row] + (1.0 - BETA_TWO) * rotated * rotated
+            )
+            direction = (
+                first_new
+                / (1.0 - BETA_ONE**STEP)
+                / (jnp.sqrt(second_new / (1.0 - BETA_TWO**STEP)) + ADAM_EPSILON)
+            )
+            update = matmul_high("lck,ldk->lcd", direction, basis)
+            firsts.append(first_new)
+            seconds.append(second_new)
+            weights_new.append(weight_block - RATE_MATRIX * (update + WEIGHT_DECAY * weight_block))
+        next_layers = jnp.concatenate(weights_new, 1)
+        next_layers_first, next_layers_second = jnp.concatenate(firsts, 1), jnp.concatenate(seconds, 1)
+        next_teacher_layers = follow(teacher_layers, next_layers)
     if not fast:
         flat_stats = next_stats.reshape(-1, D, D)
         flat_bases = bases_full.reshape(-1, D, D)
@@ -1769,8 +2683,8 @@
         embed_out[0],
         embed_out[1],
         embed_out[2],
-        jnp.concatenate(firsts, 1),
-        jnp.concatenate(seconds, 1),
+        next_layers_first,
+        next_layers_second,
         next_layers,
         stats_own,
         bases_own,
@@ -1784,7 +2698,7 @@
         protos_out[1],
         protos_out[2],
         follow(teacher_embedding, embed_out[2]),
-        follow(teacher_layers, next_layers),
+        next_teacher_layers,
         follow(teacher_hidden, hidden_out[2]),
         follow(teacher_last, last_out[2]),
         follow(teacher_protos, protos_out[2]),

time: 1070 us -> 516 us (0.48)
  matrix products: 231 us -> 0 us
  Pallas kernels: 282 us -> 461 us
  local copies, waits for them, and re-layouts: 195 us -> 24.2 us
  other arithmetic: 189 us -> 19 us
  waiting for transfers between devices: 138 us -> 0 us
  between operations: 18.6 us -> 2.1 us
    dot_general x80 -> x0, matrix products: 231 us -> none  [the longest x72 217 us: matmul_low(): return jnp.einsum(form, left, right, preferred_element_type=jnp.float32)]
    pallas_call x2 -> x3, Pallas kernels: 133 us -> 299 us  [the longest x1 159 us: fetch_forward(): pl.pallas_call(functools.partial(fetch_kernel, cuts, depth), grid=(LAYERS...]
    all_gather x3 -> x0, waiting for transfers between devices: 138 us -> none  [the longest x1 73.7 us: per_device(): lax.all_gather(layers.astype(LOW), 'dp', axis=1, tiled=True)]
    reduce_sum x38 -> x0, other arithmetic: 83.7 us -> none  [the longest x7 46.7 us: norm_back(): jnp.sum(grad_out * normed, leading)]
    slice x33 -> x24, local copies, waits for them, and re-layouts: 54.8 us -> 2.13 us  [the longest x1 0.73 us: fetch_forward(): columns = head_hidden[:, D:].astype(LOW)]
    convert_element_type x33 -> x5, other arithmetic: 36.2 us -> 1.58 us  [the longest x1 0.76 us: fetch_forward(): teacher_layers.astype(LOW)]
    sub x6 -> x0, other arithmetic: 33 us -> none  [layer_parts(): attention = jax.nn.softmax(scores, axis=-1)]
    unnamed x569 -> x74, local copies, waits for them, and re-layouts: 41 us -> 10.5 us
  transfers between devices with their start and end apart: 3 -> 0, of which waited for: 2 -> 0; matrix products, arithmetic and copies ran while one was open for 6% -> 0% of each run, Pallas kernels for 4% -> 0%
where the time goes in v3:
time: 516 us; the launch traced here: 507 us
  Pallas kernels  461 us (89%)
  local copies, waits for them, and re-layouts  24.2 us (5%)
  other arithmetic  19 us (4%)
    pallas_call x1, Pallas kernels, fetch_forward(): pl.pallas_call(functools.partial(fetch_kernel, cuts, depth), grid=(LAYERS...  159 us
    pallas_call x1, Pallas kernels, backward(): pl.pallas_call(functools.partial(backward_kernel, cuts, bounds, depth), g...  133 us
    pallas_call x1, Pallas kernels, head(): pl.pallas_call(functools.partial(head_kernel, devices), out_shape=(shape(...  92.9 us
    pallas_call x1, Pallas kernels, renew_own(): pl.pallas_call(renew_kernel, out_shape=jax.ShapeDtypeStruct(stats.shape,...  39.5 us
    pallas_call x1, Pallas kernels, deal(): pl.pallas_call(functools.partial(deal_kernel, devices), out_shape=(jax.Sh...  30.2 us
    add x4, other arithmetic, follow(): TEACHER_MOMENTUM * teacher_weight  12.6 us
    unnamed x74, local copies, waits for them, and re-layouts  10.5 us

profile of v3, /device:TPU:31, one launch (start us, length us, event | category | flops | bytes accessed | tf_op | source)
XLA Modules:
  0.0 506.8 jit_solution(17653595508241547339)
XLA Ops:
  0.7 0.9 bitcast_convert_fusion
  2.2 0.8 fusion.6
  3.1 0.8 bitcast_convert_fusion.1
  5.2 2.3 copy.97.patches_ref.refs_3_
  10.5 159.1 %fetch_forward.1 = (f32[2,3,8,384]{3,2,1,0:T(8,128)}, f32[2,3,8,384]{3,2,1,0:T(8,128)}, f32[32,384]{1,0:T(8,128)}, bf16[3,32,144,384]{3,2,1,0:T(8,128)(2,1)}, bf...) custom-call(bf16[3,256,588]{2,1,0:T(8,128)(2,1)} %copy.97.patches_re, ...), custom_call_target="tpu_custom_call" | custom-call | tf_op jit(solution)/shard_map/fetch_forward/pallas_call | solution.py:1596
  169.6 0.9 convert.56
  170.6 1.8 copy.115
  172.4 1.6 fusion.25
  174.0 1.7 unstack.13.last_ref
  175.7 1.5 unstack.15.teacher_last_ref
  177.6 1.1 copy-done.7
  178.6 1.0 copy-done.14
  179.7 92.9 %head.1 = (f32[8,128]{1,0:T(8,128)S(1)}, f32[64,2432]{1,0:T(8,128)S(1)}, f32[8,2048]{1,0:T(8,128)S(1)}, f32[256,2048]{1,0:T(8,128)}, f32[8,384]{1,0:T(8,128)S(1)...) custom-call(bf16[32,128]{1,0:T(8,128)(2,1)S(1)} %fusion.16.feat_ref, f32[64,2432]{1,0:T(8,128)S(1)} %copy-done, ...), custom_call_target="tpu_custom_call" | custom-call | tf_op jit(solution)/shard_map/head/pallas_call | solution.py:833
  272.6 0.8 copy-done.12
  276.0 1.7 copy.103
  277.7 133.1 %backward.1 = (f32[480,384]{1,0:T(8,128)}, f32[8,128]{1,0:T(8,128)}, f32[32,12,384]{2,1,0:T(8,128)}, f32[32,12,384]{2,1,0:T(8,128)}) custom-call(f32[8,128]{1,0:T(8,128)} %copy-done.16, f32[12,12,384]{2,1,0:T(8,128)} %bitcast.76, f32[12,12,384]{2,1,0:T(8,128)} %bitcast.69, bf16[3,256,588]{2,1,0:T(8,128)(2,1)} %copy.97.patches_ref.refs_3_, ...), custom_call_target="tpu_custom_call" | custom-call | tf_op jit(solution)/shard_map/backward/pallas_call | solution.py:2216
  410.8 1.2 slice.136
  412.7 9.2 %multiply_add_fusion = (f32[256,2048]{1,0:T(8,128)}, f32[256,2048]{1,0:T(8,128)}, f32[256,2048]{1,0:T(8,128)}, f32[256,2048]{1,0:T(8,128)}) fusion(f32[256,2048]{1,0:T(8,128)} %teacher_protos_ref.1, f32[256,2048]{1,0:T(8,128)} %protos_ref.1, f32[256,2048]{1,0:T(8,128)} %get-tuple-element.89, f32[]{:T(128)S(6)} %min_shard_map.3, f32[256,2048]{1,0:T(8,128)} %param.45, ...), kind=kLoop, calls=%fused_computation.3 | loop fusion | flops 9961472 | bytes 18874372 | tf_op jit(solution)/shard_map/add | solution.py:327
  422.8 1.9 multiply_add_fusion.2
  424.7 39.5 %renew.1.bases_ref = f32[32,12,384]{2,1,0:T(8,128)S(1)} custom-call(f32[32,12,384]{2,1,0:T(8,128)S(1)} %copy-done.2, f32[32,12,384]{2,1,0:T(8,128)S(1)} %copy-done.9), custom_call_target="tpu_custom_call" | custom-call | tf_op jit(solution)/shard_map/renew/pallas_call | solution.py:979
  464.2 30.2 %deal.1 = (f32[12,12,384]{2,1,0:T(8,128)S(1)}, f32[12,12,384]{2,1,0:T(8,128)S(1)}) custom-call(f32[32,12,384]{2,1,0:T(8,128)S(1)} %copy-done.2, f32[32,12,384]{2,1,0:T(8,128)S(1)} %renew.1.bases_ref), custom_call_target="tpu_custom_call" | custom-call | tf_op jit(solution)/shard_map/deal/pallas_call | solution.py:1033
  494.6 0.8 copy.113
  496.2 6.7 %soap.1 = (f32[3,144,384]{2,1,0:T(8,128)}, f32[3,144,384]{2,1,0:T(8,128)}, f32[3,144,384]{2,1,0:T(8,128)}, f32[3,144,384]{2,1,0:T(8,128)}) custom-call(f32[8,128]{1,0:T(8,128)S(1)} %copy-done.17, f32[432,384]{1,0:T(8,128)S(1)} %slice.145.grads_ref, bf16[32,144,384]{2,1,0:T(8,128)(2,1)S(1)} %copy-done.1, f32[3,144,384]{2,1,0:T(8,128)S(1)} %copy-done.4, ...), custom_call_target="tpu_custom_call" | custom-call | tf_op jit(solution)/shard_map/soap/pallas_call | solution.py:2404
  504.7 1.3 fusion.26
  (138 shorter events, 11.8 us)
Async XLA Ops:
  0.7 6.8 %copy-start.3 = (f32[3,144,384]{2,1,0:T(8,128)S(1)}, f32[3,144,384]{2,1,0:T(8,128)}, u32[]{:S(2)}) copy-start(f32[3,144,384]{2,1,0:T(8,128)} %weights_ref.1) | copy-start | bytes 1990660
  0.7 7.6 %copy-start.5 = (f32[3,144,384]{2,1,0:T(8,128)S(1)}, f32[3,144,384]{2,1,0:T(8,128)}, u32[]{:S(2)}) copy-start(f32[3,144,384]{2,1,0:T(8,128)} %teacher_ref.1) | copy-start | bytes 1990660
  4.5 4.6 copy-start
  5.2 4.5 copy-start.26
  5.2 4.6 copy-start.25
  174.0 3.3 copy-start.32
  174.0 3.4 copy-start.19
  174.0 3.5 copy-start.15
  179.7 95.0 %copy-start.31 = (f32[2,3,8,384]{3,2,1,0:T(8,128)S(1)}, f32[2,3,8,384]{3,2,1,0:T(8,128)}, u32[]{:S(2)}) copy-start(f32[2,3,8,384]{3,2,1,0:T(8,128)} %get-tuple-element.65) | copy-start | bytes 221188
  412.7 9.3 %copy-start.27 = (f32[2048,8]{0,1:T(8,128)S(1)}, f32[2048,8]{0,1:T(8,128)}, u32[]{:S(2)}) copy-start(f32[2048,8]{0,1:T(8,128)} %param.42) | copy-start | bytes 196612
  412.7 9.3 %copy-start.28 = (f32[2048,8]{0,1:T(8,128)S(1)}, f32[2048,8]{0,1:T(8,128)}, u32[]{:S(2)}) copy-start(f32[2048,8]{0,1:T(8,128)} %param.41) | copy-start | bytes 196612
  412.7 10.0 %copy-start.8 = (f32[64,2432]{1,0:T(8,128)S(1)}, f32[64,2432]{1,0:T(8,128)}, u32[]{:S(2)}) copy-start(f32[64,2432]{1,0:T(8,128)} %teacher_hidden_ref.1) | copy-start | bytes 1867780
  412.7 10.0 %copy-start.13 = (f32[64,2432]{1,0:T(8,128)S(1)}, f32[64,2432]{1,0:T(8,128)}, u32[]{:S(2)}) copy-start(f32[64,2432]{1,0:T(8,128)} %copy-done.12) | copy-start | bytes 1867780
  412.7 10.0 %copy-start.21 = (f32[64,2432]{1,0:T(8,128)S(1)}, f32[64,2432]{1,0:T(8,128)}, u32[]{:S(2)}) copy-start(f32[64,2432]{1,0:T(8,128)} %param.39) | copy-start | bytes 1867780
  412.7 10.0 %copy-start.22 = (f32[64,2432]{1,0:T(8,128)S(1)}, f32[64,2432]{1,0:T(8,128)}, u32[]{:S(2)}) copy-start(f32[64,2432]{1,0:T(8,128)} %param.38) | copy-start | bytes 1867780
  422.8 73.4 %copy-start.20 = (f32[480,384]{1,0:T(8,128)S(1)}, f32[480,384]{1,0:T(8,128)}, u32[]{:S(2)}) copy-start(f32[480,384]{1,0:T(8,128)} %get-tuple-element.78) | copy-start | bytes 2211844
  424.6 69.8 %copy-start.33 = (s32[12]{0:T(128)S(1)}, s32[12]{0:T(128)}, u32[]{:S(2)}) copy-start(s32[12]{0:T(128)} %param.28) | copy-start | bytes 148
  424.6 69.8 %copy-start.18 = (f32[3,4,12,384]{3,2,1,0:T(8,128)S(1)}, f32[3,4,12,384]{3,2,1,0:T(8,128)}, u32[]{:S(2)}) copy-start(f32[3,4,12,384]{3,2,1,0:T(8,128)} %copy.104) | copy-start | bytes 663556
  424.7 71.5 %copy-start.6 = (f32[3,144,384]{2,1,0:T(8,128)S(1)}, f32[3,144,384]{2,1,0:T(8,128)}, u32[]{:S(2)}) copy-start(f32[3,144,384]{2,1,0:T(8,128)} %teacher_ref.1) | copy-start | bytes 1990660
  424.7 71.5 %copy-start.10 = (f32[3,144,384]{2,1,0:T(8,128)S(1)}, f32[3,144,384]{2,1,0:T(8,128)}, u32[]{:S(2)}) copy-start(f32[3,144,384]{2,1,0:T(8,128)} %first_ref.1) | copy-start | bytes 1990660
  424.7 71.5 %copy-start.11 = (f32[3,144,384]{2,1,0:T(8,128)S(1)}, f32[3,144,384]{2,1,0:T(8,128)}, u32[]{:S(2)}) copy-start(f32[3,144,384]{2,1,0:T(8,128)} %second_ref.1) | copy-start | bytes 1990660
  464.2 32.0 %copy-start.1 = (bf16[32,144,384]{2,1,0:T(8,128)(2,1)S(1)}, bf16[32,144,384]{2,1,0:T(8,128)(2,1)}, u32[]{:S(2)}) copy-start(bf16[32,144,384]{2,1,0:T(8,128)(2,1)} %get-tuple-element.79.bases_ref) | copy-start | bytes 10616836
  464.2 32.0 %copy-start.4 = (f32[3,144,384]{2,1,0:T(8,128)S(1)}, f32[3,144,384]{2,1,0:T(8,128)}, u32[]{:S(2)}) copy-start(f32[3,144,384]{2,1,0:T(8,128)} %weights_ref.1) | copy-start | bytes 1990660
  464.2 32.0 %copy-start.17 = (f32[8,128]{1,0:T(8,128)S(1)}, f32[8,128]{1,0:T(8,128)}, u32[]{:S(2)}) copy-start(f32[8,128]{1,0:T(8,128)} %get-tuple-element.77.norm_ref) | copy-start | bytes 12292
  (10 other events, 11.4 us)

commit v4 on v3

--- a/solution.py
+++ b/solution.py
@@ -7,6 +7,7 @@
 from jax.experimental.pallas import tpu as pltpu
 from jax.sharding import PartitionSpec as P
 
+AXIS = "dp"
 D = 384
 HEADS = 6
 HEAD_DIM = 64
@@ -380,7 +381,7 @@
         self.depth = depth
         self.items = items
         self.sems = (own_sem, z_sent, z_landed, near_sent, near_landed, die_sent, die_landed)
-        me = lax.axis_index("dp")
+        me = lax.axis_index(AXIS)
         self.me = me
         self.total = 8 * depth
         self.core = lax.rem(me, 2)
@@ -445,29 +446,29 @@
         )
 
     def act(self, stage, at):
-        if stage == "A":
+        if stage == 0:
             self.own(at).start()
             for step in range(1, self.depth):
                 self.deep(at, step).start()
-        elif stage == "B":
+        elif stage == 1:
             self.own(at).wait()
             for step in range(1, self.depth):
                 self.deep(at, step).wait_recv()
             self.near(at, 0).start()
             self.near(at, 1).start()
             self.die(at, 0).start()
-        elif stage == "C":
+        elif stage == 2:
             self.near(at, 0).wait_recv()
             self.near(at, 2).start()
             self.die(at, 1).start()
             self.near(at, 1).wait_recv()
             self.near(at, 3).start()
             self.die(at, 2).start()
-        elif stage == "D":
+        elif stage == 3:
             self.near(at, 2).wait_recv()
             self.near(at, 3).wait_recv()
             self.die(at, 3).start()
-        elif stage == "E":
+        elif stage == 4:
             for column in range(4):
                 self.die(at, column).wait_recv()
         else:
@@ -553,7 +554,7 @@
     core_landed,
     *sems,
 ):
-    me = lax.axis_index("dp")
+    me = lax.axis_index(AXIS)
     core = lax.rem(me, 2)
     chip = me // 2
     chips = devices // 2
@@ -570,7 +571,7 @@
 
     def beside(*words):
         for word in words:
-            route.act(word[0], int(word[1:]))
+            route.act(*word)
 
     sends = []
 
@@ -609,7 +610,7 @@
     lead = row_at - 3 * col_dev
     for copy in copies:
         copy.wait_recv()
-    beside("A0")
+    beside((0, 0))
     rows_all = fb[...].reshape(devices * block_rows, LANES)
 
     def features_of(model):
@@ -646,13 +647,13 @@
     pre1[...] = pre_one
     tpre_one = dot_nt(tfeats, thid_low[:, :D])
     gather_pair(0, gelu_exact(pre_one).astype(LOW).astype(FULL), gelu_exact(tpre_one).astype(LOW).astype(FULL), act_s, act_t)
-    beside("B0", "A1")
+    beside((1, 0), (0, 1))
     pre_two = dot_nt(act_s[...], hid_low[:, D:])
     pre2[...] = pre_two
     tpre_two = dot_nt(act_t[...], thid_low[:, D:])
     gather_pair(1, gelu_exact(pre_two).astype(LOW).astype(FULL), gelu_exact(tpre_two).astype(LOW).astype(FULL), act2_s, act2_t)
 
-    beside("C0", "B1", "A2")
+    beside((2, 0), (1, 1), (0, 2))
     unit, inverse_norm = unit_rows(dot_nt(act2_s[...], last_ref[...]))
     tunit, unused = unit_rows(dot_nt(act2_t[...], teacher_last_ref[...]))
     unit_ref[...] = unit
@@ -685,7 +686,7 @@
     )
     for copy in copies:
         copy.wait_recv()
-    beside("D0", "C1", "B2")
+    beside((3, 0), (2, 1), (1, 2))
     merged = stat_all[...]
     tops, totals = merged[:, 0], merged[:, 1]
     ttops, ttotals, crosses = merged[:, 2], merged[:, 3], merged[:, 4]
@@ -744,7 +745,7 @@
         def _(group=group):
             pltpu.make_async_copy(dz_all.at[group], dz_all.at[group], wide_landed.at[3, group]).wait()
 
-    beside("E0", "D1", "C2")
+    beside((4, 0), (3, 1), (2, 2))
     grad_bottle = dz_all[...].reshape(images, unit.shape[1]).astype(LOW)
     chip_columns = pl.ds(pl.multiple_of(chip * LANES, LANES), LANES)
     pair = dot_nn(grad_bottle, last_ref[:, chip_columns])
@@ -778,7 +779,7 @@
     copy.wait_recv()
     for at in range(chips):
         dp_full[their_rows, at * LANES : (at + 1) * LANES] = dp_half[1, at]
-    beside("E1", "D2")
+    beside((4, 1), (3, 2))
     part = jnp.concatenate([part_ref[at % 2, at // 2] for at in range(devices)], 0)
     pair = dot_nn(dp_full[...], part)
     grad_act_one = jnp.where(core == 0, pair[:, :units], pair[:, units:])
@@ -801,7 +802,7 @@
     copy.wait_recv()
     whole = df_sum[...] + df_other[...]
     grad_feat_ref[...] = whole
-    beside("E2", "F0", "F1", "F2")
+    beside((4, 2), (5, 0), (5, 1), (5, 2))
     squares = jnp.sum(grad_hidden_ref[...] * grad_hidden_ref[...])
     squares = squares + jnp.sum(grad_last_ref[...] * grad_last_ref[...])
     squares = squares + jnp.sum(grad_protos_ref[...] * grad_protos_ref[...])
@@ -907,138 +908,214 @@
 def inverse_factor(block):
     size = block.shape[0]
     tiles = size // 8
+    wide = 8
     sub = lax.broadcasted_iota(jnp.int32, (8, size), 0)
     lane = lax.broadcasted_iota(jnp.int32, (8, size), 1)
     rest = [block[8 * t : 8 * t + 8] for t in range(tiles)]
     made = [jnp.where(lane == sub + 8 * t, 1.0, 0.0) for t in range(tiles)]
-    for k in range(size):
+
+    def full(value):
+        return jnp.broadcast_to(value, (8, size))
+
+    for k in range(0, size, wide):
         tile, row = k // 8, k % 8
-        pivot = rest[tile][row : row + 1]
-        scale = lax.rsqrt(pivot[:, k : k + 1])
-        factor_row = pivot * scale
-        made_row = made[tile][row : row + 1] * scale
+        factor_rows = [full(rest[tile][row + i : row + i + 1]) for i in range(wide)]
+        made_rows = [full(made[tile][row + i : row + i + 1]) for i in range(wide)]
+        entry = [
+            [full(rest[tile][row + i : row + i + 1, k + j : k + j + 1]) for j in range(i + 1)]
+            for i in range(wide)
+        ]
+        columns = [
+            [full(rest[t][:, k + j : k + j + 1]) for j in range(wide)] for t in range(tile, tiles)
+        ]
+        for j in range(wide):
+            scale = lax.rsqrt(entry[j][j])
+            factor_rows[j] = factor_rows[j] * scale
+            made_rows[j] = made_rows[j] * scale
+            for i in range(j + 1, wide):
+                entry[i][j] = entry[i][j] * scale
+            for some in columns:
+                some[j] = some[j] * scale
+            for i in range(j + 1, wide):
+                factor_rows[i] = factor_rows[i] - entry[i][j] * factor_rows[j]
+                made_rows[i] = made_rows[i] - entry[i][j] * made_rows[j]
+                for e in range(j + 1, i + 1):
+                    entry[i][e] = entry[i][e] - entry[i][j] * entry[e][j]
+                for some in columns:
+                    some[i] = some[i] - entry[i][j] * some[j]
         for t in range(tile, tiles):
-            column = rest[t][:, k : k + 1] * scale
+            some = columns[t - tile]
             if t == tile:
-                column = jnp.where(sub[:, :1] > row, column, 0.0)
-            rest[t] = rest[t] - column * factor_row
-            made[t] = made[t] - column * made_row
+                some = [jnp.where(sub >= row + wide, column, 0.0) for column in some]
+            for j in range(wide):
+                rest[t] = rest[t] - some[j] * factor_rows[j]
+                made[t] = made[t] - some[j] * made_rows[j]
             if t == tile:
-                made[t] = jnp.where(sub == row, made_row, made[t])
+                for j in range(wide):
+                    made[t] = jnp.where(sub == row + j, made_rows[j], made[t])
     return jnp.concatenate(made, 0)
 
 
-def renew_kernel(stats_ref, basis_ref, out_ref, stat, base, gram, work, done):
+def renew_kernel(
+    devices,
+    stats_ref,
+    basis_ref,
+    own_stats_ref,
+    own_bases_ref,
+    stat,
+    base,
+    gram,
+    work,
+    done,
+    given,
+    taken,
+    passed,
+    sent,
+    landed,
+    die_sent,
+    die_landed,
+):
+    me = lax.axis_index(AXIS)
+    core = lax.rem(me, 2)
+    chip = me // 2
+    chips = devices // 2
+    partner = me + 1 - 2 * core
     parts, rows = stats_ref.shape[:2]
     size = parts * rows
     blocks = size // LANES
-    for part in range(parts):
-        stat[part * rows : (part + 1) * rows] = stats_ref[part]
-        base[part * rows : (part + 1) * rows] = basis_ref[part]
-    at_row = lax.broadcasted_iota(jnp.int32, (size, size), 0)
-    at_col = lax.broadcasted_iota(jnp.int32, (size, size), 1)
-    trace = jnp.sum(jnp.where(at_row == at_col, stat[...], 0.0), axis=(0, 1), keepdims=True)
-    scaled = dot_high(stat[...], base[...], ((1,), (0,))) * (size / trace)
-    product = dot_high(scaled, scaled, ((0,), (0,)))
-    for b in range(blocks):
-        work[b] = scaled[:, b * LANES : (b + 1) * LANES]
-        for c in range(blocks):
-            gram[b, c] = product[b * LANES : (b + 1) * LANES, c * LANES : (c + 1) * LANES]
-
-    def step(b, carried):
-        inverse = inverse_factor(gram[b, b])
-        made = dot_high(work[b], inverse, ((1,), (1,)))
-        done[b] = made
-
-        def trail(c, inner):
-            panel = dot_high(inverse, gram[b, c], ((1,), (0,)))
-            work[c] = work[c] - dot_high(made, panel, ((1,), (0,)))
-
-            def against(e, innermost):
-                other = dot_high(inverse, gram[b, e], ((1,), (0,)))
-                gram[c, e] = gram[c, e] - dot_high(panel, other, ((0,), (0,)))
-                return innermost
-
-            lax.fori_loop(c, blocks, against, 0)
-            return inner
-
-        lax.fori_loop(b + 1, blocks, trail, 0)
-        return carried
-
-    lax.fori_loop(0, blocks, step, 0)
-    whole = jnp.concatenate([done[b] for b in range(blocks)], 1)
-    for part in range(parts):
-        out_ref[part] = whole[part * rows : (part + 1) * rows]
-
-
-def renew_own(stats, basis):
+    matrices = own_stats_ref.shape[0]
+    is_gram = (core == 0) & (chip < matrices)
+    spare = given.shape[3] - rows
+    greet([lax.rem(me + 2 * at, devices) for at in range(1, chips)] + [partner])
+
+    def out_copy(kind, at):
+        peer = lax.rem(me + 2 * at, devices)
+        return pltpu.make_async_remote_copy(
+            src_ref=given.at[kind, peer // 2],
+            dst_ref=taken.at[kind, chip],
+            send_sem=sent.at[kind, at],
+            recv_sem=landed.at[kind, chip],
+            device_id=(peer,),
+            device_id_type=MESH,
+        )
+
+    def across(kind):
+        return pltpu.make_async_remote_copy(
+            src_ref=taken.at[kind, :, 1],
+            dst_ref=passed.at[kind],
+            send_sem=die_sent.at[kind],
+            recv_sem=die_landed.at[kind],
+            device_id=(partner,),
+            device_id_type=MESH,
+        )
+
+    def hand_out(kind, row_of):
+        blank = jnp.zeros((spare, size), FULL)
+        for part in range(parts):
+            given[kind, part // 2, part % 2] = jnp.concatenate([row_of(part), blank], 0).astype(LOW)
+        taken[kind, chip] = given[kind, chip]
+        for at in range(1, chips):
+            out_copy(kind, at).start()
+
+    @pl.when(is_gram)
+    def _():
+        hand_out(0, lambda part: stats_ref[part])
+        for part in range(parts):
+            stat[part * rows : (part + 1) * rows] = stats_ref[part]
+            base[part * rows : (part + 1) * rows] = basis_ref[part]
+        at_row = lax.broadcasted_iota(jnp.int32, (size, size), 0)
+        at_col = lax.broadcasted_iota(jnp.int32, (size, size), 1)
+        trace = jnp.sum(jnp.where(at_row == at_col, stat[...], 0.0), axis=(0, 1), keepdims=True)
+        scaled = dot_high(stat[...], base[...], ((1,), (0,))) * (size / trace)
+        product = dot_high(scaled, scaled, ((0,), (0,)))
+        for b in range(blocks):
+            work[b] = scaled[:, b * LANES : (b + 1) * LANES]
+            for c in range(blocks):
+                gram[b, c] = product[b * LANES : (b + 1) * LANES, c * LANES : (c + 1) * LANES]
+
+        def step(b, carried):
+            inverse = inverse_factor(gram[b, b])
+            made = dot_high(work[b], inverse, ((1,), (1,)))
+            done[b] = made
+
+            def trail(c, inner):
+                panel = dot_high(inverse, gram[b, c], ((1,), (0,)))
+                work[c] = work[c] - dot_high(made, panel, ((1,), (0,)))
+
+                def against(e, innermost):
+                    other = dot_high(inverse, gram[b, e], ((1,), (0,)))
+                    gram[c, e] = gram[c, e] - dot_high(panel, other, ((0,), (0,)))
+                    return innermost
+
+                lax.fori_loop(c, blocks, against, 0)
+                return inner
+
+            lax.fori_loop(b + 1, blocks, trail, 0)
+            return carried
+
+        lax.fori_loop(0, blocks, step, 0)
+        whole = jnp.concatenate([done[b] for b in range(blocks)], 1)
+        hand_out(1, lambda part: whole[part * rows : (part + 1) * rows])
+
+    @pl.when(core == 0)
+    def _():
+        for kind in range(2):
+            for matrix in range(matrices):
+
+                @pl.when(chip != matrix)
+                def _(kind=kind, matrix=matrix):
+                    view = taken.at[kind, matrix]
+                    pltpu.make_async_copy(view, view, landed.at[kind, matrix]).wait()
+
+            across(kind).start()
+        own_stats_ref[...] = taken[0, :, 0, :rows].astype(FULL)
+        own_bases_ref[...] = taken[1, :, 0, :rows].astype(FULL)
+        for kind in range(2):
+            across(kind).wait_send()
+
+    @pl.when(core == 1)
+    def _():
+        for kind in range(2):
+            across(kind).wait_recv()
+        own_stats_ref[...] = passed[0, :, :rows].astype(FULL)
+        own_bases_ref[...] = passed[1, :, :rows].astype(FULL)
+
+    @pl.when(is_gram)
+    def _():
+        for kind in range(2):
+            for at in range(1, chips):
+                out_copy(kind, at).wait_send()
+
+
+def renew_own(stats, basis, matrices):
     devices, rows, width = stats.shape
     size = devices * rows
     blocks = size // LANES
+    padded = -(-rows // 16) * 16
     vmem = pl.BlockSpec(memory_space=pltpu.VMEM)
+    dma = pltpu.SemaphoreType.DMA
     return pl.pallas_call(
-        renew_kernel,
-        out_shape=jax.ShapeDtypeStruct(stats.shape, FULL),
+        functools.partial(renew_kernel, devices),
+        out_shape=(jax.ShapeDtypeStruct((matrices, rows, width), FULL),) * 2,
         in_specs=[vmem] * 2,
-        out_specs=vmem,
+        out_specs=(vmem,) * 2,
         scratch_shapes=[
             pltpu.VMEM((size, width), FULL),
             pltpu.VMEM((size, width), FULL),
             pltpu.VMEM((blocks, blocks, LANES, LANES), FULL),
             pltpu.VMEM((blocks, size, LANES), FULL),
             pltpu.VMEM((blocks, size, LANES), FULL),
+            pltpu.VMEM((2, devices // 2, 2, padded, width), LOW),
+            pltpu.VMEM((2, matrices, 2, padded, width), LOW),
+            pltpu.VMEM((2, matrices, padded, width), LOW),
+            dma((2, devices // 2)),
+            dma((2, matrices)),
+            dma((2,)),
+            dma((2,)),
         ],
-        compiler_params=pltpu.CompilerParams(vmem_limit_bytes=32 << 20),
+        compiler_params=params(4, 40 << 20),
         name="renew",
     )(stats, basis)
-
-
-def deal_kernel(devices, stats_ref, bases_ref, own_stats_ref, own_bases_ref, sent, landed):
-    me = lax.axis_index("dp")
-    core = lax.rem(me, 2)
-    chip = me // 2
-    matrices = own_stats_ref.shape[0]
-    is_gram = (core == 0) & (chip < matrices)
-    greet([lax.rem(me + step, devices) for step in range(1, devices)])
-
-    @pl.when(is_gram)
-    def _():
-        for step in range(1, devices):
-            peer = lax.rem(me + step, devices)
-            push(bases_ref.at[peer], own_bases_ref.at[chip], sent.at[1, step], landed.at[1, chip], peer)
-        for step in range(1, devices):
-            peer = lax.rem(me + step, devices)
-            push(stats_ref.at[peer], own_stats_ref.at[chip], sent.at[0, step], landed.at[0, chip], peer)
-        own_stats_ref[chip] = stats_ref[me]
-        own_bases_ref[chip] = bases_ref[me]
-
-    for matrix in range(matrices):
-
-        @pl.when(me != gram_device(matrix))
-        def _(matrix=matrix):
-            for at, target in ((0, own_stats_ref), (1, own_bases_ref)):
-                pltpu.make_async_copy(target.at[matrix], target.at[matrix], landed.at[at, matrix]).wait()
-
-    @pl.when(is_gram)
-    def _():
-        for step in range(1, devices):
-            for at, source in ((0, stats_ref), (1, bases_ref)):
-                pltpu.make_async_copy(source.at[0], source.at[0], sent.at[at, step]).wait()
-
-
-def deal(stats, bases, matrices):
-    devices, rows, width = stats.shape
-    vmem = pl.BlockSpec(memory_space=pltpu.VMEM)
-    dma = pltpu.SemaphoreType.DMA
-    return pl.pallas_call(
-        functools.partial(deal_kernel, devices),
-        out_shape=(jax.ShapeDtypeStruct((matrices, rows, width), FULL),) * 2,
-        in_specs=[vmem] * 2,
-        out_specs=(vmem,) * 2,
-        scratch_shapes=[dma((2, devices)), dma((2, matrices))],
-        compiler_params=params(4),
-        name="deal",
-    )(stats, bases)
 
 
 def head_slow(
@@ -1055,8 +1132,8 @@
     device_index,
 ):
     all_features, all_teacher = (
-        lax.all_gather(features, "dp", axis=0, tiled=True),
-        lax.all_gather(teacher_features, "dp", axis=0, tiled=True),
+        lax.all_gather(features, AXIS, axis=0, tiled=True),
+        lax.all_gather(teacher_features, AXIS, axis=0, tiled=True),
     )
     first_weight = head_hidden[:, :D].astype(jnp.bfloat16)
     second_weight = head_hidden[:, D:].astype(jnp.bfloat16)
@@ -1067,20 +1144,20 @@
     pre_one = matmul_low("bd,hd->bh", all_features, first_weight)
     teacher_pre_one = matmul_low("bd,hd->bh", all_teacher, teacher_first)
     act_one = (
-        lax.all_gather(gelu_exact(pre_one).astype(jnp.bfloat16), "dp", axis=1, tiled=True),
-        lax.all_gather(gelu_exact(teacher_pre_one).astype(jnp.bfloat16), "dp", axis=1, tiled=True),
+        lax.all_gather(gelu_exact(pre_one).astype(jnp.bfloat16), AXIS, axis=1, tiled=True),
+        lax.all_gather(gelu_exact(teacher_pre_one).astype(jnp.bfloat16), AXIS, axis=1, tiled=True),
     )
     pre_two = matmul_low("bh,kh->bk", act_one[0], second_weight)
     teacher_pre_two = matmul_low("bh,kh->bk", act_one[1], teacher_second)
     act_two = (
-        lax.all_gather(gelu_exact(pre_two).astype(jnp.bfloat16), "dp", axis=1, tiled=True),
-        lax.all_gather(gelu_exact(teacher_pre_two).astype(jnp.bfloat16), "dp", axis=1, tiled=True),
+        lax.all_gather(gelu_exact(pre_two).astype(jnp.bfloat16), AXIS, axis=1, tiled=True),
+        lax.all_gather(gelu_exact(teacher_pre_two).astype(jnp.bfloat16), AXIS, axis=1, tiled=True),
     )
     bottles = (
-        lax.all_gather(matmul_low("bh,hc->bc", act_two[0], last_weight), "dp", axis=1, tiled=True),
+        lax.all_gather(matmul_low("bh,hc->bc", act_two[0], last_weight), AXIS, axis=1, tiled=True),
         lax.all_gather(
             matmul_low("bh,hc->bc", act_two[1], teacher_last.astype(jnp.bfloat16)),
-            "dp",
+            AXIS,
             axis=1,
             tiled=True,
         ),
@@ -1106,7 +1183,7 @@
             jnp.sum(teacher_exp, -1),
             jnp.sum(teacher_exp * scaled, -1),
         ),
-        "dp",
+        AXIS,
         combine_parts,
     )
     log_total = merged[0] + jnp.log(merged[1])
@@ -1119,7 +1196,7 @@
         (counted / loss_count)[:, None] * (student_prob - teacher_prob) / TAU_STUDENT
     ).astype(jnp.bfloat16)
     grad_protos = matmul_low("bc,bp->cp", unit_low, grad_logits)
-    grad_unit = lax.psum(matmul_low("bp,cp->bc", grad_logits, proto_weight), "dp")
+    grad_unit = lax.psum(matmul_low("bp,cp->bc", grad_logits, proto_weight), AXIS)
     grad_bottle = inverse_norm * (grad_unit - unit * jnp.sum(unit * grad_unit, -1, keepdims=True))
     last_width = head_last.shape[1]
     grad_bottle_own = lax.dynamic_slice_in_dim(
@@ -1127,17 +1204,17 @@
     ).astype(jnp.bfloat16)
     grad_last = matmul_low("bh,bc->hc", act_two[0], grad_bottle_own)
     grad_act_two = lax.psum_scatter(
-        matmul_low("bc,hc->bh", grad_bottle_own, last_weight), "dp", scatter_dimension=1, tiled=True
+        matmul_low("bc,hc->bh", grad_bottle_own, last_weight), AXIS, scatter_dimension=1, tiled=True
     )
     grad_pre_two = (grad_act_two * gelu_slope(pre_two)).astype(jnp.bfloat16)
     grad_second = matmul_low("bk,bh->kh", grad_pre_two, act_one[0])
     grad_act_one = lax.psum_scatter(
-        matmul_low("bk,kh->bh", grad_pre_two, second_weight), "dp", scatter_dimension=1, tiled=True
+        matmul_low("bk,kh->bh", grad_pre_two, second_weight), AXIS, scatter_dimension=1, tiled=True
     )
     grad_pre_one = (grad_act_one * gelu_slope(pre_one)).astype(jnp.bfloat16)
     grad_first = matmul_low("bh,bd->hd", grad_pre_one, all_features)
     grad_features = lax.psum_scatter(
-        matmul_low("bh,hd->bd", grad_pre_one, first_weight), "dp", scatter_dimension=0, tiled=True
+        matmul_low("bh,hd->bd", grad_pre_one, first_weight), AXIS, scatter_dimension=0, tiled=True
     )
     grad_hidden = jnp.concatenate([grad_first, grad_second], 1)
     next_centre = (
@@ -1271,27 +1348,27 @@
 
 
 PLAN = {
-    "start": ("A0", "A1", "A2", "B0", "B1", "A3", "C0", "B2", "A4", "C1", "D0", "E0", "D1", "B3", "C2", "E1"),
-    0: ("B4", "A5"),
-    "middle": ("C3", "D2", "E2"),
-    1: ("C4", "D3"),
-    2: ("E3", "D4", "B5", "A6"),
-    3: ("E4",),
-    4: ("C5",),
-    5: ("D5", "B6", "A7"),
-    6: ("E5",),
-    7: ("C6",),
-    8: ("D6", "B7", "A8"),
-    9: ("E6",),
-    10: ("C7",),
-    11: ("D7", "B8", "A9"),
-    12: ("E7",),
-    13: ("C8",),
-    14: ("D8", "B9"),
-    15: ("E8",),
-    16: ("C9",),
-    17: ("D9",),
-    "end": ("E9",),
+    -1: ((0, 0), (0, 1), (0, 2), (1, 0), (1, 1), (0, 3), (2, 0), (1, 2), (0, 4), (2, 1), (3, 0), (4, 0), (3, 1), (1, 3), (2, 2), (4, 1)),
+    0: ((1, 4), (0, 5)),
+    -2: ((2, 3), (3, 2), (4, 2)),
+    1: ((2, 4), (3, 3)),
+    2: ((4, 3), (3, 4), (1, 5), (0, 6)),
+    3: ((4, 4),),
+    4: ((2, 5),),
+    5: ((3, 5), (1, 6), (0, 7)),
+    6: ((4, 5),),
+    7: ((2, 6),),
+    8: ((3, 6), (1, 7), (0, 8)),
+    9: ((4, 6),),
+    10: ((2, 7),),
+    11: ((3, 7), (1, 8), (0, 9)),
+    12: ((4, 7),),
+    13: ((2, 8),),
+    14: ((3, 8), (1, 9)),
+    15: ((4, 8),),
+    16: ((2, 9),),
+    17: ((3, 9),),
+    -3: ((4, 9),),
 }
 
 
@@ -1378,12 +1455,12 @@
 
     def run(name):
         for word in PLAN[name]:
-            route.act(word[0], int(word[1:]))
+            route.act(*word)
 
     @pl.when(step == 0)
     def _():
         greet([lax.rem(route.me + 2 * at, total) for at in range(1, chips)] + [route.partner])
-        run("start")
+        run(-1)
 
     def set_up(which):
         columns = D // total
@@ -1534,7 +1611,7 @@
 
     @pl.when(step == 0)
     def _():
-        run("middle")
+        run(-2)
 
     @pl.when(model == 0)
     def _():
@@ -1546,9 +1623,9 @@
 
     @pl.when(step == 17)
     def _():
-        run("end")
+        run(-3)
         for at in range(len(items)):
-            route.act("F", at)
+            route.act(5, at)
         for at in range(LAYERS):
             out_copy(at).wait()
         across = part_across()
@@ -1637,7 +1714,7 @@
         self.depth, self.chunks, self.sources = depth, chunks, sources
         self.die_buf, self.d_buf, self.x_buf, self.y_buf, self.z_buf = buffers
         self.die_sent, self.die_landed, self.near_sent, self.near_landed, self.z_sent, self.z_landed = sems
-        me = lax.axis_index("dp")
+        me = lax.axis_index(AXIS)
         self.me = me
         self.total = 8 * depth
         core = lax.rem(me, 2)
@@ -2319,8 +2396,7 @@
         layer_bounds(devices),
     )
     grad_embed = own_table(own[count:], embedding.shape[1])
-    renewed = renew_own(full_stats, full_bases)
-    stats_own, bases_own = deal(full_stats, renewed, matrices)
+    stats_own, bases_own = renew_own(full_stats, full_bases, matrices)
     bases_own = jnp.where(
         owners[:, None, None] >= 0, bases_own, layer_bases.reshape(matrices, own_rows, D)
     )
@@ -2449,23 +2525,23 @@
     teacher_protos,
     centre,
 ):
-    devices = lax.axis_size("dp")
-    device_index = lax.axis_index("dp")
+    devices = lax.axis_size(AXIS)
+    device_index = lax.axis_index(AXIS)
     fast = 2 * head_hidden.shape[0] == LANES
     if not fast:
         embed_table, teacher_table = (
-            lax.all_gather(embedding.astype(LOW), "dp", axis=1, tiled=True),
-            lax.all_gather(teacher_embedding.astype(LOW), "dp", axis=1, tiled=True),
+            lax.all_gather(embedding.astype(LOW), AXIS, axis=1, tiled=True),
+            lax.all_gather(teacher_embedding.astype(LOW), AXIS, axis=1, tiled=True),
         )
         layer_full, teacher_full = (
-            lax.all_gather(layers.astype(LOW), "dp", axis=1, tiled=True),
-            lax.all_gather(teacher_layers.astype(LOW), "dp", axis=1, tiled=True),
+            lax.all_gather(layers.astype(LOW), AXIS, axis=1, tiled=True),
+            lax.all_gather(teacher_layers.astype(LOW), AXIS, axis=1, tiled=True),
         )
     if not fast:
-        bases_full = lax.all_gather(layer_bases.astype(LOW), "dp", axis=2, tiled=True).astype(
+        bases_full = lax.all_gather(layer_bases.astype(LOW), AXIS, axis=2, tiled=True).astype(
             layer_bases.dtype
         )
-        stats_full = lax.all_gather(layer_stats.astype(LOW), "dp", axis=2, tiled=True).astype(
+        stats_full = lax.all_gather(layer_stats.astype(LOW), AXIS, axis=2, tiled=True).astype(
             layer_stats.dtype
         )
     if fast:
@@ -2582,8 +2658,8 @@
         )
     else:
         summed = (
-            lax.psum_scatter(grad_table, "dp", scatter_dimension=1, tiled=True),
-            lax.psum_scatter(grad_layers, "dp", scatter_dimension=1, tiled=True),
+            lax.psum_scatter(grad_table, AXIS, scatter_dimension=1, tiled=True),
+            lax.psum_scatter(grad_layers, AXIS, scatter_dimension=1, tiled=True),
         )
         grad_embed = summed[0]
         grad_layers_own = summed[1]
@@ -2605,7 +2681,7 @@
             + jnp.sum(grad_last * grad_last)
             + jnp.sum(grad_protos * grad_protos)
         )
-        totals = lax.psum((squares, grams), "dp")
+        totals = lax.psum((squares, grams), AXIS)
         grad_norm = jnp.sqrt(totals[0])
         clip_factor = jnp.minimum(1.0, CLIP_MAX / (grad_norm + 1e-06))
         next_stats = (
@@ -2669,7 +2745,7 @@
         def renew_owned(operands):
             return lax.cond(operands[2] == device_index, renew, nothing, operands[0], operands[1])
 
-        renewed = lax.psum(lax.map(renew_owned, (flat_stats, flat_bases, owners)), "dp")
+        renewed = lax.psum(lax.map(renew_owned, (flat_stats, flat_bases, owners)), AXIS)
         next_bases = jnp.where(owners[:, None, None] >= 0, renewed, flat_bases).reshape(
             bases_full.shape
         )
@@ -2708,32 +2784,32 @@
 
 def solution(mesh):
     placed = (
-        P("dp", None, None),
+        P(AXIS, None, None),
         P(),
         P(),
-        P(None, "dp"),
-        P(None, "dp"),
-        P(None, "dp"),
-        P(None, "dp", None),
-        P(None, "dp", None),
-        P(None, "dp", None),
-        P(None, None, "dp", None),
-        P(None, None, "dp", None),
-        P("dp", None),
-        P("dp", None),
-        P("dp", None),
-        P(None, "dp"),
-        P(None, "dp"),
-        P(None, "dp"),
-        P(None, "dp"),
-        P(None, "dp"),
-        P(None, "dp"),
-        P(None, "dp"),
-        P(None, "dp", None),
-        P("dp", None),
-        P(None, "dp"),
-        P(None, "dp"),
-        P("dp"),
+        P(None, AXIS),
+        P(None, AXIS),
+        P(None, AXIS),
+        P(None, AXIS, None),
+        P(None, AXIS, None),
+        P(None, AXIS, None),
+        P(None, None, AXIS, None),
+        P(None, None, AXIS, None),
+        P(AXIS, None),
+        P(AXIS, None),
+        P(AXIS, None),
+        P(None, AXIS),
+        P(None, AXIS),
+        P(None, AXIS),
+        P(None, AXIS),
+        P(None, AXIS),
+        P(None, AXIS),
+        P(None, AXIS),
+        P(None, AXIS, None),
+        P(AXIS, None),
+        P(None, AXIS),
+        P(None, AXIS),
+        P(AXIS),
     )
     return jax.shard_map(
         per_device,
@@ -2743,29 +2819,29 @@
             P(),
             P(),
             P(),
-            P(None, "dp"),
-            P(None, "dp"),
-            P(None, "dp"),
-            P(None, "dp", None),
-            P(None, "dp", None),
-            P(None, "dp", None),
-            P(None, None, "dp", None),
-            P(None, None, "dp", None),
-            P("dp", None),
-            P("dp", None),
-            P("dp", None),
-            P(None, "dp"),
-            P(None, "dp"),
-            P(None, "dp"),
-            P(None, "dp"),
-            P(None, "dp"),
-            P(None, "dp"),
-            P(None, "dp"),
-            P(None, "dp", None),
-            P("dp", None),
-            P(None, "dp"),
-            P(None, "dp"),
-            P("dp"),
+            P(None, AXIS),
+            P(None, AXIS),
+            P(None, AXIS),
+            P(None, AXIS, None),
+            P(None, AXIS, None),
+            P(None, AXIS, None),
+            P(None, None, AXIS, None),
+            P(None, None, AXIS, None),
+            P(AXIS, None),
+            P(AXIS, None),
+            P(AXIS, None),
+            P(None, AXIS),
+            P(None, AXIS),
+            P(None, AXIS),
+            P(None, AXIS),
+            P(None, AXIS),
+            P(None, AXIS),
+            P(None, AXIS),
+            P(None, AXIS, None),
+            P(AXIS, None),
+            P(None, AXIS),
+            P(None, AXIS),
+            P(AXIS),
         ),
         check_vma=False,
     )

time: 516 us -> 486 us (0.942)
  Pallas kernels: 461 us -> 431 us
    pallas_call x2 -> x1, Pallas kernels: 69.7 us -> 39.5 us  [renew_own(): pl.pallas_call(functools.partial(renew_kernel, devices), out_shape=(jax.S...]
where the time goes in v4:
time: 486 us; the launch traced here: 476 us
  Pallas kernels  431 us (89%)
  local copies, waits for them, and re-layouts  24.2 us (5%)
  other arithmetic  19 us (4%)
    pallas_call x1, Pallas kernels, fetch_forward(): pl.pallas_call(functools.partial(fetch_kernel, cuts, depth), grid=(LAYERS...  159 us
    pallas_call x1, Pallas kernels, backward(): pl.pallas_call(functools.partial(backward_kernel, cuts, bounds, depth), g...  133 us
    pallas_call x1, Pallas kernels, head(): pl.pallas_call(functools.partial(head_kernel, devices), out_shape=(shape(...  92.9 us
    pallas_call x1, Pallas kernels, renew_own(): pl.pallas_call(functools.partial(renew_kernel, devices), out_shape=(jax.S...  39.5 us
    add x4, other arithmetic, follow(): TEACHER_MOMENTUM * teacher_weight  12.5 us
    unnamed x74, local copies, waits for them, and re-layouts  10.5 us

profile of v4, /device:TPU:31, one launch (start us, length us, event | category | flops | bytes accessed | tf_op | source)
XLA Modules:
  0.0 476.5 jit_solution(2767319323157983383)
XLA Ops:
  0.7 0.9 bitcast_convert_fusion
  2.2 0.8 fusion.6
  3.1 0.8 bitcast_convert_fusion.1
  5.2 2.3 copy.97.patches_ref.refs_3_
  10.5 159.1 %fetch_forward.1 = (f32[2,3,8,384]{3,2,1,0:T(8,128)}, f32[2,3,8,384]{3,2,1,0:T(8,128)}, f32[32,384]{1,0:T(8,128)}, bf16[3,32,144,384]{3,2,1,0:T(8,128)(2,1)}, bf...) custom-call(bf16[3,256,588]{2,1,0:T(8,128)(2,1)} %copy.97.patches_re, ...), custom_call_target="tpu_custom_call" | custom-call | tf_op jit(solution)/shard_map/fetch_forward/pallas_call | solution.py:1673
  169.6 0.9 convert.56
  170.6 1.8 copy.115
  172.4 1.6 fusion.25
  174.0 1.7 unstack.13.last_ref
  175.7 1.5 unstack.15.teacher_last_ref
  177.5 1.1 copy-done.6
  178.6 1.0 copy-done.14
  179.7 92.9 %head.1 = (f32[8,128]{1,0:T(8,128)S(1)}, f32[64,2432]{1,0:T(8,128)S(1)}, f32[8,2048]{1,0:T(8,128)S(1)}, f32[256,2048]{1,0:T(8,128)}, f32[8,384]{1,0:T(8,128)S(1)...) custom-call(bf16[32,128]{1,0:T(8,128)(2,1)S(1)} %fusion.16.feat_ref, f32[64,2432]{1,0:T(8,128)S(1)} %copy-done, ...), custom_call_target="tpu_custom_call" | custom-call | tf_op jit(solution)/shard_map/head/pallas_call | solution.py:834
  272.6 0.8 copy-done.12
  276.0 1.7 copy.103
  277.7 133.0 %backward.1 = (f32[480,384]{1,0:T(8,128)}, f32[8,128]{1,0:T(8,128)}, f32[32,12,384]{2,1,0:T(8,128)}, f32[32,12,384]{2,1,0:T(8,128)}) custom-call(f32[8,128]{1,0:T(8,128)} %copy-done.16, f32[12,12,384]{2,1,0:T(8,128)} %bitcast.76, f32[12,12,384]{2,1,0:T(8,128)} %bitcast.69, bf16[3,256,588]{2,1,0:T(8,128)(2,1)} %copy.97.patches_ref.refs_3_, ...), custom_call_target="tpu_custom_call" | custom-call | tf_op jit(solution)/shard_map/backward/pallas_call | solution.py:2293
  410.7 1.2 slice.136
  412.7 9.2 %multiply_add_fusion = (f32[256,2048]{1,0:T(8,128)}, f32[256,2048]{1,0:T(8,128)}, f32[256,2048]{1,0:T(8,128)}, f32[256,2048]{1,0:T(8,128)}) fusion(f32[256,2048]{1,0:T(8,128)} %teacher_protos_ref.1, f32[256,2048]{1,0:T(8,128)} %protos_ref.1, f32[256,2048]{1,0:T(8,128)} %get-tuple-element.89, f32[]{:T(128)S(6)} %min_shard_map.3, f32[256,2048]{1,0:T(8,128)} %param.45, ...), kind=kLoop, calls=%fused_computation.3 | loop fusion | flops 9961472 | bytes 18874372 | tf_op jit(solution)/shard_map/add | solution.py:328
  422.8 1.8 multiply_add_fusion.2
  424.6 39.5 %renew.1 = (f32[12,12,384]{2,1,0:T(8,128)S(1)}, f32[12,12,384]{2,1,0:T(8,128)S(1)}) custom-call(f32[32,12,384]{2,1,0:T(8,128)S(1)} %copy-done.8, f32[32,12,384]{2,1,0:T(8,128)S(1)} %copy-done.9), custom_call_target="tpu_custom_call" | custom-call | tf_op jit(solution)/shard_map/renew/pallas_call | solution.py:1097
  464.2 0.8 copy.113
  465.0 0.8 copy.112
  465.9 6.7 %soap.1 = (f32[3,144,384]{2,1,0:T(8,128)}, f32[3,144,384]{2,1,0:T(8,128)}, f32[3,144,384]{2,1,0:T(8,128)}, f32[3,144,384]{2,1,0:T(8,128)}) custom-call(f32[8,128]{1,0:T(8,128)S(1)} %copy-done.17, f32[432,384]{1,0:T(8,128)S(1)} %slice.145.grads_ref, bf16[32,144,384]{2,1,0:T(8,128)(2,1)S(1)} %copy-done.1, f32[3,144,384]{2,1,0:T(8,128)S(1)} %copy-done.3, ...), custom_call_target="tpu_custom_call" | custom-call | tf_op jit(solution)/shard_map/soap/pallas_call | solution.py:2480
  474.3 1.3 fusion.26
  (137 shorter events, 11.1 us)
Async XLA Ops:
  0.7 6.8 %copy-start.2 = (f32[3,144,384]{2,1,0:T(8,128)S(1)}, f32[3,144,384]{2,1,0:T(8,128)}, u32[]{:S(2)}) copy-start(f32[3,144,384]{2,1,0:T(8,128)} %weights_ref.1) | copy-start | bytes 1990660
  0.7 7.6 %copy-start.4 = (f32[3,144,384]{2,1,0:T(8,128)S(1)}, f32[3,144,384]{2,1,0:T(8,128)}, u32[]{:S(2)}) copy-start(f32[3,144,384]{2,1,0:T(8,128)} %teacher_ref.1) | copy-start | bytes 1990660
  4.5 4.6 copy-start
  5.2 4.5 copy-start.26
  5.2 4.6 copy-start.25
  174.0 3.3 copy-start.32
  174.0 3.4 copy-start.19
  174.0 3.5 copy-start.15
  179.7 95.0 %copy-start.31 = (f32[2,3,8,384]{3,2,1,0:T(8,128)S(1)}, f32[2,3,8,384]{3,2,1,0:T(8,128)}, u32[]{:S(2)}) copy-start(f32[2,3,8,384]{3,2,1,0:T(8,128)} %get-tuple-element.65) | copy-start | bytes 221188
  412.6 9.3 %copy-start.27 = (f32[2048,8]{0,1:T(8,128)S(1)}, f32[2048,8]{0,1:T(8,128)}, u32[]{:S(2)}) copy-start(f32[2048,8]{0,1:T(8,128)} %param.42) | copy-start | bytes 196612
  412.6 9.3 %copy-start.28 = (f32[2048,8]{0,1:T(8,128)S(1)}, f32[2048,8]{0,1:T(8,128)}, u32[]{:S(2)}) copy-start(f32[2048,8]{0,1:T(8,128)} %param.41) | copy-start | bytes 196612
  412.6 10.0 %copy-start.7 = (f32[64,2432]{1,0:T(8,128)S(1)}, f32[64,2432]{1,0:T(8,128)}, u32[]{:S(2)}) copy-start(f32[64,2432]{1,0:T(8,128)} %teacher_hidden_ref.1) | copy-start | bytes 1867780
  412.6 10.0 %copy-start.13 = (f32[64,2432]{1,0:T(8,128)S(1)}, f32[64,2432]{1,0:T(8,128)}, u32[]{:S(2)}) copy-start(f32[64,2432]{1,0:T(8,128)} %copy-done.12) | copy-start | bytes 1867780
  412.6 10.0 %copy-start.21 = (f32[64,2432]{1,0:T(8,128)S(1)}, f32[64,2432]{1,0:T(8,128)}, u32[]{:S(2)}) copy-start(f32[64,2432]{1,0:T(8,128)} %param.39) | copy-start | bytes 1867780
  412.7 10.0 %copy-start.22 = (f32[64,2432]{1,0:T(8,128)S(1)}, f32[64,2432]{1,0:T(8,128)}, u32[]{:S(2)}) copy-start(f32[64,2432]{1,0:T(8,128)} %param.38) | copy-start | bytes 1867780
  422.7 41.4 %copy-start.33 = (s32[12]{0:T(128)S(1)}, s32[12]{0:T(128)}, u32[]{:S(2)}) copy-start(s32[12]{0:T(128)} %param.28) | copy-start | bytes 148
  422.7 41.4 %copy-start.18 = (f32[3,4,12,384]{3,2,1,0:T(8,128)S(1)}, f32[3,4,12,384]{3,2,1,0:T(8,128)}, u32[]{:S(2)}) copy-start(f32[3,4,12,384]{3,2,1,0:T(8,128)} %copy.104) | copy-start | bytes 663556
  422.7 43.1 %copy-start.20 = (f32[480,384]{1,0:T(8,128)S(1)}, f32[480,384]{1,0:T(8,128)}, u32[]{:S(2)}) copy-start(f32[480,384]{1,0:T(8,128)} %get-tuple-element.78) | copy-start | bytes 2211844
  422.7 43.1 %copy-start.5 = (f32[3,144,384]{2,1,0:T(8,128)S(1)}, f32[3,144,384]{2,1,0:T(8,128)}, u32[]{:S(2)}) copy-start(f32[3,144,384]{2,1,0:T(8,128)} %teacher_ref.1) | copy-start | bytes 1990660
  422.7 43.1 %copy-start.10 = (f32[3,144,384]{2,1,0:T(8,128)S(1)}, f32[3,144,384]{2,1,0:T(8,128)}, u32[]{:S(2)}) copy-start(f32[3,144,384]{2,1,0:T(8,128)} %first_ref.1) | copy-start | bytes 1990660
  422.7 43.1 %copy-start.11 = (f32[3,144,384]{2,1,0:T(8,128)S(1)}, f32[3,144,384]{2,1,0:T(8,128)}, u32[]{:S(2)}) copy-start(f32[3,144,384]{2,1,0:T(8,128)} %second_ref.1) | copy-start | bytes 1990660
  424.6 41.3 %copy-start.1 = (bf16[32,144,384]{2,1,0:T(8,128)(2,1)S(1)}, bf16[32,144,384]{2,1,0:T(8,128)(2,1)}, u32[]{:S(2)}) copy-start(bf16[32,144,384]{2,1,0:T(8,128)(2,1)} %get-tuple-element.79.bases_ref) | copy-start | bytes 10616836
  424.6 41.3 %copy-start.3 = (f32[3,144,384]{2,1,0:T(8,128)S(1)}, f32[3,144,384]{2,1,0:T(8,128)}, u32[]{:S(2)}) copy-start(f32[3,144,384]{2,1,0:T(8,128)} %weights_ref.1) | copy-start | bytes 1990660
  424.6 41.3 %copy-start.17 = (f32[8,128]{1,0:T(8,128)S(1)}, f32[8,128]{1,0:T(8,128)}, u32[]{:S(2)}) copy-start(f32[8,128]{1,0:T(8,128)} %get-tuple-element.77.norm_ref) | copy-start | bytes 12292
  (10 other events, 11.4 us)

commit v5 on v4

--- a/solution.py
+++ b/solution.py
@@ -494,25 +494,25 @@
 
 def head_kernel(
     devices,
-    feat_ref,
+    rows_ref,
     hidden_ref,
     teacher_hidden_ref,
     part_ref,
-    last_ref,
-    teacher_last_ref,
+    last_all_ref,
     protos_ref,
     teacher_protos_ref,
     centre_ref,
     mask_ref,
     mask_row_ref,
-    bases_ref,
     scalars_ref,
     grad_hidden_ref,
     grad_last_ref,
     grad_protos_ref,
     grad_feat_ref,
     centre_out_ref,
-    bases_all_ref,
+    feat_ref,
+    last_ref,
+    teacher_last_ref,
     fb,
     hid_low,
     thid_low,
@@ -552,7 +552,6 @@
     wide_landed,
     core_sent,
     core_landed,
-    *sems,
 ):
     me = lax.axis_index(AXIS)
     core = lax.rem(me, 2)
@@ -565,14 +564,6 @@
     units = hidden_ref.shape[0]
     groups = images // 8
     greet(everyone)
-    layer_part = bases_ref.shape[0] // LAYERS
-    items = [(bases_ref, bases_all_ref, at * layer_part, layer_part) for at in range(LAYERS)]
-    route = Route(devices // 8, items, *sems)
-
-    def beside(*words):
-        for word in words:
-            route.act(*word)
-
     sends = []
 
     def die(step, source, target):
@@ -596,12 +587,36 @@
         sends.extend(made)
         return made
 
+    pieces = [
+        rows_ref[model, image, 0:1, j * LANES : (j + 1) * LANES]
+        for model in range(2)
+        for j in range(D // LANES)
+        for image in range(rows_ref.shape[1])
+    ]
+    blank = jnp.zeros((16 - len(pieces) // 2, LANES), FULL)
+    half_count = len(pieces) // 2
+    feat_ref[...] = jnp.concatenate(
+        pieces[:half_count] + [blank] + pieces[half_count:] + [blank], 0
+    ).astype(LOW)
     fb[me] = feat_ref[...]
     copies = wide(0, feat_ref, fb.at[me])
     hid_low[...] = hidden_ref[...].astype(LOW)
     thid_low[...] = teacher_hidden_ref[...].astype(LOW)
     prot_low[0] = protos_ref[...].astype(LOW)
     prot_low[1] = teacher_protos_ref[...].astype(LOW)
+    last_width = last_ref.shape[0] // devices
+    across = last_all_ref.shape[2]
+    for model, table in enumerate((last_ref, teacher_last_ref)):
+        for half in range(2):
+            first = (2 * half + model) * last_width
+            for at in range(0, devices, 2):
+                pair_rows = [
+                    last_all_ref[slot_of(at + t, devices // 8), first : first + last_width].astype(FULL)
+                    for t in range(2)
+                ]
+                table[
+                    at * last_width : (at + 2) * last_width, half * across : (half + 1) * across
+                ] = jnp.concatenate(pair_rows, 0).astype(LOW)
     block_rows = feat_ref.shape[0]
     row_at = lax.broadcasted_iota(jnp.int32, (images, devices * block_rows), 0)
     col_at = lax.broadcasted_iota(jnp.int32, (images, devices * block_rows), 1)
@@ -610,7 +625,6 @@
     lead = row_at - 3 * col_dev
     for copy in copies:
         copy.wait_recv()
-    beside((0, 0))
     rows_all = fb[...].reshape(devices * block_rows, LANES)
 
     def features_of(model):
@@ -647,13 +661,11 @@
     pre1[...] = pre_one
     tpre_one = dot_nt(tfeats, thid_low[:, :D])
     gather_pair(0, gelu_exact(pre_one).astype(LOW).astype(FULL), gelu_exact(tpre_one).astype(LOW).astype(FULL), act_s, act_t)
-    beside((1, 0), (0, 1))
     pre_two = dot_nt(act_s[...], hid_low[:, D:])
     pre2[...] = pre_two
     tpre_two = dot_nt(act_t[...], thid_low[:, D:])
     gather_pair(1, gelu_exact(pre_two).astype(LOW).astype(FULL), gelu_exact(tpre_two).astype(LOW).astype(FULL), act2_s, act2_t)
 
-    beside((2, 0), (1, 1), (0, 2))
     unit, inverse_norm = unit_rows(dot_nt(act2_s[...], last_ref[...]))
     tunit, unused = unit_rows(dot_nt(act2_t[...], teacher_last_ref[...]))
     unit_ref[...] = unit
@@ -686,7 +698,6 @@
     )
     for copy in copies:
         copy.wait_recv()
-    beside((3, 0), (2, 1), (1, 2))
     merged = stat_all[...]
     tops, totals = merged[:, 0], merged[:, 1]
     ttops, ttotals, crosses = merged[:, 2], merged[:, 3], merged[:, 4]
@@ -745,7 +756,6 @@
         def _(group=group):
             pltpu.make_async_copy(dz_all.at[group], dz_all.at[group], wide_landed.at[3, group]).wait()
 
-    beside((4, 0), (3, 1), (2, 2))
     grad_bottle = dz_all[...].reshape(images, unit.shape[1]).astype(LOW)
     chip_columns = pl.ds(pl.multiple_of(chip * LANES, LANES), LANES)
     pair = dot_nn(grad_bottle, last_ref[:, chip_columns])
@@ -779,7 +789,6 @@
     copy.wait_recv()
     for at in range(chips):
         dp_full[their_rows, at * LANES : (at + 1) * LANES] = dp_half[1, at]
-    beside((4, 1), (3, 2))
     part = jnp.concatenate([part_ref[at % 2, at // 2] for at in range(devices)], 0)
     pair = dot_nn(dp_full[...], part)
     grad_act_one = jnp.where(core == 0, pair[:, :units], pair[:, units:])
@@ -802,7 +811,6 @@
     copy.wait_recv()
     whole = df_sum[...] + df_other[...]
     grad_feat_ref[...] = whole
-    beside((4, 2), (5, 0), (5, 1), (5, 2))
     squares = jnp.sum(grad_hidden_ref[...] * grad_hidden_ref[...])
     squares = squares + jnp.sum(grad_last_ref[...] * grad_last_ref[...])
     squares = squares + jnp.sum(grad_protos_ref[...] * grad_protos_ref[...])
@@ -821,11 +829,11 @@
             pltpu.make_async_copy(dz_own, dz_own, wide_sent.at[3, step - 1]).wait()
 
 
-def head(feat, hidden, teacher_hidden, part, last, teacher_last, protos, teacher_protos, centre, mask, mask_row, bases, devices):
+def head(rows, hidden, teacher_hidden, part, last_all, protos, teacher_protos, centre, mask, mask_row, devices):
     images = mask.shape[0]
     units, wide = hidden.shape
     bottle, width = protos.shape
-    hid = last.shape[1]
+    hid = 2 * last_all.shape[2]
     chips = devices // 2
     groups = images // 8
     vmem = pl.BlockSpec(memory_space=pltpu.VMEM)
@@ -840,12 +848,14 @@
             shape((bottle, width), FULL),
             shape((8, D), FULL),
             shape((1, width), FULL),
-            shape((devices,) + bases.shape, LOW),
         ),
-        in_specs=[vmem] * 12,
-        out_specs=(vmem,) * 6 + (pl.BlockSpec(memory_space=pl.ANY),),
+        in_specs=[vmem] * 10,
+        out_specs=(vmem,) * 6,
         scratch_shapes=[
-            pltpu.VMEM((devices,) + feat.shape, LOW),
+            pltpu.VMEM((32, LANES), LOW),
+            pltpu.VMEM((bottle, hid), LOW),
+            pltpu.VMEM((bottle, hid), LOW),
+            pltpu.VMEM((devices, 32, LANES), LOW),
             pltpu.VMEM((units, wide), LOW),
             pltpu.VMEM((units, wide), LOW),
             pltpu.VMEM((2, bottle, width), LOW),
@@ -884,11 +894,10 @@
             dma((4, devices)),
             dma((4, chips - 1)),
             dma((4, chips - 1)),
-        ]
-        + route_sems(LAYERS, devices // 8),
+        ],
         compiler_params=params(2),
         name="head",
-    )(feat, hidden, teacher_hidden, part, last, teacher_last, protos, teacher_protos, centre, mask, mask_row, bases)
+    )(rows, hidden, teacher_hidden, part, last_all, protos, teacher_protos, centre, mask, mask_row)
 
 
 def gram_device(matrix):
@@ -1224,18 +1233,8 @@
     return (loss_sum, loss_count, grad_hidden, grad_last, grad_protos, grad_features, next_centre)
 
 
-def own_feature_rows(features, teacher_features):
-    def rows(value):
-        count = value.shape[0]
-        turned = value.reshape(count, D // LANES, LANES).transpose(1, 0, 2).reshape(-1, LANES)
-        return jnp.pad(turned, ((0, 16 - turned.shape[0]), (0, 0)))
-
-    return jnp.concatenate([rows(features), rows(teacher_features)], 0)
-
-
 def head_fast(
-    features,
-    teacher_features,
+    feature_rows,
     valid_mask,
     head_hidden,
     protos,
@@ -1243,31 +1242,24 @@
     teacher_protos,
     centre,
     part,
-    last_full,
-    teacher_last_full,
-    layer_bases,
+    last_all,
     devices,
-    device_index,
 ):
     counted = valid_mask.astype(FULL)
     mask_row = jnp.pad(counted, (0, LANES - counted.size)).reshape(1, LANES)
-    scalars, grad_hidden, grad_last, grad_protos, grad_feat, next_centre, bases_all = head(
-        own_feature_rows(features, teacher_features),
+    scalars, grad_hidden, grad_last, grad_protos, grad_feat, next_centre = head(
+        feature_rows,
         head_hidden,
         teacher_hidden,
         part,
-        last_full,
-        teacher_last_full,
+        last_all,
         protos,
         teacher_protos,
         centre[None],
         counted[:, None],
         mask_row,
-        layer_bases.reshape(-1, D).astype(LOW),
         devices,
     )
-    count = features.shape[0]
-    grad_features = lax.dynamic_slice_in_dim(grad_feat, (device_index % 2) * count, count, 0)
     return (
         scalars[0, 0],
         scalars[0, 1],
@@ -1275,9 +1267,8 @@
         grad_hidden,
         grad_last.T,
         grad_protos,
-        grad_features,
+        grad_feat,
         next_centre[0],
-        bases_all,
     )
 
 
@@ -1330,6 +1321,30 @@
 WIDE_TABLE = 1152
 POSITION_AT = 640
 VECTORS_AT = 1024
+
+
+CLASS_ROWS = 16
+
+
+def by_head(row):
+    head = lax.broadcasted_iota(jnp.int32, (CLASS_ROWS, D), 0)
+    lane = lax.broadcasted_iota(jnp.int32, (CLASS_ROWS, D), 1)
+    return jnp.where(lax.shift_right_logical(lane, 6) == head, row, 0.0)
+
+
+def tail_rows_of(row):
+    at = lax.broadcasted_iota(jnp.int32, (TOKENS - HALF_ROW, D), 0)
+    return jnp.where(at == 0, row, 0.0)
+
+
+def head_halves(wide):
+    lane = lax.broadcasted_iota(jnp.int32, wide.shape, 1)
+    low_half = jnp.where(lane < HEAD_DIM, wide, 0.0)
+    return low_half.astype(LOW), (wide - low_half).astype(LOW)
+
+
+def live_keys(columns):
+    return lax.broadcasted_iota(jnp.int32, (TOKENS, columns), 0) < SEQ
 
 
 def table_rows(embedding):
@@ -1529,8 +1544,7 @@
         unpack_blocks(weights, joint_weight, output_weight, cuts, depth)
 
     vectors = vectors_all[model, pl.ds(pl.multiple_of(layer * 8, 8), 8), :]
-    lane = lax.broadcasted_iota(jnp.int32, (TOKENS, LANES), 1)
-    live = lax.broadcasted_iota(jnp.int32, (TOKENS, TOKENS), 0) < SEQ
+    live = live_keys(HALF_ROW)
 
     def attend(save):
         def keep(name, value):
@@ -1541,30 +1555,29 @@
         keep("inputs", inputs)
         normed = layer_norm(inputs, vectors[0:1], vectors[1:2]).astype(LOW)
         keep("normed", normed)
-        mixed = []
+        joint = dot_nt(normed, joint_weight[...])
+        rounded = joint.astype(LOW)
+        keep("joint", rounded)
+        queries = (rounded[:, :D].astype(FULL) * HEAD_DIM ** (-0.5)).astype(LOW)
+        keys_in, values_in = rounded[:, D : 2 * D], rounded[:, 2 * D :]
+        values = joint[:, 2 * D :].T.astype(LOW)
+        turned_heads = []
         for pair in range(D // LANES):
-            lower = pair * LANES
-            parts = [
-                dot_nt(normed, joint_weight[third * D + lower : third * D + lower + LANES])
-                for third in range(3)
-            ]
-            rounded = [part.astype(LOW) for part in parts]
-            if save:
-                for third in range(3):
-                    outs["joint"][0, 0, :, third * D + lower : third * D + lower + LANES] = rounded[
-                        third
-                    ]
-            queries = (rounded[0].astype(FULL) * HEAD_DIM ** (-0.5)).astype(LOW)
-            values = parts[2].T.astype(LOW)
-            turned_heads = []
-            for half in range(2):
-                keys_half = jnp.where(
-                    (lane >= HEAD_DIM) == bool(half), rounded[1].astype(FULL), 0.0
-                ).astype(LOW)
-                share = chance(keys_half, queries, live).astype(LOW)
-                turned_heads.append(dot_nn(values[half * HEAD_DIM : (half + 1) * HEAD_DIM], share))
-            mixed.append(jnp.concatenate(turned_heads, 0).T.astype(LOW))
-        mixed = jnp.concatenate(mixed, 1)
+            columns = slice(pair * LANES, (pair + 1) * LANES)
+            for half, keys_half in enumerate(head_halves(keys_in[:, columns].astype(FULL))):
+                lower = pair * LANES + half * HEAD_DIM
+                share = chance(keys_half, queries[:HALF_ROW, columns], live).astype(LOW)
+                turned_heads.append(dot_nn(values[lower : lower + HEAD_DIM], share))
+        class_query = by_head(queries[HALF_ROW:].astype(FULL)[:1]).astype(LOW)
+        class_share = chance(keys_in, class_query, live_keys(CLASS_ROWS)).astype(LOW)
+        class_mixed = jnp.sum(by_head(dot_tn(class_share, values_in)), 0, keepdims=True)
+        mixed = jnp.concatenate(
+            [
+                jnp.concatenate(turned_heads, 0).T.astype(LOW),
+                tail_rows_of(class_mixed).astype(LOW),
+            ],
+            0,
+        )
         keep("mixed", mixed)
         attended = dot_nt(mixed, output_weight[...])
         keep("attended", attended.astype(LOW))
@@ -1644,11 +1657,10 @@
     vmem = pl.BlockSpec(memory_space=pltpu.VMEM)
     anywhere = pl.BlockSpec(memory_space=pl.ANY)
 
-    def last_rows(value):
-        return value.T.astype(LOW).reshape(-1, LANES)
-
     table = table_rows(embedding)
-    last = jnp.concatenate([last_rows(head_last), last_rows(teacher_last)], 0)
+    last = jnp.concatenate([head_last, teacher_last], 1).T.astype(LOW)
+    across = last.shape[1] // 2
+    last = jnp.concatenate([last[:, :across], last[:, across:]], 0)
     columns = head_hidden[:, D:].astype(LOW)
     outs = [shape((2, images, 8, D), FULL)] * 2
     specs = [vmem] * 2
@@ -1704,11 +1716,6 @@
     )
 
 
-def last_tables(last_all, width, devices):
-    ordered = last_all.reshape(8, devices // 8, 2, -1, LANES).transpose(2, 1, 0, 3, 4)
-    return ordered.reshape(2, width, -1)
-
-
 class Reduce:
     def __init__(self, depth, chunks, sources, buffers, sems):
         self.depth, self.chunks, self.sources = depth, chunks, sources
@@ -1859,18 +1866,20 @@
         squares_ref,
         stats_ref,
         bases_ref,
+        bases_low_ref,
         patches_ref,
         weights_ref,
         vectors_ref,
         final_ref,
         grad_feat_ref,
-    ) = refs[:8]
-    saved = dict(zip(SAVED, refs[8 : 8 + len(SAVED)]))
+    ) = refs[:9]
+    saved = dict(zip(SAVED, refs[9 : 9 + len(SAVED)]))
     (
         own_ref,
         norm_ref,
         next_stats_ref,
         basis_ref,
+        bases_all_ref,
         grad_now,
         joint_weight,
         output_weight,
@@ -1905,9 +1914,11 @@
         gram_landed,
         square_sent,
         square_landed,
-    ) = refs[8 + len(SAVED) :]
+        *sems,
+    ) = refs[9 + len(SAVED) :]
     step, image = pl.program_id(0), pl.program_id(1)
-    images = final_ref.shape[0]
+    images = final_ref.shape[1]
+    route = Route(depth, [(bases_low_ref, bases_all_ref, 0, bases_low_ref.shape[0])], *sems)
     now = step * images + image
     layer_rows = cuts[3]
     chunks = [(layer * layer_rows, layer_rows) for layer in reversed(range(LAYERS))]
@@ -1976,6 +1987,7 @@
     @pl.when(now == 0)
     def _():
         greet(everyone)
+        route.act(0, 0)
         for matrix in range(matrices):
 
             @pl.when(me != gram_device(matrix))
@@ -1992,17 +2004,23 @@
         grad_patch[...] = jnp.zeros(grad_patch.shape, FULL)
         grad_start[...] = jnp.zeros(grad_start.shape, FULL)
 
+    @pl.when(now == 1)
+    def _():
+        route.act(1, 0)
+
     @pl.when(now == images)
     def _():
         ring.one(0)
 
     @pl.when(now == images + 1)
     def _():
+        route.act(3, 0)
         ring.two(0)
 
     @pl.when(now == 2 * images)
     def _():
         ring.one(1)
+        route.act(4, 0)
         ring.three(0)
 
     @pl.when(now == 2 * images + 1)
@@ -2021,9 +2039,9 @@
     @pl.when(step == 0)
     def _():
         first = lax.broadcasted_iota(jnp.int32, (8, D), 0) == 0
-        given = jnp.where(first, grad_feat_ref[image], 0.0)
+        given = jnp.where(first, grad_feat_ref[pl.ds(core * images + image, 1), :], 0.0)
         grad_class, grad_gain, grad_shift = norm_back(
-            final_ref[image], vectors_ref[tail + 2 : tail + 3], given
+            final_ref[0, image], vectors_ref[tail + 2 : tail + 3], given
         )
         grad_rows[tail + 2 : tail + 3] += grad_gain[None]
         grad_rows[tail + 3 : tail + 4] += grad_shift[None]
@@ -2053,40 +2071,47 @@
     grad_attended_all[rows, :] = grad_attended
     grad_scale_one = jnp.sum(grad_middle * saved["attended"][0, 0].astype(FULL), 0, keepdims=True)
     grad_mixed = dot_nn(grad_attended, output_weight[...]).astype(LOW)
-    lane = lax.broadcasted_iota(jnp.int32, (TOKENS, LANES), 1)
-    live = lax.broadcasted_iota(jnp.int32, (TOKENS, TOKENS), 0) < SEQ
+    live = live_keys(HALF_ROW)
+    rounded = saved["joint"][0, 0]
+    queries = (rounded[:, :D].astype(FULL) * HEAD_DIM ** (-0.5)).astype(LOW)
+    keys_in, values_in = rounded[:, D : 2 * D], rounded[:, 2 * D :]
+    keys_turned = keys_in.astype(FULL).T.astype(LOW)
+    turned, grad_keys, grad_values = [], [], []
+    low_half = lax.broadcasted_iota(jnp.int32, (TOKENS, LANES), 1) < HEAD_DIM
     for pair in range(D // LANES):
-        lower = pair * LANES
-        queries, keys_in, values_in = [
-            saved["joint"][0, 0, :, third * D + lower : third * D + lower + LANES]
-            for third in range(3)
-        ]
-        queries = (queries.astype(FULL) * HEAD_DIM ** (-0.5)).astype(LOW)
-        keys_wide = keys_in.astype(FULL)
-        values_wide = values_in.astype(FULL)
-        keys_turned = keys_wide.T.astype(LOW)
-        grad_head = grad_mixed[:, lower : lower + LANES]
-        turned, grad_keys, grad_values = [], [], []
+        columns = slice(pair * LANES, (pair + 1) * LANES)
+        pair_queries, grad_head = queries[:HALF_ROW, columns], grad_mixed[:HALF_ROW, columns]
+        keys_halves = head_halves(keys_in[:, columns].astype(FULL))
+        values_halves = head_halves(values_in[:, columns].astype(FULL))
+        both_keys, both_values = [], []
         for half in range(2):
-            mine = (lane >= HEAD_DIM) == bool(half)
-            share = chance(jnp.where(mine, keys_wide, 0.0).astype(LOW), queries, live)
-            grad_share = dot_nt(jnp.where(mine, values_wide, 0.0).astype(LOW), grad_head)
-            grad_values.append(dot_nn(share.astype(LOW), grad_head))
+            lower = pair * LANES + half * HEAD_DIM
+            share = chance(keys_halves[half], pair_queries, live)
+            grad_share = dot_nt(values_halves[half], grad_head)
+            both_values.append(dot_nn(share.astype(LOW), grad_head))
             grad_scores = (
                 share * (grad_share - jnp.sum(share * grad_share, 0, keepdims=True))
             ).astype(LOW)
-            grad_keys.append(dot_nn(grad_scores, queries))
-            turned.append(dot_nn(keys_turned[half * HEAD_DIM : (half + 1) * HEAD_DIM], grad_scores))
-        grad_queries = jnp.concatenate(turned, 0).T * HEAD_DIM ** (-0.5)
-        low_half = lane < HEAD_DIM
-        for third, value in enumerate(
-            (
-                grad_queries,
-                jnp.where(low_half, grad_keys[0], grad_keys[1]),
-                jnp.where(low_half, grad_values[0], grad_values[1]),
-            )
-        ):
-            grad_joint_all[rows, third * D + lower : third * D + lower + LANES] = value.astype(LOW)
+            both_keys.append(dot_nn(grad_scores, pair_queries))
+            turned.append(dot_nn(keys_turned[lower : lower + HEAD_DIM], grad_scores))
+        grad_keys.append(jnp.where(low_half, both_keys[0], both_keys[1]))
+        grad_values.append(jnp.where(low_half, both_values[0], both_values[1]))
+    class_query = by_head(queries[HALF_ROW:].astype(FULL)[:1]).astype(LOW)
+    class_grad = by_head(grad_mixed[HALF_ROW:].astype(FULL)[:1]).astype(LOW)
+    share = chance(keys_in, class_query, live_keys(CLASS_ROWS))
+    grad_share = dot_nt(values_in, class_grad)
+    grad_scores = (share * (grad_share - jnp.sum(share * grad_share, 0, keepdims=True))).astype(LOW)
+    class_row = jnp.sum(by_head(dot_tn(grad_scores, keys_in)), 0, keepdims=True)
+    grad_queries = jnp.concatenate(
+        [jnp.concatenate(turned, 0).T, tail_rows_of(class_row)], 0
+    ) * HEAD_DIM ** (-0.5)
+    grad_joint_all[rows, :D] = grad_queries.astype(LOW)
+    grad_joint_all[rows, D : 2 * D] = (
+        jnp.concatenate(grad_keys, 1) + dot_nn(grad_scores, class_query)
+    ).astype(LOW)
+    grad_joint_all[rows, 2 * D :] = (
+        jnp.concatenate(grad_values, 1) + dot_nn(share.astype(LOW), class_grad)
+    ).astype(LOW)
     grad_normed = dot_nn(grad_joint_all[rows, :], joint_weight[...])
     grad_input_norm, grad_gain_one, grad_shift_one = norm_back(
         saved["inputs"][0, 0], vectors[0:1], grad_normed
@@ -2151,6 +2176,10 @@
                 packet[first + t, cuts[1] : cuts[2]] = inner_rows[t * per[2] : (t + 1) * per[2]]
                 packet[first + t, cuts[2] : cuts[3]] = outer_rows[t * per[3] : (t + 1) * per[3]]
 
+    @pl.when(now == images - 1)
+    def _():
+        route.act(2, 0)
+
     @pl.when((image == images - 1) & (step == LAYERS - 1))
     def _():
         ring.three(1)
@@ -2245,6 +2274,7 @@
         for source in range(total):
             next_stats_ref[source] = BETA_STAT * stat_buf[0, source] + scale * next_stats_ref[source]
 
+        route.act(5, 0)
         for copy in copies:
             copy.wait_send()
         for k in range(count):
@@ -2259,7 +2289,7 @@
 
 
 def backward(
-    squares, patches, vectors, blocks, final, grad_feat, saved, stats, bases, devices
+    squares, patches, vectors, blocks, final, grad_feat, saved, stats, bases, bases_low, devices
 ):
     images = patches.shape[0]
     depth = devices // 8
@@ -2298,9 +2328,11 @@
             shape((8, LANES), FULL),
             shape((devices, own_rows, D), FULL),
             shape((devices, own_rows, D), FULL),
+            shape((devices,) + bases_low.shape, LOW),
         ),
         in_specs=[
             vmem,
+            anywhere,
             anywhere,
             anywhere,
             vmem,
@@ -2310,7 +2342,7 @@
             vmem,
         ]
         + [of_saved(name) for name in SAVED],
-        out_specs=(vmem,) * 4,
+        out_specs=(vmem,) * 4 + (anywhere,),
         scratch_shapes=[
             pltpu.VMEM((images, TOKENS, D), FULL),
             pltpu.VMEM((3 * D, D), LOW),
@@ -2346,10 +2378,11 @@
             dma((devices,)),
             dma((devices - 1,)),
             dma((devices - 1,)),
-        ],
+        ]
+        + route_sems(1, depth),
         compiler_params=params(3, 63 << 20),
         name="backward",
-    )(squares, stats, bases, patches, blocks, vectors, final, grad_feat, *saved)
+    )(squares, stats, bases, bases_low, patches, blocks, vectors, final, grad_feat, *saved)
 
 
 def own_table(rows, columns):
@@ -2378,10 +2411,9 @@
     layers_first,
     layers_second,
     teacher_layers,
-    bases_all,
     devices,
 ):
-    own, norm, full_stats, full_bases = gathered
+    own, norm, full_stats, full_bases, bases_all = gathered
     own_rows = layer_stats.shape[2]
     matrices = owners.shape[0]
     count = layers.shape[0] * layers.shape[1]
@@ -2556,11 +2588,6 @@
             head_hidden,
             devices,
         )
-        features = feature_rows[0, :, 0].astype(LOW)
-        teacher_features = feature_rows[1, :, 0].astype(LOW)
-        last_full, teacher_last_full = last_tables(
-            last_all, head_last.shape[1] * devices, devices
-        )
     else:
         features, layer_inputs, final_state = backbone(patches, embed_table, layer_full, devices)
         teacher_features, unused_inputs, unused_final = backbone(
@@ -2576,10 +2603,8 @@
             grad_protos,
             grad_features,
             next_centre,
-            bases_all,
         ) = head_fast(
-            features,
-            teacher_features,
+            feature_rows,
             valid_mask,
             head_hidden,
             protos,
@@ -2587,11 +2612,8 @@
             teacher_protos,
             centre,
             part,
-            last_full,
-            teacher_last_full,
-            layer_bases,
+            last_all,
             devices,
-            device_index,
         )
     else:
         (
@@ -2616,18 +2638,18 @@
             device_index,
         )
     if fast:
-        grad_rows = jnp.pad(grad_features[:, None], ((0, 0), (0, 7), (0, 0)))
         matrices, own_rows = owners.shape[0], layer_stats.shape[2]
         gathered = backward(
             squares,
             patches,
             vectors,
             layer_full,
-            final_rows[0],
-            grad_rows,
+            final_rows,
+            grad_features,
             saved,
             layer_stats.reshape(matrices, own_rows, D),
             layer_bases.reshape(matrices, own_rows, D),
+            layer_bases.reshape(matrices * own_rows, D).astype(LOW),
             devices,
         )
     else:
@@ -2653,7 +2675,6 @@
             layers_first,
             layers_second,
             teacher_layers,
-            bases_all,
             devices,
         )
     else:

time: 486 us -> 479 us (0.986)
  local copies, waits for them, and re-layouts: 24.2 us -> 16.7 us
    pallas_call x1, Pallas kernels: 133 us -> 151 us  [backward(): pl.pallas_call(functools.partial(backward_kernel, cuts, bounds, depth), g...]
    pallas_call x1, Pallas kernels: 92.9 us -> 84.2 us  [head(): pl.pallas_call(functools.partial(head_kernel, devices), out_shape=(shape(...]
    pallas_call x1, Pallas kernels: 39.5 us -> 33.1 us  [renew_own(): pl.pallas_call(functools.partial(renew_kernel, devices), out_shape=(jax.S...]
    unnamed x74 -> x82, local copies, waits for them, and re-layouts: 10.5 us -> 10.4 us
where the time goes in v5:
time: 479 us; the launch traced here: 471 us
  Pallas kernels  432 us (90%)
  other arithmetic  19.9 us (4%)
  local copies, waits for them, and re-layouts  16.7 us (3%)
    pallas_call x1, Pallas kernels, fetch_forward(): pl.pallas_call(functools.partial(fetch_kernel, cuts, depth), grid=(LAYERS...  157 us
    pallas_call x1, Pallas kernels, backward(): pl.pallas_call(functools.partial(backward_kernel, cuts, bounds, depth), g...  151 us
    pallas_call x1, Pallas kernels, head(): pl.pallas_call(functools.partial(head_kernel, devices), out_shape=(shape(...  84.2 us
    pallas_call x1, Pallas kernels, renew_own(): pl.pallas_call(functools.partial(renew_kernel, devices), out_shape=(jax.S...  33.1 us
    add x4, other arithmetic, follow(): TEACHER_MOMENTUM * teacher_weight  12.5 us
    unnamed x82, local copies, waits for them, and re-layouts  10.4 us

profile of v5, /device:TPU:31, one launch (start us, length us, event | category | flops | bytes accessed | tf_op | source)
XLA Modules:
  0.0 470.9 jit_solution(14391053635555420658)
XLA Ops:
  0.7 0.9 bitcast_convert_fusion
  2.2 0.9 fusion.6
  3.2 0.8 bitcast_convert_fusion.1
  5.3 0.8 convert.57
  6.2 0.8 convert.58
  7.7 1.4 copy.91.patches_ref.refs_4_
  9.1 0.8 convert_element_type.35.layers_ref
  9.8 0.8 convert_element_type.36.teacher_layers_ref
  11.3 157.3 %fetch_forward.1 = (f32[2,3,8,384]{3,2,1,0:T(8,128)}, f32[2,3,8,384]{3,2,1,0:T(8,128)}, f32[32,384]{1,0:T(8,128)}, bf16[3,32,144,384]{3,2,1,0:T(8,128)(2,1)}, bf...) custom-call(bf16[3,256,588]{2,1,0:T(8,128)(2,1)} %copy.91.patches_re, ...), custom_call_target="tpu_custom_call" | custom-call | tf_op jit(solution)/shard_map/fetch_forward/pallas_call | solution.py:1685
  168.8 1.0 copy-done.15
  169.9 0.9 copy-done.16
  170.7 84.2 %head.1 = (f32[8,128]{1,0:T(8,128)S(1)}, f32[64,2432]{1,0:T(8,128)S(1)}, f32[8,2048]{1,0:T(8,128)S(1)}, f32[256,2048]{1,0:T(8,128)S(1)}, f32[8,384]{1,0:T(8,128)S(1)}, /*index=5*/f32[1,2048]{1,0:T(1,128)S(1)}) custom-call(f32[2,3,8,384]{3,2,1,0:T(8,128)S(1)} %copy-done.16, f32[64,2432]{1,0:T(8,128)S(1)} %copy-done, f32[64,2432]{1,0:T(8,128)S(1)} %copy-done.6, ...), custom_call_target="tpu_custom_call" | custom-call | tf_op jit(solution)/shard_map/head/pallas_call | solution.py:842
  255.0 1.3 copy-done.8
  256.3 0.8 copy-done.13
  258.3 0.7 copy.94
  260.5 150.9 %backward.1 = (f32[480,384]{1,0:T(8,128)}, f32[8,128]{1,0:T(8,128)}, f32[32,12,384]{2,1,0:T(8,128)}, f32[32,12,384]{2,1,0:T(8,128)}, bf16[32,144,384]{2,1,0:T(8,128)(2,1)}) custom-call(f32[8,128]{1,0:T(8,128)} %copy-done.19, f32[12,12,384]{2,1,0:T(8,128)} %bitcast.61, f32[12,12,384]{2,1,0:T(8,128)} %bitcast.54, ...), custom_call_target="tpu_custom_call" | custom-call | tf_op jit(solution)/shard_map/backward/pallas_call | solution.py:2323
  411.5 1.2 slice.128
  413.5 9.2 %multiply_add_fusion = (f32[256,2048]{1,0:T(8,128)}, f32[256,2048]{1,0:T(8,128)}, f32[256,2048]{1,0:T(8,128)}, f32[256,2048]{1,0:T(8,128)}) fusion(f32[256,2048]{1,0:T(8,128)} %teacher_protos_ref.1, f32[256,2048]{1,0:T(8,128)} %protos_ref.1, f32[256,2048]{1,0:T(8,128)} %copy-done.8, f32[]{:T(128)S(6)} %min_shard_map.3, f32[256,2048]{1,0:T(8,128)} %param.45, ...), kind=kLoop, calls=%fused_computation.2 | loop fusion | flops 9961472 | bytes 18874372 | tf_op jit(solution)/shard_map/add | solution.py:328
  423.6 1.8 multiply_add_fusion.2
  425.4 33.1 %renew.1 = (f32[12,12,384]{2,1,0:T(8,128)S(1)}, f32[12,12,384]{2,1,0:T(8,128)S(1)}) custom-call(f32[32,12,384]{2,1,0:T(8,128)S(1)} %copy-done.9, f32[32,12,384]{2,1,0:T(8,128)S(1)} %copy-done.10), custom_call_target="tpu_custom_call" | custom-call | tf_op jit(solution)/shard_map/renew/pallas_call | solution.py:1106
  458.6 0.8 copy.104
  459.4 0.8 copy.103
  460.3 6.7 %soap.1 = (f32[3,144,384]{2,1,0:T(8,128)}, f32[3,144,384]{2,1,0:T(8,128)}, f32[3,144,384]{2,1,0:T(8,128)}, f32[3,144,384]{2,1,0:T(8,128)}) custom-call(f32[8,128]{1,0:T(8,128)S(1)} %copy-done.20, f32[432,384]{1,0:T(8,128)S(1)} %slice.137.grads_ref, bf16[32,144,384]{2,1,0:T(8,128)(2,1)S(1)} %copy-done.1, f32[3,144,384]{2,1,0:T(8,128)S(1)} %copy-done.3, ...), custom_call_target="tpu_custom_call" | custom-call | tf_op jit(solution)/shard_map/soap/pallas_call | solution.py:2512
  468.8 1.3 fusion.23
  (128 shorter events, 9.4 us)
Async XLA Ops:
  0.7 8.4 %copy-start.2 = (f32[3,144,384]{2,1,0:T(8,128)S(1)}, f32[3,144,384]{2,1,0:T(8,128)}, u32[]{:S(2)}) copy-start(f32[3,144,384]{2,1,0:T(8,128)} %weights_ref.1) | copy-start | bytes 1990660
  2.2 7.7 %copy-start.4 = (f32[3,144,384]{2,1,0:T(8,128)S(1)}, f32[3,144,384]{2,1,0:T(8,128)}, u32[]{:S(2)}) copy-start(f32[3,144,384]{2,1,0:T(8,128)} %teacher_ref.1) | copy-start | bytes 1990660
  9.1 159.6 %copy-start.36 = (s32[96]{0:T(128)S(1)}, s32[96]{0:T(128)}, u32[]{:S(2)}) copy-start(s32[96]{0:T(128)} %param.27) | copy-start | bytes 1156
  9.1 159.7 %copy-start.6 = (f32[64,2432]{1,0:T(8,128)S(1)}, f32[64,2432]{1,0:T(8,128)}, u32[]{:S(2)}) copy-start(f32[64,2432]{1,0:T(8,128)} %teacher_hidden_ref.1) | copy-start | bytes 1867780
  9.1 159.7 %copy-start.18 = (f32[2048]{0:T(1024)S(1)}, f32[2048]{0:T(1024)}, u32[]{:S(2)}) copy-start(f32[2048]{0:T(1024)} %param.51) | copy-start | bytes 24580
  170.7 87.5 %copy-start.23 = (f32[3,4,12,384]{3,1,2,0:T(4,128)S(1)}, f32[3,4,12,384]{3,1,2,0:T(4,128)}, u32[]{:S(2)}) copy-start(f32[3,4,12,384]{3,1,2,0:T(4,128)} %param.36) | copy-start | bytes 663556
  170.7 89.0 %copy-start.31 = (f32[3,4,12,384]{3,1,2,0:T(4,128)S(1)}, f32[3,4,12,384]{3,1,2,0:T(4,128)}, u32[]{:S(2)}) copy-start(f32[3,4,12,384]{3,1,2,0:T(4,128)} %param.35) | copy-start | bytes 663556
  413.4 9.3 %copy-start.29 = (f32[2048,8]{0,1:T(8,128)S(1)}, f32[2048,8]{0,1:T(8,128)}, u32[]{:S(2)}) copy-start(f32[2048,8]{0,1:T(8,128)} %param.49) | copy-start | bytes 196612
  413.4 9.3 %copy-start.30 = (f32[2048,8]{0,1:T(8,128)S(1)}, f32[2048,8]{0,1:T(8,128)}, u32[]{:S(2)}) copy-start(f32[2048,8]{0,1:T(8,128)} %param.40) | copy-start | bytes 196612
  413.4 9.3 %copy-start.32 = (f32[2048,8]{0,1:T(8,128)S(1)}, f32[2048,8]{0,1:T(8,128)}, u32[]{:S(2)}) copy-start(f32[2048,8]{0,1:T(8,128)} %param.42) | copy-start | bytes 196612
  413.4 9.3 %copy-start.33 = (f32[2048,8]{0,1:T(8,128)S(1)}, f32[2048,8]{0,1:T(8,128)}, u32[]{:S(2)}) copy-start(f32[2048,8]{0,1:T(8,128)} %param.41) | copy-start | bytes 196612
  413.4 10.0 %copy-start.7 = (f32[64,2432]{1,0:T(8,128)S(1)}, f32[64,2432]{1,0:T(8,128)}, u32[]{:S(2)}) copy-start(f32[64,2432]{1,0:T(8,128)} %teacher_hidden_ref.1) | copy-start | bytes 1867780
  413.4 10.0 %copy-start.14 = (f32[64,2432]{1,0:T(8,128)S(1)}, f32[64,2432]{1,0:T(8,128)}, u32[]{:S(2)}) copy-start(f32[64,2432]{1,0:T(8,128)} %copy-done.13) | copy-start | bytes 1867780
  413.4 10.0 %copy-start.25 = (f32[64,2432]{1,0:T(8,128)S(1)}, f32[64,2432]{1,0:T(8,128)}, u32[]{:S(2)}) copy-start(f32[64,2432]{1,0:T(8,128)} %param.39) | copy-start | bytes 1867780
  413.4 10.0 %copy-start.26 = (f32[64,2432]{1,0:T(8,128)S(1)}, f32[64,2432]{1,0:T(8,128)}, u32[]{:S(2)}) copy-start(f32[64,2432]{1,0:T(8,128)} %param.38) | copy-start | bytes 1867780
  423.5 35.0 %copy-start.37 = (s32[12]{0:T(128)S(1)}, s32[12]{0:T(128)}, u32[]{:S(2)}) copy-start(s32[12]{0:T(128)} %param.28) | copy-start | bytes 148
  423.5 35.0 %copy-start.21 = (f32[3,4,12,384]{3,2,1,0:T(8,128)S(1)}, f32[3,4,12,384]{3,2,1,0:T(8,128)}, u32[]{:S(2)}) copy-start(f32[3,4,12,384]{3,2,1,0:T(8,128)} %copy.94) | copy-start | bytes 663556
  423.5 36.7 %copy-start.24 = (f32[480,384]{1,0:T(8,128)S(1)}, f32[480,384]{1,0:T(8,128)}, u32[]{:S(2)}) copy-start(f32[480,384]{1,0:T(8,128)} %get-tuple-element.78) | copy-start | bytes 2211844
  423.5 36.7 %copy-start.5 = (f32[3,144,384]{2,1,0:T(8,128)S(1)}, f32[3,144,384]{2,1,0:T(8,128)}, u32[]{:S(2)}) copy-start(f32[3,144,384]{2,1,0:T(8,128)} %teacher_ref.1) | copy-start | bytes 1990660
  423.5 36.7 %copy-start.11 = (f32[3,144,384]{2,1,0:T(8,128)S(1)}, f32[3,144,384]{2,1,0:T(8,128)}, u32[]{:S(2)}) copy-start(f32[3,144,384]{2,1,0:T(8,128)} %first_ref.1) | copy-start | bytes 1990660
  423.5 36.7 %copy-start.12 = (f32[3,144,384]{2,1,0:T(8,128)S(1)}, f32[3,144,384]{2,1,0:T(8,128)}, u32[]{:S(2)}) copy-start(f32[3,144,384]{2,1,0:T(8,128)} %second_ref.1) | copy-start | bytes 1990660
  425.4 34.9 %copy-start.1 = (bf16[32,144,384]{2,1,0:T(8,128)(2,1)S(1)}, bf16[32,144,384]{2,1,0:T(8,128)(2,1)}, u32[]{:S(2)}) copy-start(bf16[32,144,384]{2,1,0:T(8,128)(2,1)} %get-tuple-element.79.bases_ref) | copy-start | bytes 10616836
  425.4 34.9 %copy-start.3 = (f32[3,144,384]{2,1,0:T(8,128)S(1)}, f32[3,144,384]{2,1,0:T(8,128)}, u32[]{:S(2)}) copy-start(f32[3,144,384]{2,1,0:T(8,128)} %weights_ref.1) | copy-start | bytes 1990660
  425.4 34.9 %copy-start.20 = (f32[8,128]{1,0:T(8,128)S(1)}, f32[8,128]{1,0:T(8,128)}, u32[]{:S(2)}) copy-start(f32[8,128]{1,0:T(8,128)} %get-tuple-element.77.norm_ref) | copy-start | bytes 12292
  (14 other events, 23.8 us)

commit v6 on v5

--- a/solution.py
+++ b/solution.py
@@ -1566,8 +1566,11 @@
             columns = slice(pair * LANES, (pair + 1) * LANES)
             for half, keys_half in enumerate(head_halves(keys_in[:, columns].astype(FULL))):
                 lower = pair * LANES + half * HEAD_DIM
-                share = chance(keys_half, queries[:HALF_ROW, columns], live).astype(LOW)
-                turned_heads.append(dot_nn(values[lower : lower + HEAD_DIM], share))
+                scores = jnp.where(live, dot_nt(keys_half, queries[:HALF_ROW, columns]), -jnp.inf)
+                grown = jnp.exp(scores - jnp.max(scores, 0, keepdims=True))
+                scale = 1.0 / jnp.sum(grown, 0, keepdims=True)
+                value = dot_nn(values[lower : lower + HEAD_DIM], grown.astype(LOW))
+                turned_heads.append(value * scale)
         class_query = by_head(queries[HALF_ROW:].astype(FULL)[:1]).astype(LOW)
         class_share = chance(keys_in, class_query, live_keys(CLASS_ROWS)).astype(LOW)
         class_mixed = jnp.sum(by_head(dot_tn(class_share, values_in)), 0, keepdims=True)

time: 479 us -> 475 us (level)
    pallas_call x1, Pallas kernels: 151 us -> 145 us  [backward(): pl.pallas_call(functools.partial(backward_kernel, cuts, bounds, depth), g...]
where the time goes in v6:
time: 475 us; the launch traced here: 467 us
  Pallas kernels  428 us (90%)
  other arithmetic  19.9 us (4%)
  local copies, waits for them, and re-layouts  16.7 us (4%)
    pallas_call x1, Pallas kernels, fetch_forward(): pl.pallas_call(functools.partial(fetch_kernel, cuts, depth), grid=(LAYERS...  154 us
    pallas_call x1, Pallas kernels, backward(): pl.pallas_call(functools.partial(backward_kernel, cuts, bounds, depth), g...  145 us
    pallas_call x1, Pallas kernels, head(): pl.pallas_call(functools.partial(head_kernel, devices), out_shape=(shape(...  84.9 us
    pallas_call x1, Pallas kernels, renew_own(): pl.pallas_call(functools.partial(renew_kernel, devices), out_shape=(jax.S...  37.5 us
    add x4, other arithmetic, follow(): TEACHER_MOMENTUM * teacher_weight  12.5 us
    unnamed x82, local copies, waits for them, and re-layouts  10.4 us

profile of v6, /device:TPU:31, one launch (start us, length us, event | category | flops | bytes accessed | tf_op | source)
XLA Modules:
  0.0 467.1 jit_solution(15105241649379282301)
XLA Ops:
  0.7 0.9 bitcast_convert_fusion
  2.2 0.9 fusion.6
  3.2 0.8 bitcast_convert_fusion.1
  5.3 0.8 convert.57
  6.2 0.8 convert.58
  7.7 1.4 copy.91.patches_ref.refs_4_
  9.1 0.8 convert_element_type.35.layers_ref
  9.8 0.8 convert_element_type.36.teacher_layers_ref
  11.3 154.0 %fetch_forward.1 = (f32[2,3,8,384]{3,2,1,0:T(8,128)}, f32[2,3,8,384]{3,2,1,0:T(8,128)}, f32[32,384]{1,0:T(8,128)}, bf16[3,32,144,384]{3,2,1,0:T(8,128)(2,1)}, bf...) custom-call(bf16[3,256,588]{2,1,0:T(8,128)(2,1)} %copy.91.patches_re, ...), custom_call_target="tpu_custom_call" | custom-call | tf_op jit(solution)/shard_map/fetch_forward/pallas_call | solution.py:1688
  165.5 1.0 copy-done.15
  166.5 0.9 copy-done.16
  167.4 84.9 %head.1 = (f32[8,128]{1,0:T(8,128)S(1)}, f32[64,2432]{1,0:T(8,128)S(1)}, f32[8,2048]{1,0:T(8,128)S(1)}, f32[256,2048]{1,0:T(8,128)S(1)}, f32[8,384]{1,0:T(8,128)S(1)}, /*index=5*/f32[1,2048]{1,0:T(1,128)S(1)}) custom-call(f32[2,3,8,384]{3,2,1,0:T(8,128)S(1)} %copy-done.16, f32[64,2432]{1,0:T(8,128)S(1)} %copy-done, f32[64,2432]{1,0:T(8,128)S(1)} %copy-done.6, ...), custom_call_target="tpu_custom_call" | custom-call | tf_op jit(solution)/shard_map/head/pallas_call | solution.py:842
  252.3 1.3 copy-done.8
  253.6 0.8 copy-done.13
  255.6 0.7 copy.94
  257.9 145.4 %backward.1 = (f32[480,384]{1,0:T(8,128)}, f32[8,128]{1,0:T(8,128)}, f32[32,12,384]{2,1,0:T(8,128)}, f32[32,12,384]{2,1,0:T(8,128)}, bf16[32,144,384]{2,1,0:T(8,128)(2,1)}) custom-call(f32[8,128]{1,0:T(8,128)} %copy-done.19, f32[12,12,384]{2,1,0:T(8,128)} %bitcast.61, f32[12,12,384]{2,1,0:T(8,128)} %bitcast.54, ...), custom_call_target="tpu_custom_call" | custom-call | tf_op jit(solution)/shard_map/backward/pallas_call | solution.py:2326
  403.3 1.2 slice.128
  405.2 9.2 %multiply_add_fusion = (f32[256,2048]{1,0:T(8,128)}, f32[256,2048]{1,0:T(8,128)}, f32[256,2048]{1,0:T(8,128)}, f32[256,2048]{1,0:T(8,128)}) fusion(f32[256,2048]{1,0:T(8,128)} %teacher_protos_ref.1, f32[256,2048]{1,0:T(8,128)} %protos_ref.1, f32[256,2048]{1,0:T(8,128)} %copy-done.8, f32[]{:T(128)S(6)} %min_shard_map.3, f32[256,2048]{1,0:T(8,128)} %param.45, ...), kind=kLoop, calls=%fused_computation.2 | loop fusion | flops 9961472 | bytes 18874372 | tf_op jit(solution)/shard_map/add | solution.py:328
  415.4 1.8 multiply_add_fusion.2
  417.2 37.5 %renew.1 = (f32[12,12,384]{2,1,0:T(8,128)S(1)}, f32[12,12,384]{2,1,0:T(8,128)S(1)}) custom-call(f32[32,12,384]{2,1,0:T(8,128)S(1)} %copy-done.9, f32[32,12,384]{2,1,0:T(8,128)S(1)} %copy-done.10), custom_call_target="tpu_custom_call" | custom-call | tf_op jit(solution)/shard_map/renew/pallas_call | solution.py:1106
  454.9 0.8 copy.104
  455.7 0.8 copy.103
  456.5 6.7 %soap.1 = (f32[3,144,384]{2,1,0:T(8,128)}, f32[3,144,384]{2,1,0:T(8,128)}, f32[3,144,384]{2,1,0:T(8,128)}, f32[3,144,384]{2,1,0:T(8,128)}) custom-call(f32[8,128]{1,0:T(8,128)S(1)} %copy-done.20, f32[432,384]{1,0:T(8,128)S(1)} %slice.137.grads_ref, bf16[32,144,384]{2,1,0:T(8,128)(2,1)S(1)} %copy-done.1, f32[3,144,384]{2,1,0:T(8,128)S(1)} %copy-done.3, ...), custom_call_target="tpu_custom_call" | custom-call | tf_op jit(solution)/shard_map/soap/pallas_call | solution.py:2515
  465.0 1.3 fusion.23
  (128 shorter events, 9.4 us)
Async XLA Ops:
  0.7 8.4 %copy-start.2 = (f32[3,144,384]{2,1,0:T(8,128)S(1)}, f32[3,144,384]{2,1,0:T(8,128)}, u32[]{:S(2)}) copy-start(f32[3,144,384]{2,1,0:T(8,128)} %weights_ref.1) | copy-start | bytes 1990660
  2.2 7.7 %copy-start.4 = (f32[3,144,384]{2,1,0:T(8,128)S(1)}, f32[3,144,384]{2,1,0:T(8,128)}, u32[]{:S(2)}) copy-start(f32[3,144,384]{2,1,0:T(8,128)} %teacher_ref.1) | copy-start | bytes 1990660
  9.1 156.2 %copy-start.36 = (s32[96]{0:T(128)S(1)}, s32[96]{0:T(128)}, u32[]{:S(2)}) copy-start(s32[96]{0:T(128)} %param.27) | copy-start | bytes 1156
  9.1 156.4 %copy-start.6 = (f32[64,2432]{1,0:T(8,128)S(1)}, f32[64,2432]{1,0:T(8,128)}, u32[]{:S(2)}) copy-start(f32[64,2432]{1,0:T(8,128)} %teacher_hidden_ref.1) | copy-start | bytes 1867780
  9.1 156.4 %copy-start.18 = (f32[2048]{0:T(1024)S(1)}, f32[2048]{0:T(1024)}, u32[]{:S(2)}) copy-start(f32[2048]{0:T(1024)} %param.51) | copy-start | bytes 24580
  167.4 88.2 %copy-start.23 = (f32[3,4,12,384]{3,1,2,0:T(4,128)S(1)}, f32[3,4,12,384]{3,1,2,0:T(4,128)}, u32[]{:S(2)}) copy-start(f32[3,4,12,384]{3,1,2,0:T(4,128)} %param.36) | copy-start | bytes 663556
  167.4 89.7 %copy-start.31 = (f32[3,4,12,384]{3,1,2,0:T(4,128)S(1)}, f32[3,4,12,384]{3,1,2,0:T(4,128)}, u32[]{:S(2)}) copy-start(f32[3,4,12,384]{3,1,2,0:T(4,128)} %param.35) | copy-start | bytes 663556
  405.2 9.3 %copy-start.29 = (f32[2048,8]{0,1:T(8,128)S(1)}, f32[2048,8]{0,1:T(8,128)}, u32[]{:S(2)}) copy-start(f32[2048,8]{0,1:T(8,128)} %param.49) | copy-start | bytes 196612
  405.2 9.3 %copy-start.30 = (f32[2048,8]{0,1:T(8,128)S(1)}, f32[2048,8]{0,1:T(8,128)}, u32[]{:S(2)}) copy-start(f32[2048,8]{0,1:T(8,128)} %param.40) | copy-start | bytes 196612
  405.2 9.3 %copy-start.32 = (f32[2048,8]{0,1:T(8,128)S(1)}, f32[2048,8]{0,1:T(8,128)}, u32[]{:S(2)}) copy-start(f32[2048,8]{0,1:T(8,128)} %param.42) | copy-start | bytes 196612
  405.2 9.3 %copy-start.33 = (f32[2048,8]{0,1:T(8,128)S(1)}, f32[2048,8]{0,1:T(8,128)}, u32[]{:S(2)}) copy-start(f32[2048,8]{0,1:T(8,128)} %param.41) | copy-start | bytes 196612
  405.2 10.0 %copy-start.7 = (f32[64,2432]{1,0:T(8,128)S(1)}, f32[64,2432]{1,0:T(8,128)}, u32[]{:S(2)}) copy-start(f32[64,2432]{1,0:T(8,128)} %teacher_hidden_ref.1) | copy-start | bytes 1867780
  405.2 10.0 %copy-start.14 = (f32[64,2432]{1,0:T(8,128)S(1)}, f32[64,2432]{1,0:T(8,128)}, u32[]{:S(2)}) copy-start(f32[64,2432]{1,0:T(8,128)} %copy-done.13) | copy-start | bytes 1867780
  405.2 10.0 %copy-start.25 = (f32[64,2432]{1,0:T(8,128)S(1)}, f32[64,2432]{1,0:T(8,128)}, u32[]{:S(2)}) copy-start(f32[64,2432]{1,0:T(8,128)} %param.39) | copy-start | bytes 1867780
  405.2 10.0 %copy-start.26 = (f32[64,2432]{1,0:T(8,128)S(1)}, f32[64,2432]{1,0:T(8,128)}, u32[]{:S(2)}) copy-start(f32[64,2432]{1,0:T(8,128)} %param.38) | copy-start | bytes 1867780
  415.3 39.5 %copy-start.37 = (s32[12]{0:T(128)S(1)}, s32[12]{0:T(128)}, u32[]{:S(2)}) copy-start(s32[12]{0:T(128)} %param.28) | copy-start | bytes 148
  415.3 39.5 %copy-start.21 = (f32[3,4,12,384]{3,2,1,0:T(8,128)S(1)}, f32[3,4,12,384]{3,2,1,0:T(8,128)}, u32[]{:S(2)}) copy-start(f32[3,4,12,384]{3,2,1,0:T(8,128)} %copy.94) | copy-start | bytes 663556
  415.3 41.1 %copy-start.24 = (f32[480,384]{1,0:T(8,128)S(1)}, f32[480,384]{1,0:T(8,128)}, u32[]{:S(2)}) copy-start(f32[480,384]{1,0:T(8,128)} %get-tuple-element.78) | copy-start | bytes 2211844
  415.3 41.2 %copy-start.5 = (f32[3,144,384]{2,1,0:T(8,128)S(1)}, f32[3,144,384]{2,1,0:T(8,128)}, u32[]{:S(2)}) copy-start(f32[3,144,384]{2,1,0:T(8,128)} %teacher_ref.1) | copy-start | bytes 1990660
  415.3 41.2 %copy-start.11 = (f32[3,144,384]{2,1,0:T(8,128)S(1)}, f32[3,144,384]{2,1,0:T(8,128)}, u32[]{:S(2)}) copy-start(f32[3,144,384]{2,1,0:T(8,128)} %first_ref.1) | copy-start | bytes 1990660
  415.3 41.2 %copy-start.12 = (f32[3,144,384]{2,1,0:T(8,128)S(1)}, f32[3,144,384]{2,1,0:T(8,128)}, u32[]{:S(2)}) copy-start(f32[3,144,384]{2,1,0:T(8,128)} %second_ref.1) | copy-start | bytes 1990660
  417.2 39.3 %copy-start.1 = (bf16[32,144,384]{2,1,0:T(8,128)(2,1)S(1)}, bf16[32,144,384]{2,1,0:T(8,128)(2,1)}, u32[]{:S(2)}) copy-start(bf16[32,144,384]{2,1,0:T(8,128)(2,1)} %get-tuple-element.79.bases_ref) | copy-start | bytes 10616836
  417.2 39.3 %copy-start.3 = (f32[3,144,384]{2,1,0:T(8,128)S(1)}, f32[3,144,384]{2,1,0:T(8,128)}, u32[]{:S(2)}) copy-start(f32[3,144,384]{2,1,0:T(8,128)} %weights_ref.1) | copy-start | bytes 1990660
  417.2 39.3 %copy-start.20 = (f32[8,128]{1,0:T(8,128)S(1)}, f32[8,128]{1,0:T(8,128)}, u32[]{:S(2)}) copy-start(f32[8,128]{1,0:T(8,128)} %get-tuple-element.77.norm_ref) | copy-start | bytes 12292
  (14 other events, 23.8 us)
